TPU v7x, 512 devices: a whole 4x8x8 slice. The times are simulated.
512 devices in a mesh: region: 8 (over y_lo, core), space: 64 (over y_hi, x, z).
Axes of the slice: x: 4, y: 8 (y_hi: 2, y_lo: 4; y = y_hi * 4 + y_lo), z: 8, core: 2. Of those that a mesh axis runs over, the one named last changes fastest.
Arguments:
- tokens: bfloat16 [8, 18432, 384], P('region', 'space'), may hold values from -6 to 6
- cotangent: bfloat16 [8, 18432, 384], P('region', 'space'), may hold values from -6 to 6
- neighbours: int32 [8, 576, 27], P('region', 'space'), may hold values from -1 to 575, as said below
- active: int32 [8, 576], P('region', 'space'), may hold values from 0 to 1
- gain: float32 [384], replicated, may hold values from 0.1 to 1.9
- w_qkv: bfloat16 [384, 1152], replicated, may hold values from -4.082483 to 4.082483
- w_out: bfloat16 [384, 384], replicated, may hold values from -0.3125 to 0.3125
Outputs:
- grad_input: bfloat16 [8, 18432, 384], P('region', 'space')
- grad_qkv: float32 [384, 1152], replicated
- grad_out: float32 [384, 384], replicated
- grad_gain: float32 [384], replicated
Inputs may be any that keep to these rules, and one draw needn't show every extreme that they name: `neighbours`: row b lists first b itself, then the other active blocks of its region whose layer, row and column each differ from b's by at most one, each once; the rest is -1, and the row of an inactive block is all -1. In every region some block lists 27 blocks.
All inputs are finite; a program needn't handle non-finite values.
Results may differ from a plain program's by a relative error of at most 0.012.
Values may be sent and summed in bfloat16 or wider, within the bound.
No kernel may reach another device: no remote copies, remote signals or barrier semaphores. Data moves between devices by JAX's collectives and lax.ppermute only.
A program may use at most 64 MiB of HBM per device.

v0:
```python
import math

import jax
import jax.numpy as jnp
from jax import lax
from jax.sharding import PartitionSpec as P

HEADS = 6
GY = 3
GZ = 3


def padded(block, sides, width):
    for axis, dim in sides:
        count = lax.axis_size(axis)
        forward = [(i, i + 1) for i in range(count - 1)]
        backward = [(target, source) for source, target in forward]
        low = lax.ppermute(
            lax.slice_in_dim(block, block.shape[dim] - width, None, axis=dim), axis, forward
        )
        high = lax.ppermute(lax.slice_in_dim(block, 0, width, axis=dim), axis, backward)
        block = jnp.concatenate([low, block, high], axis=dim)
    return block


def passed_along(block, axis, distance):
    devices = range(lax.axis_size(axis))
    route = [(i - distance, i) for i in devices if i - distance in devices]
    return lax.ppermute(block, axis, route)


def normalize(values, gain):
    power = jnp.mean(values * values, axis=1, keepdims=True)
    return values * lax.rsqrt(power + 1e-06) * gain


def block_mask(lists, table_ids):
    listed = lists[:, :, None]
    hit = (listed == table_ids[None, None, :]) & (listed >= 0)
    return jnp.any(hit, axis=1)


def inner(left, right):
    return lax.dot_general(
        left, right, (((1,), (1,)), ((), ())), preferred_element_type=jnp.float32
    )


def across(left, right):
    return lax.dot_general(
        left, right, (((0,), (0,)), ((), ())), preferred_element_type=jnp.float32
    )


def attend(queries, table, blockmask):
    rows, border_width = queries.shape
    head_size = border_width // HEADS
    nqb, ntb = blockmask.shape
    block = rows // nqb
    keys = table.shape[0]
    factor = 1.0 / head_size**0.5
    outputs = []
    weights = []
    for head in range(HEADS):
        lo = head * head_size
        scores = inner(queries[:, lo : lo + head_size], table[:, lo : lo + head_size]) * factor
        scores = jnp.where(
            blockmask[:, None, :, None], scores.reshape(nqb, block, ntb, block), -1e30
        ).reshape(rows, keys)
        top = lax.stop_gradient(jnp.max(scores, axis=1, keepdims=True))
        expo = jnp.exp(scores - top)
        share = (expo / jnp.sum(expo, axis=1, keepdims=True)).astype(jnp.bfloat16)
        outputs.append(
            jnp.dot(
                share,
                table[:, border_width + lo : border_width + lo + head_size],
                preferred_element_type=jnp.float32,
            )
        )
        weights.append(share)
    return (jnp.concatenate(outputs, axis=1).astype(jnp.bfloat16), weights)


def attend_back(d_attn, queries, table, weights):
    rows, border_width = queries.shape
    head_size = border_width // HEADS
    factor = 1.0 / head_size**0.5
    dq_parts = []
    dk_parts = []
    dv_parts = []
    for head in range(HEADS):
        lo = head * head_size
        grad_out = d_attn[:, lo : lo + head_size]
        share = weights[head]
        d_share = inner(grad_out, table[:, border_width + lo : border_width + lo + head_size])
        share32 = share.astype(jnp.float32)
        d_scores = (
            share32 * (d_share - jnp.sum(share32 * d_share, axis=1, keepdims=True)) * factor
        ).astype(jnp.bfloat16)
        dq_parts.append(
            jnp.dot(d_scores, table[:, lo : lo + head_size], preferred_element_type=jnp.float32)
        )
        dk_parts.append(across(d_scores, queries[:, lo : lo + head_size]))
        dv_parts.append(across(share, grad_out))
    d_queries = jnp.concatenate(dq_parts, axis=1).astype(jnp.bfloat16)
    d_table = jnp.concatenate(dk_parts + dv_parts, axis=1).astype(jnp.bfloat16)
    return (d_queries, d_table)


def shards(tokens, cotangent, neighbours, active, gain, w_qkv, w_out):
    values = tokens[0]
    cot = cotangent[0]
    lists = neighbours[0]
    alive = active[0]
    rows, border_width = values.shape
    nqb = alive.shape[0]
    block = rows // nqb
    side = GY * GZ
    boundary_plane = side * block
    top_rows = rows - boundary_plane
    position = lax.axis_index("space")
    values32 = values.astype(jnp.float32)
    normed = normalize(values32, gain).astype(jnp.bfloat16)
    w_query = w_qkv[:, :border_width]
    w_keyval = w_qkv[:, border_width:]
    queries = jnp.dot(normed, w_query, preferred_element_type=jnp.float32).astype(jnp.bfloat16)
    keyval = jnp.dot(normed, w_keyval, preferred_element_type=jnp.float32).astype(jnp.bfloat16)
    table = padded(keyval, (("space", 0),), boundary_plane)
    table_ids = position * nqb - side + jnp.arange(nqb + 2 * side)
    blockmask = block_mask(lists, table_ids)
    scaled = (
        cot.reshape(nqb, block, border_width) * alive.astype(jnp.bfloat16)[:, None, None]
    ).reshape(rows, border_width)
    d_attn = inner(scaled, w_out).astype(jnp.bfloat16)
    attn, weights = attend(queries, table, blockmask)
    grad_wout = across(attn, scaled)
    d_queries, d_table = attend_back(d_attn, queries, table, weights)
    own_part = d_table[boundary_plane : boundary_plane + rows]
    kv_back = inner(own_part, w_keyval)
    from_above = passed_along(d_table[:boundary_plane], "space", -1)
    from_below = passed_along(d_table[boundary_plane + rows :], "space", 1)
    grad_kv = across(normed, own_part) + across(normed, from_above) + across(normed, from_below)
    back_above = inner(from_above, w_keyval).astype(jnp.bfloat16)
    back_below = inner(from_below, w_keyval).astype(jnp.bfloat16)
    kv_back = kv_back.at[top_rows:].add(back_above.astype(jnp.float32))
    kv_back = kv_back.at[:boundary_plane].add(back_below.astype(jnp.float32))
    grad_wqkv = jnp.concatenate([across(normed, d_queries), grad_kv], axis=1)
    d_normed = (inner(d_queries, w_query) + kv_back).astype(jnp.bfloat16)
    unused, pullback = jax.vjp(normalize, values32, gain)
    d_norm_in, d_gain = pullback(d_normed.astype(jnp.float32))
    grad_input = (cot.astype(jnp.float32) + d_norm_in).astype(jnp.bfloat16)
    summed_qkv, summed_out, summed_gain = lax.psum(
        (grad_wqkv, grad_wout, d_gain), ("region", "space")
    )
    factor = 1.0 / math.sqrt(lax.axis_size("region") * lax.axis_size("space") * rows)
    return (grad_input[None], summed_qkv * factor, summed_out * factor, summed_gain * factor)


def solution(mesh):
    in_specs = (
        P("region", "space", None),
        P("region", "space", None),
        P("region", "space", None),
        P("region", "space"),
        P(),
        P(),
        P(),
    )
    out_specs = (P("region", "space", None), P(), P(), P())
    return jax.shard_map(shards, mesh=mesh, in_specs=in_specs, out_specs=out_specs, check_vma=False)
```

profile of v0, /device:TPU:1, one launch (start us, length us, event | category | flops | bytes accessed | tf_op | source)
XLA Modules:
  0.0 395.9 jit_solution(12785989811796476450)
XLA Ops:
  7.2 1.1 fusion.70
  8.4 1.6 convolution_convert_fusion
  10.0 1.3 collective-permute-start.1
  11.3 6.2 %collective-permute-start = (bf16[288,768]{1,0:T(8,128)(2,1)S(1)}, bf16[288,768]{1,0:T(8,128)(2,1)}, u32[]{:S(2)}, u32[]{:S(2)}) collective-permute-start(bf16[288,768]{1,0:T(8,128)(2,1)S(1)} %convolution_convert_fusion), channel_id=1, source_target_pairs={{0,1},{1,2},{2,3},{3,4},{4,5},{5,6},{6,7},{7,8},{8,9},{9,10},{10,1... | collective-permute-start | bytes 1327112 | tf_op jit(solution)/shard_map/ppermute | solution.py:18
  18.4 2.3 broadcast_in_dim.39
  21.0 1.3 convolution_convert_fusion.2
  22.4 1.1 pad_maximum_fusion.1
  23.5 0.5 fusion.150
  24.4 0.5 fusion.148
  25.0 0.4 fusion.147
  25.4 0.5 fusion.146
  25.9 0.4 fusion.145
  26.7 0.5 fusion.36
  28.7 0.6 fusion.51
  29.6 0.5 fusion.48
  30.5 0.6 fusion.45
  31.4 0.5 fusion.42
  32.2 0.6 fusion.39
  37.7 1.5 fusion.64
  39.2 0.7 fusion.62
  39.9 1.3 fusion.144
  41.2 0.5 fusion.34
  42.0 0.5 fusion.32
  42.8 0.5 fusion.30
  43.3 0.5 fusion.28
  44.2 0.5 fusion.26
  45.0 1.3 fusion.140
  46.3 2.1 copy.17
  48.3 2.0 copy.16
  50.4 1.3 collective-permute-start.2
  51.7 7.1 %collective-permute-start.3 = (bf16[288,768]{1,0:T(8,128)(2,1)}, bf16[288,768]{1,0:T(8,128)(2,1)S(1)}, u32[]{:S(2)}, u32[]{:S(2)}) collective-permute-start(bf16[288,768]{1,0:T(8,128)(2,1)} %copy.17), channel_id=1, source_target_pairs={{0,1},{1,2},{2,3},{3,4},{4,5},{5,6},{6,7},{7,8},{8,9},{9,10},{10,1... | collective-permute-start | bytes 1327112 | tf_op jit(solution)/shard_map/ppermute | solution.py:29
  58.8 1.1 fusion.24
  59.9 2.2 fusion.79
  62.1 1.5 collective-permute-done.2
  63.6 0.6 convolution_add_fusion.1
  64.6 0.8 copy-done.7
  65.4 0.6 convolution_add_fusion
  66.0 1.3 pad_maximum_fusion
  67.4 1.1 copy-done.3
  69.2 0.6 copy-done.8
  70.2 0.5 copy-done.10
  70.7 0.5 fusion.67
  71.2 140.2 %psum.23 = f32[384]{0:T(512)S(1)} all-reduce(f32[384]{0:T(512)S(1)} %get-tuple-element.44), channel_id=1, replica_groups=mesh['region'=8,'space'=64] {'region','space'}, use_global_device_ids=true, to_apply=%region_24.25 | all-reduce | flops 384 | bytes 3072 | tf_op jit(solution)/shard_map/psum | solution.py:152
  211.4 0.6 broadcast_multiply_fusion.2
  212.0 0.9 fusion.78
  212.9 172.3 %all-reduce.3.cloned.1.call-done = (f32[384,1152]{1,0:T(8,128)}, f32[384,384]{1,0:T(8,128)}) async-done(((f32[384,1152]{1,0:T(8,128)}, f32[384,384]{1,0:T(8,128)}), (f32[384,1152]{1,0:T(8,128)}, f32[384,384]{1,0:T(8,128)})) %all-reduce.3.cloned.1.call-update) | async-done | bytes 2359312 | tf_op jit(solution)/shard_map/psum | solution.py:152
  385.2 2.9 broadcast_multiply_fusion
  388.1 0.9 broadcast_multiply_fusion.1
  (83 shorter events, 12.3 us)
Async XLA Ops:
  7.2 13.5 %copy-start = (bf16[384,384]{1,0:T(8,128)(2,1)S(1)}, bf16[384,384]{1,0:T(8,128)(2,1)}, u32[]{:S(2)}) copy-start(bf16[384,384]{1,0:T(8,128)(2,1)} %param.21) | copy-start | bytes 884740
  7.2 10.4 %copy-start.17 = (s32[1,9,27]{2,0,1:T(1,128)S(1)}, s32[1,9,27]{2,0,1:T(1,128)}, u32[]{:S(2)}) copy-start(s32[1,9,27]{2,0,1:T(1,128)} %param.17) | copy-start | bytes 2920
  7.2 10.4 %copy-start.18 = (s32[1,9]{1,0:T(1,128)S(1)}, s32[1,9]{1,0:T(1,128)}, u32[]{:S(2)}) copy-start(s32[1,9]{1,0:T(1,128)} %param.18) | copy-start | bytes 112
  7.2 378.0 %all-reduce.3.cloned.1.call-start = ((), (), s32[]{:S(2)}) async-start(), calls=%async_computation | async-start | bytes 4718592 | tf_op jit(solution)/shard_map/psum | solution.py:152
  10.0 12.3 %collective-permute-start.1 = (bf16[288,768]{1,0:T(8,128)(2,1)S(1)}, bf16[288,768]{1,0:T(8,128)(2,1)S(1)}, u32[]{:S(2)}, u32[]{:S(2)}) collective-permute-start(bf16[288,768]{1,0:T(8,128)(2,1)S(1)} %convolution_convert_fusion), channel_id=1, source_target_pairs={{1,0},{2,1},{3,2},{4,3},{5,4},{6,5},{7,6},{8,7},{9,8},{10,9},{11,1... | collective-permute-start | bytes 1327112 | tf_op jit(solution)/shard_map/ppermute | solution.py:21
  11.3 11.0 %collective-permute-start = (bf16[288,768]{1,0:T(8,128)(2,1)S(1)}, bf16[288,768]{1,0:T(8,128)(2,1)}, u32[]{:S(2)}, u32[]{:S(2)}) collective-permute-start(bf16[288,768]{1,0:T(8,128)(2,1)S(1)} %convolution_convert_fusion), channel_id=1, source_target_pairs={{0,1},{1,2},{2,3},{3,4},{4,5},{5,6},{6,7},{7,8},{8,9},{9,10},{10,1... | collective-permute-start | bytes 1327112 | tf_op jit(solution)/shard_map/ppermute | solution.py:18
  17.6 3.1 copy-start.11
  18.3 2.7 copy-start.1
  18.3 2.7 copy-start.16
  36.4 1.3 copy-start.2
  43.3 1.6 copy-start.9
  45.0 1.3 copy-start.15
  50.4 13.2 %collective-permute-start.2 = (bf16[288,768]{1,0:T(8,128)(2,1)}, bf16[288,768]{1,0:T(8,128)(2,1)S(1)}, u32[]{:S(2)}, u32[]{:S(2)}) collective-permute-start(bf16[288,768]{1,0:T(8,128)(2,1)} %copy.16), channel_id=1, source_target_pairs={{1,0},{2,1},{3,2},{4,3},{5,4},{6,5},{7,6},{8,7},{9,8},{10,9},{11,1... | collective-permute-start | bytes 1327112 | tf_op jit(solution)/shard_map/ppermute | solution.py:29
  51.7 12.9 %collective-permute-start.3 = (bf16[288,768]{1,0:T(8,128)(2,1)}, bf16[288,768]{1,0:T(8,128)(2,1)S(1)}, u32[]{:S(2)}, u32[]{:S(2)}) collective-permute-start(bf16[288,768]{1,0:T(8,128)(2,1)} %copy.17), channel_id=1, source_target_pairs={{0,1},{1,2},{2,3},{3,4},{4,5},{5,6},{6,7},{7,8},{8,9},{9,10},{10,1... | collective-permute-start | bytes 1327112 | tf_op jit(solution)/shard_map/ppermute | solution.py:29
  63.6 0.8 copy-start.5
  64.4 1.6 copy-start.4
  64.6 0.8 copy-start.7
  67.3 1.2 copy-start.3
  67.3 1.3 copy-start.6
  67.3 1.4 copy-start.14
  68.7 1.0 copy-start.8
  69.8 1.0 copy-start.10
  70.7 141.3 %copy-start.12 = (bf16[1,288,384]{2,1,0:T(8,128)(2,1)S(1)}, bf16[1,288,384]{2,1,0:T(8,128)(2,1)}, u32[]{:S(2)}) copy-start(bf16[1,288,384]{2,1,0:T(8,128)(2,1)} %param.16) | copy-start | bytes 663556
  385.2 2.9 copy-start.13
Sparse Core Ops, SparseCore 0:
  67.5 317.7 all-reduce.2
where the time goes:
time: 396 us
  waiting for transfers between devices  174 us (44%)
  blocking collectives  140 us (35%)
  matrix products  26.9 us (7%)
  starting transfers between devices  16 us (4%)
  between operations  14.5 us (4%)
  other arithmetic  12.6 us (3%)
  local copies, waits for them, and re-layouts  11.7 us (3%)
    psum x1, waiting for transfers between devices, shards(): lax.psum((grad_wqkv, grad_wout, d_gain), ('region', 'space'))  172 us
    psum x1, blocking collectives, shards(): lax.psum((grad_wqkv, grad_wout, d_gain), ('region', 'space'))  140 us
    dot_general x17, matrix products, inner(): lax.dot_general(left, right, (((1,), (1,)), ((), ())), preferred_element_...  9.33 us
    dot_general x17, matrix products, across(): lax.dot_general(left, right, (((0,), (0,)), ((), ())), preferred_element_...  9.18 us
    ppermute x2, starting transfers between devices, passed_along(): return lax.ppermute(block, axis, route)  8.41 us
  transfers between devices with their start and end apart: 5, of which 3 were waited for; matrix products, arithmetic and copies ran while one was open for 3% of the time, Pallas kernels for 0%

commit v1 on v0

v1 whole, which is shorter than its diff:
```python
import math

import jax
import jax.numpy as jnp
from jax import lax
from jax.sharding import Mesh
from jax.sharding import PartitionSpec as P

HEADS = 6
SIDE = 9
SPACE = ("yh", "x", "z")


def inner(left, right):
    return lax.dot_general(
        left, right, (((1,), (1,)), ((), ())), preferred_element_type=jnp.float32
    )


def across(left, right):
    return lax.dot_general(
        left, right, (((0,), (0,)), ((), ())), preferred_element_type=jnp.float32
    )


def shifted(block, distance):
    count = lax.axis_size(SPACE)
    route = [(i, i + distance) for i in range(count) if 0 <= i + distance < count]
    return lax.ppermute(block, SPACE, route)


def spread(part, axes):
    count = lax.axis_size(axes)
    copies = jnp.broadcast_to(part[None], (count,) + part.shape)
    return lax.all_to_all(copies, axes, 0, 0, tiled=True)


def total(parts):
    return jnp.sum(parts.astype(jnp.float32), axis=0).astype(jnp.bfloat16)


def reduced(blocks):
    core = lax.axis_index("c")
    own = lax.dynamic_index_in_dim(blocks, core, 0, False)
    other = lax.dynamic_index_in_dim(blocks, 1 - core, 0, False)
    swap = [(0, 1), (1, 0)]
    half = total(jnp.stack([own, lax.ppermute(other, "c", swap)]))
    plane = lax.axis_size(("x", "z"))
    rows, columns = half.shape
    parts = half.reshape(plane, rows // plane, columns)
    part = total(lax.all_to_all(parts, ("x", "z"), 0, 0, tiled=True))
    part = total(spread(part, ("yl", "yh")))
    half = spread(part, ("x", "z")).reshape(rows, columns)
    other = lax.ppermute(half, "c", swap)
    return jnp.where(core == 0, jnp.stack([half, other]), jnp.stack([other, half]))


def shards(tokens, cotangent, neighbours, active, gain, w_qkv, w_out):
    values = tokens[0]
    cot = cotangent[0]
    lists = neighbours[0]
    alive = active[0]
    rows, width = values.shape
    nqb = alive.shape[0]
    block = rows // nqb
    head_size = width // HEADS
    factor = 1.0 / head_size**0.5
    position = lax.axis_index(SPACE)
    window = jnp.concatenate([shifted(values, 1), values, shifted(values, -1)], axis=0)
    window32 = window.astype(jnp.float32)
    root = lax.rsqrt(jnp.mean(window32 * window32, axis=1, keepdims=True) + 1e-06)
    normed = (window32 * root * gain).astype(jnp.bfloat16)
    own = normed[rows : 2 * rows]
    w_query = w_qkv[:, :width]
    w_keyval = w_qkv[:, width:]
    queries = jnp.dot(own, w_query, preferred_element_type=jnp.float32).astype(jnp.bfloat16)
    table = jnp.dot(normed, w_keyval, preferred_element_type=jnp.float32).astype(jnp.bfloat16)
    ids = position * nqb - SIDE + jnp.arange(nqb + 2 * SIDE)
    mask = jnp.any((lists[:, :, None] == ids[None, None, :]) & (lists[:, :, None] >= 0), axis=1)
    ntb = nqb + 2 * SIDE
    scaled = (
        cot.reshape(nqb, block, width) * alive.astype(jnp.bfloat16)[:, None, None]
    ).reshape(rows, width)
    d_attn = inner(scaled, w_out).astype(jnp.bfloat16)
    outs, dqs, dks, dvs = [], [], [], []
    for head in range(HEADS):
        at = slice(head * head_size, (head + 1) * head_size)
        q, k, v, g = queries[:, at], table[:, at], table[:, width:][:, at], d_attn[:, at]
        scores = inner(q, k) * factor
        scores = jnp.where(
            mask[:, None, :, None], scores.reshape(nqb, block, ntb, block), -1e30
        ).reshape(rows, -1)
        expo = jnp.exp(scores - jnp.max(scores, axis=1, keepdims=True))
        share = (expo / jnp.sum(expo, axis=1, keepdims=True)).astype(jnp.bfloat16)
        out = jnp.dot(share, v, preferred_element_type=jnp.float32)
        d_share = inner(g, v)
        share32 = share.astype(jnp.float32)
        delta = jnp.sum(share32 * d_share, axis=1, keepdims=True)
        d_scores = (share32 * (d_share - delta) * factor).astype(jnp.bfloat16)
        outs.append(out)
        dqs.append(jnp.dot(d_scores, k, preferred_element_type=jnp.float32))
        dks.append(across(d_scores, q))
        dvs.append(across(share, g))
    attn = jnp.concatenate(outs, axis=1).astype(jnp.bfloat16)
    d_queries = jnp.concatenate(dqs, axis=1).astype(jnp.bfloat16)
    d_table = jnp.concatenate(dks + dvs, axis=1).astype(jnp.bfloat16)
    back = inner(d_table, w_keyval)
    above = shifted(back[:rows].astype(jnp.bfloat16), -1)
    below = shifted(back[2 * rows :].astype(jnp.bfloat16), 1)
    grad_q = across(own, d_queries)
    grad_kv = across(normed, d_table)
    grad_out = across(attn, scaled)
    blocks = jnp.stack(
        [
            jnp.concatenate([grad_q, grad_kv[:, :width]], axis=0),
            jnp.concatenate([grad_kv[:, width:], grad_out], axis=0),
        ]
    ).astype(jnp.bfloat16)
    summed = reduced(blocks)
    d_normed = inner(d_queries, w_query) + back[rows : 2 * rows]
    d_normed = d_normed + above.astype(jnp.float32) + below.astype(jnp.float32)
    d_normed = d_normed.astype(jnp.bfloat16).astype(jnp.float32)
    own32 = window32[rows : 2 * rows]
    own_root = root[rows : 2 * rows]
    inward = d_normed * gain
    slope = jnp.mean(inward * own32, axis=1, keepdims=True) * own_root * own_root
    grad_input = cot.astype(jnp.float32) + own_root * (inward - own32 * slope)
    scale = 1.0 / math.sqrt(512 * rows)
    summed = summed.astype(jnp.float32) * scale
    grad_wqkv = jnp.concatenate([summed[0, :width], summed[0, width:], summed[1, :width]], axis=1)
    grad_gain = jnp.sum(grad_wqkv * w_qkv.astype(jnp.float32), axis=1) / gain
    return (grad_input.astype(jnp.bfloat16)[None], grad_wqkv, summed[1, width:], grad_gain)


def solution(mesh):
    fine = Mesh(mesh.devices.reshape(4, 2, 2, 4, 8), ("yl", "c", "yh", "x", "z"))
    region = ("yl", "c")
    split = P(region, SPACE, None)
    return jax.shard_map(
        shards,
        mesh=fine,
        in_specs=(split, split, split, P(region, SPACE), P(), P(), P()),
        out_specs=(split, P(), P(), P()),
        check_vma=False,
    )
```

time: 396 us -> 145 us (0.37)
  the two profiles are of different devices: /device:TPU:1 before, /device:TPU:48 now
where the time goes in v1:
time: 145 us; the launch traced here: 144 us
  starting transfers between devices  38.5 us (27%)
  blocking collectives  32.4 us (22%)
  waiting for transfers between devices  31.4 us (22%)
  matrix products  22.9 us (16%)
  other arithmetic  11.6 us (8%)
  local copies, waits for them, and re-layouts  6.58 us (5%)
    ppermute x4, starting transfers between devices, shifted(): return lax.ppermute(block, SPACE, route)  28.6 us
    ppermute x4, waiting for transfers between devices, shifted(): return lax.ppermute(block, SPACE, route)  27.7 us
    all_to_all x1, blocking collectives, reduced(): part = total(lax.all_to_all(parts, ('x', 'z'), 0, 0, tiled=True))  21.5 us
    dot_general x15, matrix products, inner(): lax.dot_general(left, right, (((1,), (1,)), ((), ())), preferred_element_...  11.6 us
    all_to_all x1, blocking collectives, spread(): return lax.all_to_all(copies, axes, 0, 0, tiled=True)  10.8 us
    all_to_all x1, starting transfers between devices, spread(): return lax.all_to_all(copies, axes, 0, 0, tiled=True)  6.07 us
    dot_general x15, matrix products, across(): lax.dot_general(left, right, (((0,), (0,)), ((), ())), preferred_element_...  5.33 us
  transfers between devices with their start and end apart: 7, of which 6 were waited for; matrix products, arithmetic and copies ran while one was open for 9% of the time, Pallas kernels for 0%

profile of v1, /device:TPU:48, one launch (start us, length us, event | category | flops | bytes accessed | tf_op | source)
XLA Modules:
  0.0 144.5 jit_solution(15084771229832518447)
XLA Ops:
  0.6 14.6 %collective-permute-start.1 = (bf16[288,384]{1,0:T(8,128)(2,1)}, bf16[288,384]{1,0:T(8,128)(2,1)S(1)}, u32[]{:S(2)}, u32[]{:S(2)}) collective-permute-start(bf16[288,384]{1,0:T(8,128)(2,1)} %bitcast.72), channel_id=1, source_target_pairs={{1,0},{2,1},{3,2},{4,3},{5,4},{6,5},{7,6},{8,7},{9,8},{10,9},{11,1... | collective-permute-start | bytes 663560 | tf_op jit(solution)/shard_map/ppermute | solution.py:29
  15.3 1.9 %collective-permute-start = (bf16[288,384]{1,0:T(8,128)(2,1)}, bf16[288,384]{1,0:T(8,128)(2,1)S(1)}, u32[]{:S(2)}, u32[]{:S(2)}) collective-permute-start(bf16[288,384]{1,0:T(8,128)(2,1)} %bitcast.73), channel_id=1, source_target_pairs={{0,1},{1,2},{2,3},{3,4},{4,5},{5,6},{6,7},{7,8},{8,9},{9,10},{10,1... | collective-permute-start | bytes 663560 | tf_op jit(solution)/shard_map/ppermute | solution.py:29
  17.2 0.7 broadcast_compare_fusion
  17.9 0.7 copy.15
  18.6 0.7 convert_bitcast_fusion
  20.0 2.3 %broadcast_in_dim.41 = pred[288,864]{1,0:T(32,128)(4,1)S(1)} reshape(pred[9,32,27,32]{3,2,1,0:T(8,128)(4,1)S(1)} %broadcast_in_dim.40) | data formatting | bytes 497664 | tf_op jit(solution)/shard_map/jit(_where)/broadcast_in_dim | solution.py:90
  22.7 2.1 %collective-permute-done.1 = bf16[288,384]{1,0:T(8,128)(2,1)S(1)} collective-permute-done((bf16[288,384]{1,0:T(8,128)(2,1)}, bf16[288,384]{1,0:T(8,128)(2,1)S(1)}, u32[]{:S(2)}, u32[]{:S(2)}) %collective-permute-start.1) | collective-permute-done | bytes 221216 | tf_op jit(solution)/shard_map/ppermute | solution.py:29
  24.8 12.1 %collective-permute-done = bf16[288,384]{1,0:T(8,128)(2,1)S(1)} collective-permute-done((bf16[288,384]{1,0:T(8,128)(2,1)}, bf16[288,384]{1,0:T(8,128)(2,1)S(1)}, u32[]{:S(2)}, u32[]{:S(2)}) %collective-permute-start) | collective-permute-done | bytes 221216 | tf_op jit(solution)/shard_map/ppermute | solution.py:29
  37.7 0.9 convolution_convert_fusion
  38.6 0.5 fusion.133
  39.1 0.4 fusion.132
  39.5 0.5 fusion.131
  40.5 0.5 fusion.129
  41.0 0.4 fusion.128
  41.8 0.5 fusion.30
  43.8 0.6 fusion.45
  44.7 0.5 fusion.42
  45.6 0.6 fusion.39
  46.5 0.5 fusion.36
  47.3 0.6 fusion.33
  48.1 0.5 fusion.28
  49.6 0.5 fusion.26
  50.9 0.5 fusion.24
  51.8 0.5 fusion.22
  52.6 0.5 fusion.20
  53.5 0.5 fusion.18
  57.9 0.8 convolution_convert_fusion.1
  59.2 1.1 fusion.55
  60.3 1.9 %collective-permute-start.4 = (bf16[768,384]{1,0:T(8,128)(2,1)}, bf16[768,384]{1,0:T(8,128)(2,1)S(1)}, u32[]{:S(2)}, u32[]{:S(2)}) collective-permute-start(bf16[768,384]{1,0:T(8,128)(2,1)} %fusion.55), channel_id=1, source_target_pairs={{0,64},{64,0},{1,65},{65,1},{2,66},{66,2},{3,67},{67,3},{4,68},{68... | collective-permute-start | bytes 1769480 | tf_op jit(solution)/shard_map/ppermute | solution.py:47
  62.2 2.2 %collective-permute-done.4 = bf16[768,384]{1,0:T(8,128)(2,1)S(1)} collective-permute-done((bf16[768,384]{1,0:T(8,128)(2,1)}, bf16[768,384]{1,0:T(8,128)(2,1)S(1)}, u32[]{:S(2)}, u32[]{:S(2)}) %collective-permute-start.4) | collective-permute-done | bytes 589856 | tf_op jit(solution)/shard_map/ppermute | solution.py:47
  64.6 21.5 %all_to_all.15 = bf16[32,24,384]{2,1,0:T(8,128)(2,1)S(1)} all-to-all(bf16[32,24,384]{2,1,0:T(8,128)(2,1)S(1)} %bitcast.69), channel_id=1, replica_groups=mesh['yl'=4,'c'=2,'yh'=2,'x'=4,'z'=8] {'x','z'}, dimensions={0} | all-to-all | bytes 1179648 | tf_op jit(solution)/shard_map/all_to_all | solution.py:51
  86.3 10.8 %all_to_all.16 = bf16[8,24,384]{2,1,0:T(8,128)(2,1)S(1)} all-to-all(bf16[8,24,384]{2,1,0:T(8,128)(2,1)S(1)} %broadcast_in_dim.44), channel_id=1, replica_groups=mesh['yl'=4,'c'=2,'yh'=2,'x'=4,'z'=8] {'yl','yh'}, dimensions={0} | all-to-all | bytes 294912 | tf_op jit(solution)/shard_map/all_to_all | solution.py:35
  97.1 0.9 broadcast_in_dim.45
  98.0 6.1 %all-to-all-start.2 = ((bf16[32,24,384]{2,1,0:T(8,128)(2,1)}), bf16[32,24,384]{2,1,0:T(8,128)(2,1)S(1)}, u32[]{:S(2)}, u32[]{:S(2)}) async-start(bf16[32,24,384]{2,1,0:T(8,128)(2,1)} %broadcast_in_dim.45), calls=%async_computation.2 | async-start | bytes 1179648 | tf_op jit(solution)/shard_map/all_to_all | solution.py:35
  104.1 3.3 %fusion.134 = (bf16[864,384]{1,0:T(8,128)(2,1)S(1)}, f32[864,384]{1,0:T(8,128)}) fusion(bf16[864,768]{0,1:T(8,128)(2,1)} %copy-done.4, bf16[384,1152]{1,0:T(8,128)(2,1)S(1)} %copy-done.1), kind=kOutput, calls=%fused_computation.223 | convolution fusion | flops 509939712 | bytes 3907584 | tf_op jit(solution)/shard_map/dot_general | solution.py:15
  107.4 0.8 fusion.126
  108.2 10.1 %collective-permute-start.2 = (bf16[288,384]{1,0:T(8,128)(2,1)}, bf16[288,384]{1,0:T(8,128)(2,1)}, u32[]{:S(2)}, u32[]{:S(2)}) collective-permute-start(bf16[288,384]{1,0:T(8,128)(2,1)} %get-tuple-element.22), channel_id=1, source_target_pairs={{1,0},{2,1},{3,2},{4,3},{5,4},{6,5},{7,6},{8,7},{9,8},{10,9},{11,1... | collective-permute-start | bytes 663560 | tf_op jit(solution)/shard_map/ppermute | solution.py:29
  118.4 1.9 %collective-permute-start.3 = (bf16[288,384]{1,0:T(8,128)(2,1)}, bf16[288,384]{1,0:T(8,128)(2,1)}, u32[]{:S(2)}, u32[]{:S(2)}) collective-permute-start(bf16[288,384]{1,0:T(8,128)(2,1)} %get-tuple-element.23), channel_id=1, source_target_pairs={{0,1},{1,2},{2,3},{3,4},{4,5},{5,6},{6,7},{7,8},{8,9},{9,10},{10,1... | collective-permute-start | bytes 663560 | tf_op jit(solution)/shard_map/ppermute | solution.py:29
  120.4 1.0 maximum_convert_fusion
  121.4 1.6 %all-to-all-done.2 = bf16[32,24,384]{2,1,0:T(8,128)(2,1)S(1)} async-done(((bf16[32,24,384]{2,1,0:T(8,128)(2,1)}), bf16[32,24,384]{2,1,0:T(8,128)(2,1)S(1)}, u32[]{:S(2)}, u32[]{:S(2)}) %all-to-all-start.2) | async-done | bytes 589856 | tf_op jit(solution)/shard_map/all_to_all | solution.py:35
  123.0 1.9 %collective-permute-start.5 = (bf16[768,384]{1,0:T(8,128)(2,1)S(1)}, bf16[768,384]{1,0:T(8,128)(2,1)S(1)}, u32[]{:S(2)}, u32[]{:S(2)}) collective-permute-start(bf16[768,384]{1,0:T(8,128)(2,1)S(1)} %bitcast.70), channel_id=1, source_target_pairs={{0,64},{64,0},{1,65},{65,1},{2,66},{66,2},{3,67},{67,3},{4,68},{68... | collective-permute-start | bytes 1769480 | tf_op jit(solution)/shard_map/ppermute | solution.py:54
  124.9 1.2 collective-permute-done.2
  126.1 12.2 %collective-permute-done.3 = bf16[288,384]{1,0:T(8,128)(2,1)} collective-permute-done((bf16[288,384]{1,0:T(8,128)(2,1)}, bf16[288,384]{1,0:T(8,128)(2,1)}, u32[]{:S(2)}, u32[]{:S(2)}) %collective-permute-start.3) | collective-permute-done | bytes 221216 | tf_op jit(solution)/shard_map/ppermute | solution.py:29
  138.4 1.8 %multiply_reduce_fusion.2 = (f32[288]{0:T(512)S(1)}, bf16[288,384]{1,0:T(8,128)(2,1)S(1)}) fusion(f32[864,384]{1,0:T(8,128)S(1)} %maximum_convert_fusion, f32[384]{0:T(512)S(1)} %copy-done.8, bf16[288,384]{1,0:T(8,128)(2,1)} %collective-permute-done.3, bf16[288,384]{1,0:T(8,128)(2,1)} %collective-permute-done.2, f32[864,384]{1,0:T(8,128)} %get-tuple-element.45, ...), kind=kOutput, calls=%fused_computation.141 | convolution fusion | flops 86040288 | bytes 2067584 | tf_op jit(solution)/shard_map/dot_general | solution.py:15
  140.3 0.9 fusion.66
  141.5 1.0 slice_bitcast_fusion
  142.4 1.5 %multiply_reduce_fusion = (f32[384]{0:T(512)S(1)}, f32[384,1152]{1,0:T(8,128)}) fusion(bf16[384,1152]{1,0:T(8,128)(2,1)S(1)} %copy-done.1, f32[384,384]{1,0:T(8,128)S(1)} %get-tuple-element.19, f32[384,384]{1,0:T(8,128)S(1)} %get-tuple-element.20, f32[384,384]{1,0:T(8,128)S(1)} %get-tuple-element.21), kind=kLoop, calls=%fused_computation.2 | loop fusion | flops 2211456 | bytes 4425216 | tf_op jit(solution)/shard_map/reduce_sum | solution.py:131
  143.9 0.6 div.82
  (72 shorter events, 13.7 us)
Async XLA Ops:
  0.6 21.7 %copy-start = (bf16[384,384]{1,0:T(8,128)(2,1)S(1)}, bf16[384,384]{1,0:T(8,128)(2,1)}, u32[]{:S(2)}) copy-start(bf16[384,384]{1,0:T(8,128)(2,1)} %param.13) | copy-start | bytes 884740
  0.6 24.1 %collective-permute-start.1 = (bf16[288,384]{1,0:T(8,128)(2,1)}, bf16[288,384]{1,0:T(8,128)(2,1)S(1)}, u32[]{:S(2)}, u32[]{:S(2)}) collective-permute-start(bf16[288,384]{1,0:T(8,128)(2,1)} %bitcast.72), channel_id=1, source_target_pairs={{1,0},{2,1},{3,2},{4,3},{5,4},{6,5},{7,6},{8,7},{9,8},{10,9},{11,1... | collective-permute-start | bytes 663560 | tf_op jit(solution)/shard_map/ppermute | solution.py:29
  15.3 21.6 %collective-permute-start = (bf16[288,384]{1,0:T(8,128)(2,1)}, bf16[288,384]{1,0:T(8,128)(2,1)S(1)}, u32[]{:S(2)}, u32[]{:S(2)}) collective-permute-start(bf16[288,384]{1,0:T(8,128)(2,1)} %bitcast.73), channel_id=1, source_target_pairs={{0,1},{1,2},{2,3},{3,4},{4,5},{5,6},{6,7},{7,8},{8,9},{9,10},{10,1... | collective-permute-start | bytes 663560 | tf_op jit(solution)/shard_map/ppermute | solution.py:29
  18.6 3.7 %copy-start.6 = (bf16[1,288,384]{2,1,0:T(8,128)(2,1)S(1)}, bf16[1,288,384]{2,1,0:T(8,128)(2,1)}, u32[]{:S(2)}) copy-start(bf16[1,288,384]{2,1,0:T(8,128)(2,1)} %param.8) | copy-start | bytes 663556
  20.0 16.9 %copy-start.2 = (bf16[1,288,384]{2,1,0:T(8,128)(2,1)S(1)}, bf16[1,288,384]{2,1,0:T(8,128)(2,1)}, u32[]{:S(2)}) copy-start(bf16[1,288,384]{2,1,0:T(8,128)(2,1)} %param.7) | copy-start | bytes 663556
  20.0 17.1 %copy-start.8 = (f32[384]{0:T(512)S(1)}, f32[384]{0:T(512)}, u32[]{:S(2)}) copy-start(f32[384]{0:T(512)} %param.11) | copy-start | bytes 4612
  22.3 15.1 %copy-start.1 = (bf16[384,1152]{1,0:T(8,128)(2,1)S(1)}, bf16[384,1152]{1,0:T(8,128)(2,1)}, u32[]{:S(2)}) copy-start(bf16[384,1152]{1,0:T(8,128)(2,1)} %param.12) | copy-start | bytes 2654212
  36.9 0.8 copy-start.3
  51.4 1.7 %copy-start.5 = (bf16[288,384]{0,1:T(8,128)(2,1)}, bf16[288,384]{0,1:T(8,128)(2,1)S(1)}, u32[]{:S(2)}) copy-start(bf16[288,384]{0,1:T(8,128)(2,1)S(1)} %fusion.24) | copy-start | bytes 663556
  57.9 1.1 copy-start.4
  60.3 4.1 %collective-permute-start.4 = (bf16[768,384]{1,0:T(8,128)(2,1)}, bf16[768,384]{1,0:T(8,128)(2,1)S(1)}, u32[]{:S(2)}, u32[]{:S(2)}) collective-permute-start(bf16[768,384]{1,0:T(8,128)(2,1)} %fusion.55), channel_id=1, source_target_pairs={{0,64},{64,0},{1,65},{65,1},{2,66},{66,2},{3,67},{67,3},{4,68},{68... | collective-permute-start | bytes 1769480 | tf_op jit(solution)/shard_map/ppermute | solution.py:47
  98.0 25.0 %all-to-all-start.2 = ((bf16[32,24,384]{2,1,0:T(8,128)(2,1)}), bf16[32,24,384]{2,1,0:T(8,128)(2,1)S(1)}, u32[]{:S(2)}, u32[]{:S(2)}) async-start(bf16[32,24,384]{2,1,0:T(8,128)(2,1)} %broadcast_in_dim.45), calls=%async_computation.2 | async-start | bytes 1179648 | tf_op jit(solution)/shard_map/all_to_all | solution.py:35
  108.2 17.9 %collective-permute-start.2 = (bf16[288,384]{1,0:T(8,128)(2,1)}, bf16[288,384]{1,0:T(8,128)(2,1)}, u32[]{:S(2)}, u32[]{:S(2)}) collective-permute-start(bf16[288,384]{1,0:T(8,128)(2,1)} %get-tuple-element.22), channel_id=1, source_target_pairs={{1,0},{2,1},{3,2},{4,3},{5,4},{6,5},{7,6},{8,7},{9,8},{10,9},{11,1... | collective-permute-start | bytes 663560 | tf_op jit(solution)/shard_map/ppermute | solution.py:29
  118.4 20.0 %collective-permute-start.3 = (bf16[288,384]{1,0:T(8,128)(2,1)}, bf16[288,384]{1,0:T(8,128)(2,1)}, u32[]{:S(2)}, u32[]{:S(2)}) collective-permute-start(bf16[288,384]{1,0:T(8,128)(2,1)} %get-tuple-element.23), channel_id=1, source_target_pairs={{0,1},{1,2},{2,3},{3,4},{4,5},{5,6},{6,7},{7,8},{8,9},{9,10},{10,1... | collective-permute-start | bytes 663560 | tf_op jit(solution)/shard_map/ppermute | solution.py:29
  121.4 18.8 %copy-start.7 = (bf16[1,288,384]{2,1,0:T(8,128)(2,1)S(1)}, bf16[1,288,384]{2,1,0:T(8,128)(2,1)}, u32[]{:S(2)}) copy-start(bf16[1,288,384]{2,1,0:T(8,128)(2,1)} %param.8) | copy-start | bytes 663556
  123.0 18.1 %collective-permute-start.5 = (bf16[768,384]{1,0:T(8,128)(2,1)S(1)}, bf16[768,384]{1,0:T(8,128)(2,1)S(1)}, u32[]{:S(2)}, u32[]{:S(2)}) collective-permute-start(bf16[768,384]{1,0:T(8,128)(2,1)S(1)} %bitcast.70), channel_id=1, source_target_pairs={{0,64},{64,0},{1,65},{65,1},{2,66},{66,2},{3,67},{67,3},{4,68},{68... | collective-permute-start | bytes 1769480 | tf_op jit(solution)/shard_map/ppermute | solution.py:54

commit v2 on v1

v2 whole, which is shorter than its diff:
```python
import math

import jax
import jax.numpy as jnp
from jax import lax
from jax.experimental import pallas as pl
from jax.experimental.pallas import tpu as pltpu
from jax.sharding import Mesh
from jax.sharding import PartitionSpec as P

HEADS = 6
SIDE = 9
ROWS = 288
WIDTH = 384
HEAD = 64
KEYS = 896
SPACE = ("yh", "x", "z")
HIDDEN = -1e30


def inner(left, right):
    return lax.dot_general(
        left, right, (((1,), (1,)), ((), ())), preferred_element_type=jnp.float32
    )


def dot(left, right):
    return jnp.dot(left, right, preferred_element_type=jnp.float32)


def swapped(block, first):
    count = lax.axis_size(SPACE)
    pairs = [(i, i + 1) for i in range(first, count - 1, 2)]
    return lax.ppermute(block, SPACE, pairs + [(b, a) for a, b in pairs])


def spread(part, axes):
    count = lax.axis_size(axes)
    copies = jnp.broadcast_to(part[None], (count,) + part.shape)
    return lax.all_to_all(copies, axes, 0, 0, tiled=True)


def total(parts):
    return jnp.sum(parts.astype(jnp.float32), axis=0).astype(jnp.bfloat16)


def attention_kernel(
    core, near, far, own, kv, q8, q8t, g, scaled, fq, fk, gain, wkv,
    out, dt, dq, normed, table, scores, expo, dshare, dscores,
):
    def unit(ref):
        values = ref[...].astype(jnp.float32)
        power = jnp.mean(values * values, axis=1, keepdims=True)
        return (values * lax.rsqrt(power + 1e-06) * gain[...]).astype(jnp.bfloat16)

    normed[0:ROWS] = own[...]
    normed[ROWS : 2 * ROWS] = unit(near)
    normed[2 * ROWS : 3 * ROWS] = unit(far)
    normed[3 * ROWS : KEYS] = jnp.zeros((KEYS - 3 * ROWS, WIDTH), jnp.bfloat16)
    table[0:ROWS] = kv[...]
    table[ROWS : 3 * ROWS] = dot(normed[ROWS : 3 * ROWS], wkv[...]).astype(jnp.bfloat16)
    table[3 * ROWS : KEYS] = jnp.zeros((KEYS - 3 * ROWS, 2 * WIDTH), jnp.bfloat16)
    low = lax.broadcasted_iota(jnp.int32, (ROWS, 128), 1) < HEAD
    chunks = [slice(at, at + 32) for at in range(0, ROWS, 32)]
    attn = []
    for pair in range(HEADS // 2):
        lanes = slice(pair * 128, pair * 128 + 128)
        keys = table[:, lanes]
        values = table[:, WIDTH + pair * 128 : WIDTH + pair * 128 + 128]
        wide_keys = jnp.concatenate([keys, fk[...]], axis=1)
        outs, grads, dqs = [], [], []
        for half in range(2):
            head = 2 * pair + half
            keep = low if half == 0 else jnp.logical_not(low)
            zero = jnp.zeros((ROWS, 128), jnp.float32)
            queries = jnp.where(keep, q8[:, lanes].astype(jnp.float32), zero)
            queries = jnp.concatenate([queries.astype(jnp.bfloat16), fq[...]], axis=1)
            scores[half] = inner(queries, wide_keys)
            shares = []
            for rows in chunks:
                block = scores[half, rows]
                block = jnp.exp(block - jnp.max(block, axis=1, keepdims=True))
                shares.append(1.0 / jnp.sum(block, axis=1, keepdims=True))
                expo[half, rows] = block.astype(jnp.bfloat16)
            share = jnp.concatenate(shares, axis=0)
            result = dot(expo[half], values) * share
            grad = jnp.where(keep, g[:, lanes] * share, zero).astype(jnp.bfloat16)
            delta = jnp.sum(grad.astype(jnp.float32) * result, axis=1, keepdims=True)
            dshare[half] = inner(grad, values)
            for rows in chunks:
                block = expo[half, rows].astype(jnp.float32)
                block = block * (dshare[half, rows] - delta[rows])
                dscores[half, rows] = block.astype(jnp.bfloat16)
            dqs.append(dot(dscores[half], keys) * (1.0 / math.sqrt(HEAD)))
            at = slice(head * HEAD, head * HEAD + HEAD)
            dt[at] = dot(q8t[at], dscores[half]).astype(jnp.bfloat16)
            outs.append(result)
            grads.append(grad)
        attn.append(jnp.where(low, outs[0], outs[1]).astype(jnp.bfloat16))
        dq[:, lanes] = jnp.where(low, dqs[0], dqs[1]).astype(jnp.bfloat16)
        turned = (grads[0] + grads[1]).T
        for half in range(2):
            at = WIDTH + (2 * pair + half) * HEAD
            part = turned[half * HEAD : half * HEAD + HEAD]
            dt[at : at + HEAD] = dot(part, expo[half]).astype(jnp.bfloat16)
    mine = core[0]
    normed_t = normed[...].T
    out[mine, 0:WIDTH] = dot(normed[0:ROWS].T, dq[...]).astype(jnp.bfloat16)
    out[mine, WIDTH:] = inner(normed_t, dt[0:WIDTH]).astype(jnp.bfloat16)
    out[1 - mine, 0:WIDTH] = inner(normed_t, dt[WIDTH:]).astype(jnp.bfloat16)
    attn_t = jnp.concatenate(attn, axis=1).T
    out[1 - mine, WIDTH:] = dot(attn_t, scaled[...]).astype(jnp.bfloat16)


def output_kernel(core, mine, other, wqkv, gain, grad_qkv, grad_out, grad_gain):
    scale = 1.0 / math.sqrt(512 * ROWS)
    me = core[0]

    def halves(first, second):
        query = first[0:WIDTH].astype(jnp.float32) * scale
        key = first[WIDTH:].astype(jnp.float32) * scale
        value = second[0:WIDTH].astype(jnp.float32) * scale
        grad_qkv[:, 0:WIDTH] = query
        grad_qkv[:, WIDTH : 2 * WIDTH] = key
        grad_qkv[:, 2 * WIDTH :] = value
        grad_out[...] = second[WIDTH:].astype(jnp.float32) * scale
        moved = query * wqkv[:, 0:WIDTH].astype(jnp.float32)
        moved += key * wqkv[:, WIDTH : 2 * WIDTH].astype(jnp.float32)
        moved += value * wqkv[:, 2 * WIDTH :].astype(jnp.float32)
        grad_gain[...] = jnp.sum(moved.T, axis=0, keepdims=True) / gain[...]

    @pl.when(me == 0)
    def _():
        halves(mine, other)

    @pl.when(me == 1)
    def _():
        halves(other, mine)


def shards(tokens, cotangent, neighbours, active, gain, w_qkv, w_out):
    values = tokens[0]
    cot = cotangent[0]
    lists = neighbours[0]
    alive = active[0]
    block = ROWS // SIDE
    position = lax.axis_index(SPACE)
    core = lax.axis_index("c")
    near = swapped(values, 0)
    far = swapped(values, 1)

    values32 = values.astype(jnp.float32)
    root = lax.rsqrt(jnp.mean(values32 * values32, axis=1, keepdims=True) + 1e-06)
    own = (values32 * root * gain).astype(jnp.bfloat16)
    w_query = w_qkv[:, :WIDTH]
    w_keyval = w_qkv[:, WIDTH:]
    q8 = (dot(own, w_query).astype(jnp.bfloat16) * (1.0 / math.sqrt(HEAD))).astype(jnp.bfloat16)
    kv = dot(own, w_keyval).astype(jnp.bfloat16)
    scaled = (
        cot.reshape(SIDE, block, WIDTH) * alive.astype(jnp.bfloat16)[:, None, None]
    ).reshape(ROWS, WIDTH)
    d_attn = inner(scaled, w_out).astype(jnp.bfloat16).astype(jnp.float32)
    parity = position % 2
    slabs = jnp.stack([position, position + 1 - 2 * parity, position - 1 + 2 * parity])
    ids = (slabs[:, None] * SIDE + jnp.arange(SIDE)[None, :]).reshape(-1)
    seen = jnp.any((lists[:, :, None] == ids) & (lists[:, :, None] >= 0), axis=1)
    hidden = jnp.where(seen, 0.0, HIDDEN).T.astype(jnp.bfloat16)
    fk = jnp.pad(jnp.repeat(hidden, block, axis=0), ((0, KEYS - 3 * ROWS), (0, 0)), constant_values=HIDDEN)
    fk = jnp.pad(fk, ((0, 0), (0, 128 - SIDE)))
    row_block = lax.broadcasted_iota(jnp.int32, (ROWS, 128), 0) // block
    fq = (row_block == lax.broadcasted_iota(jnp.int32, (ROWS, 128), 1)).astype(jnp.bfloat16)

    whole = pl.BlockSpec(memory_space=pltpu.VMEM)
    scalar = pl.BlockSpec(memory_space=pltpu.SMEM)
    core_ref = jnp.reshape(core, (1,)).astype(jnp.int32)
    blocks, d_table, d_queries = pl.pallas_call(
        attention_kernel,
        out_shape=(
            jax.ShapeDtypeStruct((2, 2 * WIDTH, WIDTH), jnp.bfloat16),
            jax.ShapeDtypeStruct((2 * WIDTH, KEYS), jnp.bfloat16),
            jax.ShapeDtypeStruct((ROWS, WIDTH), jnp.bfloat16),
        ),
        in_specs=[scalar] + [whole] * 12,
        out_specs=(whole,) * 3,
        scratch_shapes=[
            pltpu.VMEM((KEYS, WIDTH), jnp.bfloat16),
            pltpu.VMEM((KEYS, 2 * WIDTH), jnp.bfloat16),
            pltpu.VMEM((2, ROWS, KEYS), jnp.float32),
            pltpu.VMEM((2, ROWS, KEYS), jnp.bfloat16),
            pltpu.VMEM((2, ROWS, KEYS), jnp.float32),
            pltpu.VMEM((2, ROWS, KEYS), jnp.bfloat16),
        ],
        compiler_params=pltpu.CompilerParams(vmem_limit_bytes=40 * 2**20),
        cost_estimate=pl.CostEstimate(flops=3 * 10**9, bytes_accessed=4 * 10**6, transcendentals=1500000),
        name="attention",
    )(core_ref, near, far, own, kv, q8, q8.T, d_attn, scaled, fq, fk, gain[None], w_keyval)

    pair = [(0, 1), (1, 0)]
    half = total(jnp.stack([blocks[0], lax.ppermute(blocks[1], "c", pair)]))
    plane = lax.axis_size(("x", "z"))
    parts = half.reshape(plane, 2 * WIDTH // plane, WIDTH)
    part = total(lax.all_to_all(parts, ("x", "z"), 0, 0, tiled=True))
    part = total(spread(part, ("yl", "yh")))
    half = spread(part, ("x", "z")).reshape(2 * WIDTH, WIDTH)
    other = lax.ppermute(half, "c", pair)

    back = lax.dot_general(
        d_table, w_keyval, (((0,), (1,)), ((), ())), preferred_element_type=jnp.float32
    )
    back_near = swapped(back[ROWS : 2 * ROWS].astype(jnp.bfloat16), 0)
    back_far = swapped(back[2 * ROWS : 3 * ROWS].astype(jnp.bfloat16), 1)
    d_normed = inner(d_queries, w_query) + back[:ROWS]
    d_normed = d_normed + back_near.astype(jnp.float32) + back_far.astype(jnp.float32)
    d_normed = d_normed.astype(jnp.bfloat16).astype(jnp.float32)
    inward = d_normed * gain
    slope = jnp.mean(inward * values32, axis=1, keepdims=True) * root * root
    grad_input = cot.astype(jnp.float32) + root * (inward - values32 * slope)

    grad_wqkv, grad_wout, grad_gain = pl.pallas_call(
        output_kernel,
        out_shape=(
            jax.ShapeDtypeStruct((WIDTH, 3 * WIDTH), jnp.float32),
            jax.ShapeDtypeStruct((WIDTH, WIDTH), jnp.float32),
            jax.ShapeDtypeStruct((1, WIDTH), jnp.float32),
        ),
        in_specs=[scalar] + [whole] * 4,
        out_specs=(whole,) * 3,
        compiler_params=pltpu.CompilerParams(vmem_limit_bytes=24 * 2**20),
        name="outputs",
    )(core_ref, half, other, w_qkv, gain[None])
    return (grad_input.astype(jnp.bfloat16)[None], grad_wqkv, grad_wout, grad_gain[0])


def solution(mesh):
    fine = Mesh(mesh.devices.reshape(4, 2, 2, 4, 8), ("yl", "c", "yh", "x", "z"))
    region = ("yl", "c")
    split = P(region, SPACE, None)
    return jax.shard_map(
        shards,
        mesh=fine,
        in_specs=(split, split, split, P(region, SPACE), P(), P(), P()),
        out_specs=(split, P(), P(), P()),
        check_vma=False,
    )
```

time: 145 us -> 122 us (0.84)
  the two profiles are of different devices: /device:TPU:48 before, /device:TPU:1 now
where the time goes in v2:
time: 122 us; the launch traced here: 121 us
  blocking collectives  46 us (38%)
  starting transfers between devices  36.5 us (30%)
  Pallas kernels  10.8 us (9%)
  local copies, waits for them, and re-layouts  8.02 us (7%)
  matrix products  6.45 us (5%)
  waiting for transfers between devices  6.36 us (5%)
  other arithmetic  5.69 us (5%)
    all_to_all x1, blocking collectives, shards(): part = total(lax.all_to_all(parts, ('x', 'z'), 0, 0, tiled=True))  31.5 us
    all_to_all x1, blocking collectives, spread(): return lax.all_to_all(copies, axes, 0, 0, tiled=True)  14.6 us
    ppermute x4, starting transfers between devices, swapped(): return lax.ppermute(block, SPACE, pairs + [(b, a) for a, b in pairs])  11.8 us
    ppermute x1, starting transfers between devices, shards(): other = lax.ppermute(half, 'c', pair)  10.5 us
    pallas_call x1, Pallas kernels, shards(): pl.pallas_call(attention_kernel, out_shape=(jax.ShapeDtypeStruct((2, 2 *...  8.98 us
    all_to_all x1, starting transfers between devices, spread(): return lax.all_to_all(copies, axes, 0, 0, tiled=True)  8.26 us
    ppermute x1, starting transfers between devices, shards(): half = total(jnp.stack([blocks[0], lax.ppermute(blocks[1], 'c', pair)]))  5.88 us
    unnamed x33, local copies, waits for them, and re-layouts  5.38 us
  transfers between devices with their start and end apart: 7, of which 2 were waited for; matrix products, arithmetic and copies ran while one was open for 10% of the time, Pallas kernels for 0%

profile of v2, /device:TPU:1, one launch (start us, length us, event | category | flops | bytes accessed | tf_op | source)
XLA Modules:
  0.0 120.8 jit_solution(3420489832525750787)
XLA Ops:
  0.6 0.0 copy-start
  0.7 5.0 %collective-permute-start = (bf16[288,384]{1,0:T(8,128)(2,1)}, bf16[288,384]{1,0:T(8,128)(2,1)S(1)}, u32[]{:S(2)}, u32[]{:S(2)}) collective-permute-start(bf16[288,384]{1,0:T(8,128)(2,1)} %bitcast.40), channel_id=1, source_target_pairs={{0,1},{2,3},{4,5},{6,7},{8,9},{10,11},{12,13},{14,15},{16,17},{18,... | collective-permute-start | bytes 663560 | tf_op jit(solution)/shard_map/ppermute | solution.py:34
  5.7 0.7 collective-permute-start.1
  6.3 1.1 fusion.7
  7.4 1.1 fusion.9.own
  8.5 2.2 %convolution_convert_fusion.kv = bf16[288,768]{1,0:T(8,128)(2,1)} fusion(bf16[288,384]{1,0:T(8,128)(2,1)S(1)} %fusion.9.own, bf16[384,1152]{1,0:T(8,128)(2,1)} %wqkv.1), kind=kOutput, calls=%fused_computation | convolution fusion | flops 170090496 | bytes 1253376 | tf_op jit(solution)/shard_map/dot_general | solution.py:28
  10.7 0.3 convolution_convert_fusion.2
  11.2 0.0 copy-start.15
  11.2 0.9 slice.23.wkv
  12.0 0.2 copy.16
  12.2 0.1 fusion.23
  12.3 0.2 copy.18.q8
  12.5 0.1 mul.105
  12.6 0.1 mul.106
  12.7 0.1 add_multiply_fusion
  12.8 0.1 iota_add_fusion
  12.8 0.1 add.79
  12.9 0.2 and_reduce_fusion
  13.1 0.1 copy.17
  13.2 0.1 fusion.6.fk
  13.3 0.1 bitcast_multiply_fusion.scaled
  13.5 0.3 fusion.5.g
  13.8 0.2 fusion.18.fq
  14.0 0.7 copy-done.6
  14.7 0.7 copy-done.8
  15.4 1.1 copy-done.2
  16.4 1.0 copy-done.3
  17.4 0.9 copy-done.7
  18.4 0.9 copy-done.9
  19.3 9.0 %attention.1 = (bf16[2,768,384]{2,1,0:T(8,128)(2,1)S(1)}, bf16[768,896]{1,0:T(8,128)(2,1)S(1)}, bf16[288,384]{1,0:T(8,128)(2,1)S(1)}) custom-call(s32[1]{0:T(128)} %bitcast.2.core, bf16[288,384]{1,0:T(8,128)(2,1)S(1)} %copy-done.7, bf16[288,384]{1,0:T(8,128)(2,1)S(1)} %copy-done.9, bf16[288,384]{1,0:T(8,128)(2,1)S(1)} %fusion.9.own, ...), custom_call_target="tpu_custom_call" | custom-call | flops 3000000000 | bytes 4000000 | tf_op jit(solution)/shard_map/attention/pallas_call | solution.py:176
  28.3 0.1 slice_bitcast_fusion
  28.4 5.9 %collective-permute-start.4 = (bf16[768,384]{1,0:T(8,128)(2,1)S(1)}, bf16[768,384]{1,0:T(8,128)(2,1)S(1)}, u32[]{:S(2)}, u32[]{:S(2)}) collective-permute-start(bf16[768,384]{1,0:T(8,128)(2,1)S(1)} %slice_bitcast_fusion), channel_id=1, source_target_pairs={{0,64},{64,0},{1,65},{65,1},{2,66},{66,2},{3,67},{67,3},{4,68},{68... | collective-permute-start | bytes 1769480 | tf_op jit(solution)/shard_map/ppermute | solution.py:199
  34.3 1.6 %collective-permute-done.4 = bf16[768,384]{1,0:T(8,128)(2,1)S(1)} collective-permute-done((bf16[768,384]{1,0:T(8,128)(2,1)S(1)}, bf16[768,384]{1,0:T(8,128)(2,1)S(1)}, u32[]{:S(2)}, u32[]{:S(2)}) %collective-permute-start.4) | collective-permute-done | bytes 589856 | tf_op jit(solution)/shard_map/ppermute | solution.py:199
  35.9 0.1 bitcast_add_fusion
  36.0 31.5 %all_to_all.15 = bf16[32,24,384]{2,1,0:T(8,128)(2,1)} all-to-all(bf16[32,24,384]{2,1,0:T(8,128)(2,1)S(1)} %bitcast.42), channel_id=1, replica_groups=mesh['yl'=4,'c'=2,'yh'=2,'x'=4,'z'=8] {'x','z'}, dimensions={0} | all-to-all | bytes 1179648 | tf_op jit(solution)/shard_map/all_to_all | solution.py:202
  67.4 1.2 reduce_sum.58
  68.6 14.6 %all_to_all.16 = bf16[8,24,384]{2,1,0:T(8,128)(2,1)S(1)} all-to-all(bf16[8,24,384]{2,1,0:T(8,128)(2,1)S(1)} %broadcast_in_dim.42), channel_id=1, replica_groups=mesh['yl'=4,'c'=2,'yh'=2,'x'=4,'z'=8] {'yl','yh'}, dimensions={0} | all-to-all | bytes 294912 | tf_op jit(solution)/shard_map/all_to_all | solution.py:40
  83.2 0.9 broadcast_in_dim.43
  84.1 8.3 %all-to-all-start.2 = ((bf16[32,24,384]{2,1,0:T(8,128)(2,1)}), bf16[32,24,384]{2,1,0:T(8,128)(2,1)S(1)}, u32[]{:S(2)}, u32[]{:S(2)}) async-start(bf16[32,24,384]{2,1,0:T(8,128)(2,1)} %broadcast_in_dim.43), calls=%async_computation.2 | async-start | bytes 1179648 | tf_op jit(solution)/shard_map/all_to_all | solution.py:40
  92.3 2.0 %fusion.28 = (bf16[896,384]{1,0:T(8,128)(2,1)S(1)}, f32[896,384]{1,0:T(8,128)}) fusion(bf16[768,896]{1,0:T(8,128)(2,1)S(1)} %get-tuple-element.11, bf16[384,1152]{1,0:T(8,128)(2,1)S(1)} %copy-done.1), kind=kOutput, calls=%fused_computation.55 | convolution fusion | flops 528826368 | bytes 4030464 | tf_op jit(solution)/shard_map/dot_general | solution.py:207
  94.4 0.8 collective-permute-start.3
  95.2 5.4 %collective-permute-start.2 = (bf16[288,384]{1,0:T(8,128)(2,1)S(1)}, bf16[288,384]{1,0:T(8,128)(2,1)S(1)}, u32[]{:S(2)}, u32[]{:S(2)}) collective-permute-start(bf16[288,384]{1,0:T(8,128)(2,1)S(1)} %get-tuple-element.16), channel_id=1, source_target_pairs={{0,1},{2,3},{4,5},{6,7},{8,9},{10,11},{12,13},{14,15},{16,17},{18,... | collective-permute-start | bytes 663560 | tf_op jit(solution)/shard_map/ppermute | solution.py:34
  100.6 4.7 %all-to-all-done.2 = bf16[32,24,384]{2,1,0:T(8,128)(2,1)S(1)} async-done(((bf16[32,24,384]{2,1,0:T(8,128)(2,1)}), bf16[32,24,384]{2,1,0:T(8,128)(2,1)S(1)}, u32[]{:S(2)}, u32[]{:S(2)}) %all-to-all-start.2) | async-done | bytes 589856 | tf_op jit(solution)/shard_map/all_to_all | solution.py:40
  105.3 10.5 %collective-permute-start.5 = (bf16[768,384]{1,0:T(8,128)(2,1)S(1)}, bf16[768,384]{1,0:T(8,128)(2,1)S(1)}, u32[]{:S(2)}, u32[]{:S(2)}) collective-permute-start(bf16[768,384]{1,0:T(8,128)(2,1)S(1)} %bitcast.38), channel_id=1, source_target_pairs={{0,64},{64,0},{1,65},{65,1},{2,66},{66,2},{3,67},{67,3},{4,68},{68... | collective-permute-start | bytes 1769480 | tf_op jit(solution)/shard_map/ppermute | solution.py:205
  115.9 1.6 %fusion.10 = (f32[288]{0:T(512)S(1)}, f32[288,384]{1,0:T(8,128)S(1)}) fusion(bf16[1,288,384]{2,1,0:T(8,128)(2,1)} %param.7, f32[384]{0:T(512)S(1)} %copy-done.14, bf16[288,384]{1,0:T(8,128)(2,1)S(1)} %collective-permute-done.3, bf16[288,384]{1,0:T(8,128)(2,1)S(1)} %collective-permute-done.2, f32[896,384]{1,0:T(8,128)} %get-tuple-element.21, ...), kind=kOutput, calls=%fused_computation.21 | convolution fusion | flops 86150880 | bytes 2067584 | tf_op jit(solution)/shard_map/dot_general | solution.py:22
  117.6 0.9 fusion.17
  118.4 1.8 %outputs.1 = (f32[384,1152]{1,0:T(8,128)}, f32[384,384]{1,0:T(8,128)}, f32[1,384]{1,0:T(1,128)S(1)}) custom-call(s32[1]{0:T(128)} %bitcast.2.core, bf16[768,384]{1,0:T(8,128)(2,1)S(1)} %bitcast.39, bf16[768,384]{1,0:T(8,128)(2,1)S(1)} %collective-permute-done.5.other, bf16[384,1152]{1,0:T(8,128)(2,1)S(1)} %copy-done.1, f32[1,384]{1,0:T(1,128)S(1)} %broadcast_in_dim.21.gain), custom_call_target="tpu_custom_call" | custom-call | tf_op jit(solution)/shard_map/outputs/pallas_call | solution.py:219
  120.2 0.6 reduce.5
  (42 shorter events, 0.2 us)
Async XLA Ops:
  0.6 12.8 %copy-start = (bf16[384,384]{1,0:T(8,128)(2,1)S(1)}, bf16[384,384]{1,0:T(8,128)(2,1)}, u32[]{:S(2)}) copy-start(bf16[384,384]{1,0:T(8,128)(2,1)} %param.13) | copy-start | bytes 884740
  0.6 10.5 %copy-start.14 = (f32[384]{0:T(512)S(1)}, f32[384]{0:T(512)}, u32[]{:S(2)}) copy-start(f32[384]{0:T(512)} %param.11) | copy-start | bytes 4612
  0.7 10.1 %copy-start.1 = (bf16[384,1152]{1,0:T(8,128)(2,1)S(1)}, bf16[384,1152]{1,0:T(8,128)(2,1)}, u32[]{:S(2)}) copy-start(bf16[384,1152]{1,0:T(8,128)(2,1)} %wqkv.1) | copy-start | bytes 2654212
  0.7 10.4 %copy-start.13 = (s32[1,9,27]{2,0,1:T(1,128)S(1)}, s32[1,9,27]{2,0,1:T(1,128)}, u32[]{:S(2)}) copy-start(s32[1,9,27]{2,0,1:T(1,128)} %param.9) | copy-start | bytes 2920
  0.7 13.3 %collective-permute-start = (bf16[288,384]{1,0:T(8,128)(2,1)}, bf16[288,384]{1,0:T(8,128)(2,1)S(1)}, u32[]{:S(2)}, u32[]{:S(2)}) collective-permute-start(bf16[288,384]{1,0:T(8,128)(2,1)} %bitcast.40), channel_id=1, source_target_pairs={{0,1},{2,3},{4,5},{6,7},{8,9},{10,11},{12,13},{14,15},{16,17},{18,... | collective-permute-start | bytes 663560 | tf_op jit(solution)/shard_map/ppermute | solution.py:34
  5.7 9.0 %collective-permute-start.1 = (bf16[288,384]{1,0:T(8,128)(2,1)}, bf16[288,384]{1,0:T(8,128)(2,1)S(1)}, u32[]{:S(2)}, u32[]{:S(2)}) collective-permute-start(bf16[288,384]{1,0:T(8,128)(2,1)} %bitcast.41), channel_id=1, source_target_pairs={{1,2},{3,4},{5,6},{7,8},{9,10},{11,12},{13,14},{15,16},{17,18},{19... | collective-permute-start | bytes 663560 | tf_op jit(solution)/shard_map/ppermute | solution.py:34
  11.2 1.3 %copy-start.15 = (s32[1,9]{1,0:T(1,128)S(1)}, s32[1,9]{1,0:T(1,128)}, u32[]{:S(2)}) copy-start(s32[1,9]{1,0:T(1,128)} %param.10) | copy-start | bytes 112
  12.0 1.3 %copy-start.11 = (bf16[1,288,384]{2,1,0:T(8,128)(2,1)S(1)}, bf16[1,288,384]{2,1,0:T(8,128)(2,1)}, u32[]{:S(2)}) copy-start(bf16[1,288,384]{2,1,0:T(8,128)(2,1)} %param.8) | copy-start | bytes 663556
  14.0 0.7 copy-start.6
  14.7 0.7 copy-start.8
  15.4 1.1 copy-start.2
  16.4 1.0 copy-start.3
  17.4 0.9 copy-start.7
  18.4 0.9 copy-start.9
  28.3 7.7 %copy-start.4 = (bf16[288,384]{1,0:T(8,128)(2,1)}, bf16[288,384]{1,0:T(8,128)(2,1)S(1)}, u32[]{:S(2)}) copy-start(bf16[288,384]{1,0:T(8,128)(2,1)S(1)} %get-tuple-element.10) | copy-start | bytes 663556
  28.4 7.5 %collective-permute-start.4 = (bf16[768,384]{1,0:T(8,128)(2,1)S(1)}, bf16[768,384]{1,0:T(8,128)(2,1)S(1)}, u32[]{:S(2)}, u32[]{:S(2)}) collective-permute-start(bf16[768,384]{1,0:T(8,128)(2,1)S(1)} %slice_bitcast_fusion), channel_id=1, source_target_pairs={{0,64},{64,0},{1,65},{65,1},{2,66},{66,2},{3,67},{67,3},{4,68},{68... | collective-permute-start | bytes 1769480 | tf_op jit(solution)/shard_map/ppermute | solution.py:199
  84.1 21.3 %all-to-all-start.2 = ((bf16[32,24,384]{2,1,0:T(8,128)(2,1)}), bf16[32,24,384]{2,1,0:T(8,128)(2,1)S(1)}, u32[]{:S(2)}, u32[]{:S(2)}) async-start(bf16[32,24,384]{2,1,0:T(8,128)(2,1)} %broadcast_in_dim.43), calls=%async_computation.2 | async-start | bytes 1179648 | tf_op jit(solution)/shard_map/all_to_all | solution.py:40
  92.3 23.6 %copy-start.5 = (bf16[288,384]{1,0:T(8,128)(2,1)S(1)}, bf16[288,384]{1,0:T(8,128)(2,1)}, u32[]{:S(2)}) copy-start(bf16[288,384]{1,0:T(8,128)(2,1)} %copy-done.4) | copy-start | bytes 663556
  94.3 23.2 %copy-start.10 = (bf16[1,288,384]{2,1,0:T(8,128)(2,1)S(1)}, bf16[1,288,384]{2,1,0:T(8,128)(2,1)}, u32[]{:S(2)}) copy-start(bf16[1,288,384]{2,1,0:T(8,128)(2,1)} %param.7) | copy-start | bytes 663556
  94.4 23.2 %copy-start.12 = (bf16[1,288,384]{2,1,0:T(8,128)(2,1)S(1)}, bf16[1,288,384]{2,1,0:T(8,128)(2,1)}, u32[]{:S(2)}) copy-start(bf16[1,288,384]{2,1,0:T(8,128)(2,1)} %param.8) | copy-start | bytes 663556
  94.4 21.5 %collective-permute-start.3 = (bf16[288,384]{1,0:T(8,128)(2,1)S(1)}, bf16[288,384]{1,0:T(8,128)(2,1)S(1)}, u32[]{:S(2)}, u32[]{:S(2)}) collective-permute-start(bf16[288,384]{1,0:T(8,128)(2,1)S(1)} %get-tuple-element.17), channel_id=1, source_target_pairs={{1,2},{3,4},{5,6},{7,8},{9,10},{11,12},{13,14},{15,16},{17,18},{19... | collective-permute-start | bytes 663560 | tf_op jit(solution)/shard_map/ppermute | solution.py:34
  95.2 20.7 %collective-permute-start.2 = (bf16[288,384]{1,0:T(8,128)(2,1)S(1)}, bf16[288,384]{1,0:T(8,128)(2,1)S(1)}, u32[]{:S(2)}, u32[]{:S(2)}) collective-permute-start(bf16[288,384]{1,0:T(8,128)(2,1)S(1)} %get-tuple-element.16), channel_id=1, source_target_pairs={{0,1},{2,3},{4,5},{6,7},{8,9},{10,11},{12,13},{14,15},{16,17},{18,... | collective-permute-start | bytes 663560 | tf_op jit(solution)/shard_map/ppermute | solution.py:34
  105.3 13.1 %collective-permute-start.5 = (bf16[768,384]{1,0:T(8,128)(2,1)S(1)}, bf16[768,384]{1,0:T(8,128)(2,1)S(1)}, u32[]{:S(2)}, u32[]{:S(2)}) collective-permute-start(bf16[768,384]{1,0:T(8,128)(2,1)S(1)} %bitcast.38), channel_id=1, source_target_pairs={{0,64},{64,0},{1,65},{65,1},{2,66},{66,2},{3,67},{67,3},{4,68},{68... | collective-permute-start | bytes 1769480 | tf_op jit(solution)/shard_map/ppermute | solution.py:205

commit v3 on v2

v3 whole, which is shorter than its diff:
```python
import math

import jax
import jax.numpy as jnp
from jax import lax
from jax.experimental import pallas as pl
from jax.experimental.pallas import tpu as pltpu
from jax.sharding import Mesh
from jax.sharding import PartitionSpec as P

HEADS = 6
SIDE = 9
ROWS = 288
WIDTH = 384
HEAD = 64
KEYS = 896
SPACE = ("yh", "x", "z")
HIDDEN = -1e30


def inner(left, right):
    return lax.dot_general(
        left, right, (((1,), (1,)), ((), ())), preferred_element_type=jnp.float32
    )


def dot(left, right):
    return jnp.dot(left, right, preferred_element_type=jnp.float32)


def swapped(block, first):
    count = lax.axis_size(SPACE)
    pairs = [(i, i + 1) for i in range(first, count - 1, 2)]
    return lax.ppermute(block, SPACE, pairs + [(b, a) for a, b in pairs])


def spread(part, axes):
    count = lax.axis_size(axes)
    copies = jnp.broadcast_to(part[None], (count,) + part.shape)
    return lax.all_to_all(copies, axes, 0, 0, tiled=True)


def total(parts):
    return jnp.sum(parts.astype(jnp.float32), axis=0).astype(jnp.bfloat16)


def unit_rows(values, gain):
    power = jnp.mean(values * values, axis=1, keepdims=True)
    return values * lax.rsqrt(power + 1e-06) * gain


def prepare_kernel(alive, tokens, cot, gain, wqkv, wout, own, kv, q8, q8t, g, scaled):
    own[...] = unit_rows(tokens[...].astype(jnp.float32), gain[...]).astype(jnp.bfloat16)
    queries = dot(own[...], wqkv[:, 0:WIDTH]).astype(jnp.bfloat16).astype(jnp.float32)
    eighth = (queries * (1.0 / math.sqrt(HEAD))).astype(jnp.bfloat16)
    q8[...] = eighth
    q8t[...] = eighth.T
    kv[...] = dot(own[...], wqkv[:, WIDTH:]).astype(jnp.bfloat16)
    block = ROWS // SIDE
    for at in range(SIDE):
        rows = slice(at * block, at * block + block)
        part = cot[rows].astype(jnp.float32) * alive[at].astype(jnp.float32)
        scaled[rows] = part.astype(jnp.bfloat16)
    g[...] = inner(scaled[...], wout[...]).astype(jnp.bfloat16)


def attention_kernel(
    core, near, far, own, kv, q8, q8t, g, scaled, fq, fk, gain, wqkv,
    out, dt, dq, halo, normed, table, scores, expo, dshare, dscores, sems,
):
    copies = [
        pltpu.make_async_copy(near, halo.at[0], sems.at[0]),
        pltpu.make_async_copy(far, halo.at[1], sems.at[1]),
    ]
    for copy in copies:
        copy.start()
    normed[0:ROWS] = own[...]
    normed[3 * ROWS : KEYS] = jnp.zeros((KEYS - 3 * ROWS, WIDTH), jnp.bfloat16)
    table[0:ROWS] = kv[...]
    table[3 * ROWS : KEYS] = jnp.zeros((KEYS - 3 * ROWS, 2 * WIDTH), jnp.bfloat16)
    for side in range(2):
        copies[side].wait()
        rows = slice((side + 1) * ROWS, (side + 2) * ROWS)
        unit = unit_rows(halo[side].astype(jnp.float32), gain[...]).astype(jnp.bfloat16)
        normed[rows] = unit
        table[rows] = dot(unit, wqkv[:, WIDTH:]).astype(jnp.bfloat16)
    low = lax.broadcasted_iota(jnp.int32, (ROWS, 128), 1) < HEAD
    zero = jnp.zeros((ROWS, 128), jnp.float32)
    chunks = [slice(at, at + 32) for at in range(0, ROWS, 32)]
    attn = []
    for pair in range(HEADS // 2):
        lanes = slice(pair * 128, pair * 128 + 128)
        keys = table[:, lanes]
        values = table[:, WIDTH + pair * 128 : WIDTH + pair * 128 + 128]
        wide_keys = jnp.concatenate([keys, fk[...]], axis=1)
        outs, grads, dqs = [], [], []
        for half in range(2):
            head = 2 * pair + half
            keep = low if half == 0 else jnp.logical_not(low)
            queries = jnp.where(keep, q8[:, lanes].astype(jnp.float32), zero)
            queries = jnp.concatenate([queries.astype(jnp.bfloat16), fq[...]], axis=1)
            scores[half] = inner(queries, wide_keys)
            shares = []
            for rows in chunks:
                block = scores[half, rows]
                block = jnp.exp(block - jnp.max(block, axis=1, keepdims=True))
                shares.append(1.0 / jnp.sum(block, axis=1, keepdims=True))
                expo[half, rows] = block.astype(jnp.bfloat16)
            share = jnp.concatenate(shares, axis=0)
            result = dot(expo[half], values) * share
            grad = jnp.where(keep, g[:, lanes].astype(jnp.float32) * share, zero)
            grad = grad.astype(jnp.bfloat16)
            delta = jnp.sum(grad.astype(jnp.float32) * result, axis=1, keepdims=True)
            dshare[half] = inner(grad, values)
            for rows in chunks:
                block = expo[half, rows].astype(jnp.float32)
                block = block * (dshare[half, rows] - delta[rows])
                dscores[half, rows] = block.astype(jnp.bfloat16)
            dqs.append(dot(dscores[half], keys) * (1.0 / math.sqrt(HEAD)))
            at = slice(head * HEAD, head * HEAD + HEAD)
            dt[at] = dot(q8t[at], dscores[half]).astype(jnp.bfloat16)
            outs.append(result)
            grads.append(grad)
        attn.append(jnp.where(low, outs[0], outs[1]).astype(jnp.bfloat16))
        dq[:, lanes] = jnp.where(low, dqs[0], dqs[1]).astype(jnp.bfloat16)
        turned = (grads[0] + grads[1]).T
        for half in range(2):
            at = WIDTH + (2 * pair + half) * HEAD
            part = turned[half * HEAD : half * HEAD + HEAD]
            dt[at : at + HEAD] = dot(part, expo[half]).astype(jnp.bfloat16)
    mine = core[0]
    normed_t = normed[...].T
    out[mine, 0:WIDTH] = dot(normed[0:ROWS].T, dq[...]).astype(jnp.bfloat16)
    out[mine, WIDTH:] = inner(normed_t, dt[0:WIDTH]).astype(jnp.bfloat16)
    out[1 - mine, 0:WIDTH] = inner(normed_t, dt[WIDTH:]).astype(jnp.bfloat16)
    attn_t = jnp.concatenate(attn, axis=1).T
    out[1 - mine, WIDTH:] = dot(attn_t, scaled[...]).astype(jnp.bfloat16)


def back_kernel(dt, dq, wqkv, base, near, far):
    back = lax.dot_general(
        dt[...], wqkv[:, WIDTH:], (((0,), (1,)), ((), ())), preferred_element_type=jnp.float32
    )
    near[...] = back[ROWS : 2 * ROWS].astype(jnp.bfloat16)
    far[...] = back[2 * ROWS : 3 * ROWS].astype(jnp.bfloat16)
    base[...] = back[0:ROWS] + inner(dq[...], wqkv[:, 0:WIDTH])


def input_kernel(base, near, far, tokens, cot, gain, grad_input):
    d_normed = base[...] + near[...].astype(jnp.float32) + far[...].astype(jnp.float32)
    inward = d_normed.astype(jnp.bfloat16).astype(jnp.float32) * gain[...]
    values = tokens[...].astype(jnp.float32)
    root = lax.rsqrt(jnp.mean(values * values, axis=1, keepdims=True) + 1e-06)
    slope = jnp.mean(inward * values, axis=1, keepdims=True) * root * root
    moved = cot[...].astype(jnp.float32) + root * (inward - values * slope)
    grad_input[...] = moved.astype(jnp.bfloat16)


def output_kernel(core, mine, other, wqkv, gain, grad_qkv, grad_out, grad_gain):
    scale = 1.0 / math.sqrt(512 * ROWS)
    me = core[0]

    def halves(first, second):
        query = first[0:WIDTH].astype(jnp.float32) * scale
        key = first[WIDTH:].astype(jnp.float32) * scale
        value = second[0:WIDTH].astype(jnp.float32) * scale
        grad_qkv[:, 0:WIDTH] = query
        grad_qkv[:, WIDTH : 2 * WIDTH] = key
        grad_qkv[:, 2 * WIDTH :] = value
        grad_out[...] = second[WIDTH:].astype(jnp.float32) * scale
        moved = query * wqkv[:, 0:WIDTH].astype(jnp.float32)
        moved += key * wqkv[:, WIDTH : 2 * WIDTH].astype(jnp.float32)
        moved += value * wqkv[:, 2 * WIDTH :].astype(jnp.float32)
        grad_gain[...] = jnp.sum(moved.T, axis=0) / gain[...]

    @pl.when(me == 0)
    def _():
        halves(mine, other)

    @pl.when(me == 1)
    def _():
        halves(other, mine)


def local(body, name, shapes, in_specs, vmem, scratch=(), flops=10**8, moved=10**6):
    return pl.pallas_call(
        body,
        out_shape=tuple(jax.ShapeDtypeStruct(shape, kind) for shape, kind in shapes),
        in_specs=in_specs,
        out_specs=(pl.BlockSpec(memory_space=pltpu.VMEM),) * len(shapes),
        scratch_shapes=scratch,
        compiler_params=pltpu.CompilerParams(vmem_limit_bytes=vmem * 2**20),
        cost_estimate=pl.CostEstimate(flops=flops, bytes_accessed=moved, transcendentals=0),
        name=name,
    )


def shards(tokens, cotangent, neighbours, active, gain, w_qkv, w_out):
    values = tokens[0]
    cot = cotangent[0]
    lists = neighbours[0]
    block = ROWS // SIDE
    position = lax.axis_index(SPACE)
    core = jnp.reshape(lax.axis_index("c"), (1,)).astype(jnp.int32)
    near = swapped(values, 0)
    far = swapped(values, 1)
    gains = gain[None]

    b16, f32 = jnp.bfloat16, jnp.float32
    whole = pl.BlockSpec(memory_space=pltpu.VMEM)
    scalar = pl.BlockSpec(memory_space=pltpu.SMEM)
    anywhere = pl.BlockSpec(memory_space=pl.ANY)
    rows = ((ROWS, WIDTH), b16)
    own, kv, q8, q8t, g, scaled = local(
        prepare_kernel,
        "prepare",
        (rows, ((ROWS, 2 * WIDTH), b16), rows, ((WIDTH, ROWS), b16), rows, rows),
        [scalar] + [whole] * 5,
        8,
        flops=4 * 10**8,
    )(active[0], values, cot, gains, w_qkv, w_out)

    parity = position % 2
    slabs = jnp.stack([position, position + 1 - 2 * parity, position - 1 + 2 * parity])
    ids = (slabs[:, None] * SIDE + jnp.arange(SIDE)[None, :]).reshape(-1)
    seen = jnp.any((lists[:, :, None] == ids) & (lists[:, :, None] >= 0), axis=1)
    hidden = jnp.where(seen, 0.0, HIDDEN).T.astype(b16)
    fk = jnp.repeat(hidden, block, axis=0)
    fk = jnp.pad(fk, ((0, KEYS - 3 * ROWS), (0, 0)), constant_values=HIDDEN)
    fk = jnp.pad(fk, ((0, 0), (0, 128 - SIDE)))
    row_block = lax.broadcasted_iota(jnp.int32, (ROWS, 128), 0) // block
    fq = (row_block == lax.broadcasted_iota(jnp.int32, (ROWS, 128), 1)).astype(b16)

    blocks, d_table, d_queries = local(
        attention_kernel,
        "attention",
        (((2, 2 * WIDTH, WIDTH), b16), ((2 * WIDTH, KEYS), b16), rows),
        [scalar, anywhere, anywhere] + [whole] * 10,
        14,
        (
            pltpu.VMEM((2, ROWS, WIDTH), b16),
            pltpu.VMEM((KEYS, WIDTH), b16),
            pltpu.VMEM((KEYS, 2 * WIDTH), b16),
            pltpu.VMEM((2, ROWS, KEYS), f32),
            pltpu.VMEM((2, ROWS, KEYS), b16),
            pltpu.VMEM((2, ROWS, KEYS), f32),
            pltpu.VMEM((2, ROWS, KEYS), b16),
            pltpu.SemaphoreType.DMA((2,)),
        ),
        flops=3 * 10**9,
        moved=4 * 10**6,
    )(core, near, far, own, kv, q8, q8t, g, scaled, fq, fk, gains, w_qkv)

    pair = [(0, 1), (1, 0)]
    half = total(jnp.stack([blocks[0], lax.ppermute(blocks[1], "c", pair)]))
    base, back_near, back_far = local(
        back_kernel, "back", (((ROWS, WIDTH), f32), rows, rows), [whole] * 3, 8, flops=6 * 10**8
    )(d_table, d_queries, w_qkv)
    half, base, back_near, back_far = lax.optimization_barrier((half, base, back_near, back_far))
    back_near = swapped(back_near, 0)
    back_far = swapped(back_far, 1)
    plane = lax.axis_size(("x", "z"))
    parts = half.reshape(plane, 2 * WIDTH // plane, WIDTH)
    part = total(lax.all_to_all(parts, ("x", "z"), 0, 0, tiled=True))
    part, back_near, back_far = lax.optimization_barrier((part, back_near, back_far))
    (grad_input,) = local(input_kernel, "grad_input", (rows,), [whole] * 6, 8, moved=3 * 10**7)(
        base, back_near, back_far, values, cot, gains
    )
    part = total(spread(part, ("yl", "yh")))
    half = spread(part, ("x", "z")).reshape(2 * WIDTH, WIDTH)
    half, grad_input = lax.optimization_barrier((half, grad_input))
    other = lax.ppermute(half, "c", pair)

    grad_wqkv, grad_wout, grad_gain = local(
        output_kernel,
        "outputs",
        (((WIDTH, 3 * WIDTH), f32), ((WIDTH, WIDTH), f32), ((WIDTH,), f32)),
        [scalar] + [whole] * 4,
        8,
        moved=4 * 10**6,
    )(core, half, other, w_qkv, gain)
    return (grad_input[None], grad_wqkv, grad_wout, grad_gain)


def solution(mesh):
    fine = Mesh(mesh.devices.reshape(4, 2, 2, 4, 8), ("yl", "c", "yh", "x", "z"))
    region = ("yl", "c")
    split = P(region, SPACE, None)
    return jax.shard_map(
        shards,
        mesh=fine,
        in_specs=(split, split, split, P(region, SPACE), P(), P(), P()),
        out_specs=(split, P(), P(), P()),
        check_vma=False,
    )
```

time: 122 us -> 117 us (0.959)
  blocking collectives: 46 us -> 20.1 us
  waiting for transfers between devices: 6.36 us -> 29.8 us
  matrix products: 6.45 us -> 0 us
  Pallas kernels: 10.8 us -> 15.1 us
  starting transfers between devices: 36.5 us -> 40.2 us
  other arithmetic: 5.69 us -> 2.27 us
    all_to_all x1 -> x0, blocking collectives: 31.5 us -> none  [shards(): part = total(lax.all_to_all(parts, ('x', 'z'), 0, 0, tiled=True))]
    all_to_all x0 -> x1, starting transfers between devices: none -> 12.6 us  [shards(): part = total(lax.all_to_all(parts, ('x', 'z'), 0, 0, tiled=True))]
    all_to_all x0 -> x1, waiting for transfers between devices: none -> 11.7 us  [shards(): part = total(lax.all_to_all(parts, ('x', 'z'), 0, 0, tiled=True))]
    all_to_all x1, waiting for transfers between devices: 4.74 us -> 12.5 us  [spread(): return lax.all_to_all(copies, axes, 0, 0, tiled=True)]
    dot_general x5 -> x0, matrix products: 6.45 us -> none  [the longest x2 2.54 us: dot(): return jnp.dot(left, right, preferred_element_type=jnp.float32)]
    all_to_all x1, blocking collectives: 14.6 us -> 20.1 us  [spread(): return lax.all_to_all(copies, axes, 0, 0, tiled=True)]
    pallas_call x2 -> x5, Pallas kernels: 10.8 us -> 15.1 us  [the longest x1 9.98 us: shards(): local(attention_kernel, 'attention', (((2, 2 * WIDTH, WIDTH), b16), ((2 *...]
    all_to_all x1, starting transfers between devices: 8.26 us -> 4.03 us  [spread(): return lax.all_to_all(copies, axes, 0, 0, tiled=True)]
  transfers between devices with their start and end apart: 7 -> 8, of which waited for: 2 -> 5; matrix products, arithmetic and copies ran while one was open for 10% -> 3% of each run, Pallas kernels for 0% -> 3%
where the time goes in v3:
time: 117 us; the launch traced here: 115 us
  starting transfers between devices  40.2 us (34%)
  waiting for transfers between devices  29.8 us (25%)
  blocking collectives  20.1 us (17%)
  Pallas kernels  15.1 us (13%)
  local copies, waits for them, and re-layouts  7.21 us (6%)
  other arithmetic  2.27 us (2%)
    all_to_all x1, blocking collectives, spread(): return lax.all_to_all(copies, axes, 0, 0, tiled=True)  20.1 us
    ppermute x4, starting transfers between devices, swapped(): return lax.ppermute(block, SPACE, pairs + [(b, a) for a, b in pairs])  12.6 us
    all_to_all x1, starting transfers between devices, shards(): part = total(lax.all_to_all(parts, ('x', 'z'), 0, 0, tiled=True))  12.6 us
    all_to_all x1, waiting for transfers between devices, spread(): return lax.all_to_all(copies, axes, 0, 0, tiled=True)  12.5 us
    all_to_all x1, waiting for transfers between devices, shards(): part = total(lax.all_to_all(parts, ('x', 'z'), 0, 0, tiled=True))  11.7 us
    pallas_call x1, Pallas kernels, shards(): local(attention_kernel, 'attention', (((2, 2 * WIDTH, WIDTH), b16), ((2 *...  9.98 us
    ppermute x1, starting transfers between devices, shards(): other = lax.ppermute(half, 'c', pair)  7.77 us
    unnamed x19, local copies, waits for them, and re-layouts  5.36 us
  transfers between devices with their start and end apart: 8, of which 5 were waited for; matrix products, arithmetic and copies ran while one was open for 3% of the time, Pallas kernels for 3%

profile of v3, /device:TPU:1, one launch (start us, length us, event | category | flops | bytes accessed | tf_op | source)
XLA Modules:
  0.0 115.5 jit_solution(9304277374687897936)
XLA Ops:
  0.6 0.7 collective-permute-start.1
  1.3 8.2 %collective-permute-start = (bf16[288,384]{1,0:T(8,128)(2,1)}, bf16[288,384]{1,0:T(8,128)(2,1)S(1)}, u32[]{:S(2)}, u32[]{:S(2)}) collective-permute-start(bf16[288,384]{1,0:T(8,128)(2,1)} %bitcast.25), channel_id=1, source_target_pairs={{0,1},{2,3},{4,5},{6,7},{8,9},{10,11},{12,13},{14,15},{16,17},{18,... | collective-permute-start | bytes 663560 | tf_op jit(solution)/shard_map/ppermute | solution.py:34
  9.5 0.7 broadcast_compare_fusion
  10.2 0.7 copy.16
  10.9 0.7 broadcast_in_dim.31.gain
  11.6 0.1 add_multiply_fusion
  11.7 0.1 iota_add_fusion
  11.7 0.1 add.51
  11.8 0.2 and_reduce_fusion
  12.0 0.1 copy.11
  12.2 0.1 fusion.fk
  12.2 0.0 copy-start
  12.2 1.2 %copy-done = bf16[384,1152]{1,0:T(8,128)(2,1)S(1)} copy-done((bf16[384,1152]{1,0:T(8,128)(2,1)S(1)}, bf16[384,1152]{1,0:T(8,128)(2,1)}, u32[]{:S(2)}) %copy-start) | copy-done | bytes 884760
  13.4 0.9 copy-done.2
  14.3 0.9 copy-done.4
  15.3 1.0 copy-done.6
  16.2 0.7 copy-done.8
  16.9 1.3 %prepare.1 = (bf16[288,384]{1,0:T(8,128)(2,1)S(1)}, bf16[288,768]{1,0:T(8,128)(2,1)S(1)}, bf16[288,384]{1,0:T(8,128)(2,1)S(1)}, bf16[384,288]{1,0:T(8,128)(2,1)S...) custom-call(s32[9]{0:T(128)S(1)} %bitcast.30, bf16[288,384]{1,0:T(8,128)(2,1)S(1)} %bitcast.26, ...), custom_call_target="tpu_custom_call" | custom-call | flops 400000000 | bytes 1000000 | tf_op jit(solution)/shard_map/prepare/pallas_call | solution.py:214
  18.2 0.2 fusion.1.fq
  18.4 0.0 collective-permute-done.1.far
  18.4 0.0 collective-permute-done.near
  18.4 0.0 copy-done.1
  18.4 10.0 %attention.1 = (bf16[2,768,384]{2,1,0:T(8,128)(2,1)S(1)}, bf16[768,896]{1,0:T(8,128)(2,1)S(1)}, bf16[288,384]{1,0:T(8,128)(2,1)S(1)}) custom-call(s32[1]{0:T(128)} %bitcast.core, bf16[288,384]{1,0:T(8,128)(2,1)S(1)} %collective-permute-done.near, bf16[288,384]{1,0:T(8,128)(2,1)S(1)} %collective-permute-done.1.far, ...), custom_call_target="tpu_custom_call" | custom-call | flops 3000000000 | bytes 4000000 | tf_op jit(solution)/shard_map/attention/pallas_call | solution.py:234
  28.4 0.1 slice_bitcast_fusion
  28.5 3.1 %collective-permute-start.2 = (bf16[768,384]{1,0:T(8,128)(2,1)S(1)}, bf16[768,384]{1,0:T(8,128)(2,1)S(1)}, u32[]{:S(2)}, u32[]{:S(2)}) collective-permute-start(bf16[768,384]{1,0:T(8,128)(2,1)S(1)} %slice_bitcast_fusion), channel_id=1, source_target_pairs={{0,64},{64,0},{1,65},{65,1},{2,66},{66,2},{3,67},{67,3},{4,68},{68... | collective-permute-start | bytes 1769480 | tf_op jit(solution)/shard_map/ppermute | solution.py:255
  31.6 1.0 back.1
  32.7 0.6 collective-permute-done.2
  33.2 0.9 bitcast_add_fusion
  34.1 12.6 %all-to-all-start = ((bf16[32,24,384]{2,1,0:T(8,128)(2,1)}), bf16[32,24,384]{2,1,0:T(8,128)(2,1)S(1)}, u32[]{:S(2)}, u32[]{:S(2)}) async-start(bf16[32,24,384]{2,1,0:T(8,128)(2,1)} %bitcast.11), calls=%async_computation | async-start | bytes 1179648 | tf_op jit(solution)/shard_map/all_to_all | solution.py:264
  46.7 3.1 %collective-permute-start.3 = (bf16[288,384]{1,0:T(8,128)(2,1)S(1)}, bf16[288,384]{1,0:T(8,128)(2,1)S(1)}, u32[]{:S(2)}, u32[]{:S(2)}) collective-permute-start(bf16[288,384]{1,0:T(8,128)(2,1)S(1)} %get-tuple-element.41), channel_id=1, source_target_pairs={{0,1},{2,3},{4,5},{6,7},{8,9},{10,11},{12,13},{14,15},{16,17},{18,... | collective-permute-start | bytes 663560 | tf_op jit(solution)/shard_map/ppermute | solution.py:34
  49.9 0.7 collective-permute-start.4
  50.5 11.7 %all-to-all-done = bf16[32,24,384]{2,1,0:T(8,128)(2,1)S(1)} async-done(((bf16[32,24,384]{2,1,0:T(8,128)(2,1)}), bf16[32,24,384]{2,1,0:T(8,128)(2,1)S(1)}, u32[]{:S(2)}, u32[]{:S(2)}) %all-to-all-start) | async-done | bytes 589856 | tf_op jit(solution)/shard_map/all_to_all | solution.py:264
  62.3 0.1 reduce_sum.38
  62.3 0.0 copy-start.3
  62.4 0.0 copy-start.5
  62.4 3.3 %collective-permute-done.3.near = bf16[288,384]{1,0:T(8,128)(2,1)S(1)} collective-permute-done((bf16[288,384]{1,0:T(8,128)(2,1)S(1)}, bf16[288,384]{1,0:T(8,128)(2,1)S(1)}, u32[]{:S(2)}, u32[]{:S(2)}) %collective-permute-start.3) | collective-permute-done | bytes 221216 | tf_op jit(solution)/shard_map/ppermute | solution.py:34
  65.7 0.0 collective-permute-done.4.far
  65.7 20.1 %all_to_all.15 = bf16[8,24,384]{2,1,0:T(8,128)(2,1)S(1)} all-to-all(bf16[8,24,384]{2,1,0:T(8,128)(2,1)S(1)} %broadcast_in_dim.35), channel_id=1, replica_groups=mesh['yl'=4,'c'=2,'yh'=2,'x'=4,'z'=8] {'yl','yh'}, dimensions={0} | all-to-all | bytes 294912 | tf_op jit(solution)/shard_map/all_to_all | solution.py:40
  85.8 0.9 broadcast_in_dim.36
  86.7 4.0 %all-to-all-start.2 = ((bf16[32,24,384]{2,1,0:T(8,128)(2,1)}), bf16[32,24,384]{2,1,0:T(8,128)(2,1)S(1)}, u32[]{:S(2)}, u32[]{:S(2)}) async-start(bf16[32,24,384]{2,1,0:T(8,128)(2,1)} %broadcast_in_dim.36), calls=%async_computation.2 | async-start | bytes 1179648 | tf_op jit(solution)/shard_map/all_to_all | solution.py:40
  90.7 0.0 copy-done.3
  90.7 0.0 copy-done.5
  90.7 1.0 grad_input.1
  91.7 12.5 %all-to-all-done.2 = bf16[32,24,384]{2,1,0:T(8,128)(2,1)S(1)} async-done(((bf16[32,24,384]{2,1,0:T(8,128)(2,1)}), bf16[32,24,384]{2,1,0:T(8,128)(2,1)S(1)}, u32[]{:S(2)}, u32[]{:S(2)}) %all-to-all-start.2) | async-done | bytes 589856 | tf_op jit(solution)/shard_map/all_to_all | solution.py:40
  104.3 7.8 %collective-permute-start.5 = (bf16[768,384]{1,0:T(8,128)(2,1)S(1)}, bf16[768,384]{1,0:T(8,128)(2,1)S(1)}, u32[]{:S(2)}, u32[]{:S(2)}) collective-permute-start(bf16[768,384]{1,0:T(8,128)(2,1)S(1)} %bitcast.22), channel_id=1, source_target_pairs={{0,64},{64,0},{1,65},{65,1},{2,66},{66,2},{3,67},{67,3},{4,68},{68... | collective-permute-start | bytes 1769480 | tf_op jit(solution)/shard_map/ppermute | solution.py:272
  112.0 1.6 %collective-permute-done.5.other = bf16[768,384]{1,0:T(8,128)(2,1)S(1)} collective-permute-done((bf16[768,384]{1,0:T(8,128)(2,1)S(1)}, bf16[768,384]{1,0:T(8,128)(2,1)S(1)}, u32[]{:S(2)}, u32[]{:S(2)}) %collective-permute-start.5) | collective-permute-done | bytes 589856 | tf_op jit(solution)/shard_map/ppermute | solution.py:272
  113.7 0.0 copy-done.7
  113.7 1.8 %outputs.1 = (f32[384,1152]{1,0:T(8,128)}, f32[384,384]{1,0:T(8,128)}, f32[384]{0:T(512)}) custom-call(s32[1]{0:T(128)} %bitcast.core, bf16[768,384]{1,0:T(8,128)(2,1)S(1)} %bitcast.23, bf16[768,384]{1,0:T(8,128)(2,1)S(1)} %collective-permute-done.5.other, bf16[384,1152]{1,0:T(8,128)(2,1)S(1)} %copy-done.1, f32[384]{0:T(512)S(1)} %copy-done.7), custom_call_target="tpu_custom_call" | custom-call | flops 100000000 | bytes 4000000 | tf_op jit(solution)/shard_map/outputs/pallas_call | solution.py:274
  (12 shorter events, 0.1 us)
Async XLA Ops:
  0.6 17.7 %collective-permute-start.1 = (bf16[288,384]{1,0:T(8,128)(2,1)}, bf16[288,384]{1,0:T(8,128)(2,1)S(1)}, u32[]{:S(2)}, u32[]{:S(2)}) collective-permute-start(bf16[288,384]{1,0:T(8,128)(2,1)} %bitcast.24), channel_id=1, source_target_pairs={{1,2},{3,4},{5,6},{7,8},{9,10},{11,12},{13,14},{15,16},{17,18},{19... | collective-permute-start | bytes 663560 | tf_op jit(solution)/shard_map/ppermute | solution.py:34
  1.3 17.1 %collective-permute-start = (bf16[288,384]{1,0:T(8,128)(2,1)}, bf16[288,384]{1,0:T(8,128)(2,1)S(1)}, u32[]{:S(2)}, u32[]{:S(2)}) collective-permute-start(bf16[288,384]{1,0:T(8,128)(2,1)} %bitcast.25), channel_id=1, source_target_pairs={{0,1},{2,3},{4,5},{6,7},{8,9},{10,11},{12,13},{14,15},{16,17},{18,... | collective-permute-start | bytes 663560 | tf_op jit(solution)/shard_map/ppermute | solution.py:34
  12.2 1.2 %copy-start = (bf16[384,1152]{1,0:T(8,128)(2,1)S(1)}, bf16[384,1152]{1,0:T(8,128)(2,1)}, u32[]{:S(2)}) copy-start(bf16[384,1152]{1,0:T(8,128)(2,1)} %wqkv.7) | copy-start | bytes 2654212
  13.4 0.9 copy-start.2
  14.3 0.9 copy-start.4
  15.3 1.0 copy-start.6
  16.2 0.7 copy-start.8
  16.9 1.5 %copy-start.1 = (bf16[384,1152]{1,0:T(8,128)(2,1)S(1)}, bf16[384,1152]{1,0:T(8,128)(2,1)}, u32[]{:S(2)}) copy-start(bf16[384,1152]{1,0:T(8,128)(2,1)} %wqkv.7) | copy-start | bytes 2654212
  28.5 4.8 %collective-permute-start.2 = (bf16[768,384]{1,0:T(8,128)(2,1)S(1)}, bf16[768,384]{1,0:T(8,128)(2,1)S(1)}, u32[]{:S(2)}, u32[]{:S(2)}) collective-permute-start(bf16[768,384]{1,0:T(8,128)(2,1)S(1)} %slice_bitcast_fusion), channel_id=1, source_target_pairs={{0,64},{64,0},{1,65},{65,1},{2,66},{66,2},{3,67},{67,3},{4,68},{68... | collective-permute-start | bytes 1769480 | tf_op jit(solution)/shard_map/ppermute | solution.py:255
  34.1 28.2 %all-to-all-start = ((bf16[32,24,384]{2,1,0:T(8,128)(2,1)}), bf16[32,24,384]{2,1,0:T(8,128)(2,1)S(1)}, u32[]{:S(2)}, u32[]{:S(2)}) async-start(bf16[32,24,384]{2,1,0:T(8,128)(2,1)} %bitcast.11), calls=%async_computation | async-start | bytes 1179648 | tf_op jit(solution)/shard_map/all_to_all | solution.py:264
  46.7 19.0 %collective-permute-start.3 = (bf16[288,384]{1,0:T(8,128)(2,1)S(1)}, bf16[288,384]{1,0:T(8,128)(2,1)S(1)}, u32[]{:S(2)}, u32[]{:S(2)}) collective-permute-start(bf16[288,384]{1,0:T(8,128)(2,1)S(1)} %get-tuple-element.41), channel_id=1, source_target_pairs={{0,1},{2,3},{4,5},{6,7},{8,9},{10,11},{12,13},{14,15},{16,17},{18,... | collective-permute-start | bytes 663560 | tf_op jit(solution)/shard_map/ppermute | solution.py:34
  49.9 15.8 %collective-permute-start.4 = (bf16[288,384]{1,0:T(8,128)(2,1)S(1)}, bf16[288,384]{1,0:T(8,128)(2,1)S(1)}, u32[]{:S(2)}, u32[]{:S(2)}) collective-permute-start(bf16[288,384]{1,0:T(8,128)(2,1)S(1)} %get-tuple-element.42), channel_id=1, source_target_pairs={{1,2},{3,4},{5,6},{7,8},{9,10},{11,12},{13,14},{15,16},{17,18},{19... | collective-permute-start | bytes 663560 | tf_op jit(solution)/shard_map/ppermute | solution.py:34
  62.3 28.4 %copy-start.3 = (bf16[1,288,384]{2,1,0:T(8,128)(2,1)S(1)}, bf16[1,288,384]{2,1,0:T(8,128)(2,1)}, u32[]{:S(2)}) copy-start(bf16[1,288,384]{2,1,0:T(8,128)(2,1)} %param.7) | copy-start | bytes 663556
  62.4 28.4 %copy-start.5 = (bf16[1,288,384]{2,1,0:T(8,128)(2,1)S(1)}, bf16[1,288,384]{2,1,0:T(8,128)(2,1)}, u32[]{:S(2)}) copy-start(bf16[1,288,384]{2,1,0:T(8,128)(2,1)} %param.8) | copy-start | bytes 663556
  86.7 27.0 %copy-start.7 = (f32[384]{0:T(512)S(1)}, f32[384]{0:T(512)}, u32[]{:S(2)}) copy-start(f32[384]{0:T(512)} %gain.1) | copy-start | bytes 4612
  86.7 17.6 %all-to-all-start.2 = ((bf16[32,24,384]{2,1,0:T(8,128)(2,1)}), bf16[32,24,384]{2,1,0:T(8,128)(2,1)S(1)}, u32[]{:S(2)}, u32[]{:S(2)}) async-start(bf16[32,24,384]{2,1,0:T(8,128)(2,1)} %broadcast_in_dim.36), calls=%async_computation.2 | async-start | bytes 1179648 | tf_op jit(solution)/shard_map/all_to_all | solution.py:40
  104.3 9.4 %collective-permute-start.5 = (bf16[768,384]{1,0:T(8,128)(2,1)S(1)}, bf16[768,384]{1,0:T(8,128)(2,1)S(1)}, u32[]{:S(2)}, u32[]{:S(2)}) collective-permute-start(bf16[768,384]{1,0:T(8,128)(2,1)S(1)} %bitcast.22), channel_id=1, source_target_pairs={{0,64},{64,0},{1,65},{65,1},{2,66},{66,2},{3,67},{67,3},{4,68},{68... | collective-permute-start | bytes 1769480 | tf_op jit(solution)/shard_map/ppermute | solution.py:272

commit v4 on v3

v4 whole, which is shorter than its diff:
```python
import math

import jax
import jax.numpy as jnp
from jax import lax
from jax.experimental import pallas as pl
from jax.experimental.pallas import tpu as pltpu
from jax.sharding import Mesh
from jax.sharding import PartitionSpec as P

HEADS = 6
SIDE = 9
ROWS = 288
WIDTH = 384
HEAD = 64
KEYS = 896
SPACE = ("yh", "x", "z")
HIDDEN = -1e30


def inner(left, right):
    return lax.dot_general(
        left, right, (((1,), (1,)), ((), ())), preferred_element_type=jnp.float32
    )


def dot(left, right):
    return jnp.dot(left, right, preferred_element_type=jnp.float32)


def swapped(block, first):
    count = lax.axis_size(SPACE)
    pairs = [(i, i + 1) for i in range(first, count - 1, 2)]
    return lax.ppermute(block, SPACE, pairs + [(b, a) for a, b in pairs])


def spread(part, axes):
    count = lax.axis_size(axes)
    copies = jnp.broadcast_to(part[None], (count,) + part.shape)
    return lax.all_to_all(copies, axes, 0, 0, tiled=True)


def total(parts):
    return jnp.sum(parts.astype(jnp.float32), axis=0).astype(jnp.bfloat16)


def unit_rows(values, gain):
    power = jnp.mean(values * values, axis=1, keepdims=True)
    return values * lax.rsqrt(power + 1e-06) * gain


def fetch(pairs, sems):
    copies = [
        pltpu.make_async_copy(source, target, sems.at[i]) for i, (source, target) in enumerate(pairs)
    ]
    for copy in copies:
        copy.start()
    return copies


def prepare_kernel(
    alive, tokens_in, cot_in, gain, wqkv_in, wout_in, own, kv, q8, q8t, g, scaled,
    tokens, cot, wqkv, wout, sems,
):
    copies = fetch([(tokens_in, tokens), (wqkv_in, wqkv), (cot_in, cot), (wout_in, wout)], sems)
    copies[0].wait()
    own[...] = unit_rows(tokens[...].astype(jnp.float32), gain[...]).astype(jnp.bfloat16)
    copies[1].wait()
    queries = dot(own[...], wqkv[:, 0:WIDTH]).astype(jnp.bfloat16).astype(jnp.float32)
    eighth = (queries * (1.0 / math.sqrt(HEAD))).astype(jnp.bfloat16)
    q8[...] = eighth
    q8t[...] = eighth.T
    kv[...] = dot(own[...], wqkv[:, WIDTH:]).astype(jnp.bfloat16)
    copies[2].wait()
    block = ROWS // SIDE
    for at in range(SIDE):
        rows = slice(at * block, at * block + block)
        part = cot[rows].astype(jnp.float32) * alive[at].astype(jnp.float32)
        scaled[rows] = part.astype(jnp.bfloat16)
    copies[3].wait()
    g[...] = inner(scaled[...], wout[...]).astype(jnp.bfloat16)


def attention_kernel(
    core, near, far, own, kv, q8, q8t, g, scaled, fq, fk, gain, wqkv,
    send, dt, dq, normed_t, attn_t, normed, table, scores, expo, dshare, dscores,
):
    normed[0:ROWS] = own[...]
    normed[3 * ROWS : KEYS] = jnp.zeros((KEYS - 3 * ROWS, WIDTH), jnp.bfloat16)
    table[0:ROWS] = kv[...]
    table[3 * ROWS : KEYS] = jnp.zeros((KEYS - 3 * ROWS, 2 * WIDTH), jnp.bfloat16)
    for side, halo in enumerate((near, far)):
        rows = slice((side + 1) * ROWS, (side + 2) * ROWS)
        unit = unit_rows(halo[...].astype(jnp.float32), gain[...]).astype(jnp.bfloat16)
        normed[rows] = unit
        table[rows] = dot(unit, wqkv[:, WIDTH:]).astype(jnp.bfloat16)
    normed_t[...] = normed[...].T
    both = lax.broadcasted_iota(jnp.int32, (2 * ROWS, 128), 0) < ROWS
    low = lax.broadcasted_iota(jnp.int32, (2 * ROWS, 128), 1) < HEAD
    keep = both == low
    zero = jnp.zeros((2 * ROWS, 128), jnp.float32)
    chunks = [slice(at, at + 32) for at in range(0, 2 * ROWS, 32)]
    pairs = range(HEADS // 2)
    lanes = [slice(pair * 128, pair * 128 + 128) for pair in pairs]
    values = [slice(WIDTH + at.start, WIDTH + at.stop) for at in lanes]
    shares, results, grads, deltas = [], [], [], []

    def twice(block):
        return jnp.concatenate([block, block], axis=0).astype(jnp.float32)

    def joined(block):
        return jnp.where(low[:ROWS], block[:ROWS], block[ROWS:]).astype(jnp.bfloat16)

    for pair in pairs:
        queries = jnp.where(keep, twice(q8[:, lanes[pair]]), zero).astype(jnp.bfloat16)
        queries = jnp.concatenate([queries, jnp.concatenate([fq[...], fq[...]], axis=0)], axis=1)
        scores[pair] = inner(queries, jnp.concatenate([table[:, lanes[pair]], fk[...]], axis=1))
    for pair in pairs:
        share = []
        for rows in chunks:
            block = scores[pair, rows]
            block = jnp.exp(block - jnp.max(block, axis=1, keepdims=True))
            share.append(1.0 / jnp.sum(block, axis=1, keepdims=True))
            expo[pair, rows] = block.astype(jnp.bfloat16)
        shares.append(jnp.concatenate(share, axis=0))
    for pair in pairs:
        results.append(dot(expo[pair], table[:, values[pair]]) * shares[pair])
        grad = jnp.where(keep, twice(g[:, lanes[pair]]) * shares[pair], zero)
        grads.append(grad.astype(jnp.bfloat16))
        dshare[pair] = inner(grads[pair], table[:, values[pair]])
        delta = grads[pair].astype(jnp.float32) * results[pair]
        deltas.append(jnp.sum(delta, axis=1, keepdims=True))
    for pair in pairs:
        for rows in chunks:
                block = (dshare[pair, rows] - deltas[pair][rows]).astype(jnp.bfloat16)
                dscores[pair, rows] = expo[pair, rows] * block
    for pair in pairs:
        moved = dot(dscores[pair], table[:, lanes[pair]]) * (1.0 / math.sqrt(HEAD))
        dq[:, lanes[pair]] = joined(moved)
        attn_t[lanes[pair]] = joined(results[pair]).T
        turned = (grads[pair][:ROWS] + grads[pair][ROWS:]).T
        for half in range(2):
            rows = slice(half * ROWS, half * ROWS + ROWS)
            at = (2 * pair + half) * HEAD
            part = q8t[at : at + HEAD]
            dt[at : at + HEAD] = dot(part, dscores[pair, rows]).astype(jnp.bfloat16)
            part = turned[half * HEAD : half * HEAD + HEAD]
            at += WIDTH
            dt[at : at + HEAD] = dot(part, expo[pair, rows]).astype(jnp.bfloat16)

    @pl.when(core[0] == 0)
    def _():
        value_half(send, normed_t, dt, attn_t, scaled)

    @pl.when(core[0] == 1)
    def _():
        key_half(send, normed_t, dt, dq)


def key_half(out, normed_t, dt, dq):
    out[0:WIDTH] = dot(normed_t[:, 0:ROWS], dq[...]).astype(jnp.bfloat16)
    out[WIDTH:] = inner(normed_t[...], dt[0:WIDTH]).astype(jnp.bfloat16)


def value_half(out, normed_t, dt, attn_t, scaled):
    out[0:WIDTH] = inner(normed_t[...], dt[WIDTH:]).astype(jnp.bfloat16)
    out[WIDTH:] = dot(attn_t[...], scaled[...]).astype(jnp.bfloat16)


def back_kernel(core, dt, dq, normed_t, attn_t, scaled, wqkv, held, base, near, far):
    back = lax.dot_general(
        dt[...], wqkv[:, WIDTH:], (((0,), (1,)), ((), ())), preferred_element_type=jnp.float32
    )
    near[...] = back[ROWS : 2 * ROWS].astype(jnp.bfloat16)
    far[...] = back[2 * ROWS : 3 * ROWS].astype(jnp.bfloat16)
    base[...] = back[0:ROWS] + inner(dq[...], wqkv[:, 0:WIDTH])

    @pl.when(core[0] == 0)
    def _():
        key_half(held, normed_t, dt, dq)

    @pl.when(core[0] == 1)
    def _():
        value_half(held, normed_t, dt, attn_t, scaled)


def gather_kernel(parts, copies):
    part = jnp.sum(parts[...].astype(jnp.float32), axis=0).astype(jnp.bfloat16)
    copies[...] = jnp.broadcast_to(part[None], copies.shape)


def input_kernel(base, near, far, tokens, cot, gain, grad_input):
    d_normed = base[...] + near[...].astype(jnp.float32) + far[...].astype(jnp.float32)
    inward = d_normed.astype(jnp.bfloat16).astype(jnp.float32) * gain[...]
    values = tokens[...].astype(jnp.float32)
    root = lax.rsqrt(jnp.mean(values * values, axis=1, keepdims=True) + 1e-06)
    slope = jnp.mean(inward * values, axis=1, keepdims=True) * root * root
    moved = cot[...].astype(jnp.float32) + root * (inward - values * slope)
    grad_input[...] = moved.astype(jnp.bfloat16)


def output_kernel(core, mine, other, wqkv, gain, grad_qkv, grad_out, grad_gain):
    scale = 1.0 / math.sqrt(512 * ROWS)
    me = core[0]

    def halves(first, second):
        query = first[0:WIDTH].astype(jnp.float32) * scale
        key = first[WIDTH:].astype(jnp.float32) * scale
        value = second[0:WIDTH].astype(jnp.float32) * scale
        grad_qkv[:, 0:WIDTH] = query
        grad_qkv[:, WIDTH : 2 * WIDTH] = key
        grad_qkv[:, 2 * WIDTH :] = value
        grad_out[...] = second[WIDTH:].astype(jnp.float32) * scale
        moved = query * wqkv[:, 0:WIDTH].astype(jnp.float32)
        moved += key * wqkv[:, WIDTH : 2 * WIDTH].astype(jnp.float32)
        moved += value * wqkv[:, 2 * WIDTH :].astype(jnp.float32)
        grad_gain[...] = jnp.sum(moved.T, axis=0) / gain[...]

    @pl.when(me == 0)
    def _():
        halves(mine, other)

    @pl.when(me == 1)
    def _():
        halves(other, mine)


def local(body, name, shapes, in_specs, vmem, scratch=(), flops=10**8, moved=10**6):
    return pl.pallas_call(
        body,
        out_shape=tuple(jax.ShapeDtypeStruct(shape, kind) for shape, kind in shapes),
        in_specs=in_specs,
        out_specs=(pl.BlockSpec(memory_space=pltpu.VMEM),) * len(shapes),
        scratch_shapes=scratch,
        compiler_params=pltpu.CompilerParams(vmem_limit_bytes=vmem * 2**20),
        cost_estimate=pl.CostEstimate(flops=flops, bytes_accessed=moved, transcendentals=0),
        name=name,
    )


def shards(tokens, cotangent, neighbours, active, gain, w_qkv, w_out):
    values = tokens[0]
    cot = cotangent[0]
    lists = neighbours[0]
    block = ROWS // SIDE
    position = lax.axis_index(SPACE)
    core = jnp.reshape(lax.axis_index("c"), (1,)).astype(jnp.int32)
    near = swapped(values, 0)
    far = swapped(values, 1)
    gains = gain[None]

    b16, f32 = jnp.bfloat16, jnp.float32
    whole = pl.BlockSpec(memory_space=pltpu.VMEM)
    scalar = pl.BlockSpec(memory_space=pltpu.SMEM)
    outside = pl.BlockSpec(memory_space=pltpu.HBM)
    rows = ((ROWS, WIDTH), b16)
    half_rows = ((2 * WIDTH, WIDTH), b16)
    dma = pltpu.SemaphoreType.DMA
    own, kv, q8, q8t, g, scaled = local(
        prepare_kernel,
        "prepare",
        (rows, ((ROWS, 2 * WIDTH), b16), rows, ((WIDTH, ROWS), b16), rows, rows),
        [scalar, outside, outside, whole, outside, outside],
        8,
        (
            pltpu.VMEM((ROWS, WIDTH), b16),
            pltpu.VMEM((ROWS, WIDTH), b16),
            pltpu.VMEM((WIDTH, 3 * WIDTH), b16),
            pltpu.VMEM((WIDTH, WIDTH), b16),
            dma((4,)),
        ),
        flops=4 * 10**8,
    )(active[0], values, cot, gains, w_qkv, w_out)

    parity = position % 2
    slabs = jnp.stack([position, position + 1 - 2 * parity, position - 1 + 2 * parity])
    ids = (slabs[:, None] * SIDE + jnp.arange(SIDE)[None, :]).reshape(-1)
    seen = jnp.any((lists[:, :, None] == ids) & (lists[:, :, None] >= 0), axis=1)
    hidden = jnp.where(seen, 0.0, HIDDEN).T.astype(b16)
    fk = jnp.repeat(hidden, block, axis=0)
    fk = jnp.pad(fk, ((0, KEYS - 3 * ROWS), (0, 0)), constant_values=HIDDEN)
    fk = jnp.pad(fk, ((0, 0), (0, 128 - SIDE)))
    row_block = lax.broadcasted_iota(jnp.int32, (ROWS, 128), 0) // block
    fq = (row_block == lax.broadcasted_iota(jnp.int32, (ROWS, 128), 1)).astype(b16)

    pair_rows = (HEADS // 2, 2 * ROWS, KEYS)
    send, d_table, d_queries, normed_t, attn_t = local(
        attention_kernel,
        "attention",
        (half_rows, ((2 * WIDTH, KEYS), b16), rows, ((WIDTH, KEYS), b16), ((WIDTH, ROWS), b16)),
        [scalar] + [whole] * 12,
        32,
        (
            pltpu.VMEM((KEYS, WIDTH), b16),
            pltpu.VMEM((KEYS, 2 * WIDTH), b16),
            pltpu.VMEM(pair_rows, f32),
            pltpu.VMEM(pair_rows, b16),
            pltpu.VMEM(pair_rows, f32),
            pltpu.VMEM(pair_rows, b16),
        ),
        flops=3 * 10**9,
        moved=4 * 10**6,
    )(core, near, far, own, kv, q8, q8t, g, scaled, fq, fk, gains, w_qkv)

    pair = [(0, 1), (1, 0)]
    arrived = lax.ppermute(send, "c", pair)
    held, base, back_near, back_far = local(
        back_kernel,
        "back",
        (half_rows, ((ROWS, WIDTH), f32), rows, rows),
        [scalar] + [whole] * 6,
        8,
        flops=10**9,
    )(core, d_table, d_queries, normed_t, attn_t, scaled, w_qkv)
    half = (held.astype(f32) + arrived.astype(f32)).astype(b16)
    half, base, back_near, back_far = lax.optimization_barrier((half, base, back_near, back_far))
    back_near = swapped(back_near, 0)
    count = lax.axis_size(SPACE)
    middle = count // 2
    ends = [(middle - 1, count - 1), (0, middle)]
    crossed = lax.ppermute(back_far, SPACE, ends + [(b, a) for a, b in ends])
    plane = lax.axis_size(("x", "z"))
    parts = half.reshape(plane, 2 * WIDTH // plane, WIDTH)
    part = total(lax.all_to_all(parts, ("x", "z"), 0, 0, tiled=True))
    part, crossed = lax.optimization_barrier((part, crossed))
    at_end = jnp.logical_or(position == 0, position == count - 1)
    back_far = jnp.where(at_end, crossed, back_far)
    pairs = [(i, i + 1) for i in range(1, count - 1, 2) if i != middle - 1]
    pairs = pairs + [(b, a) for a, b in pairs] + [(count - 1, middle), (0, middle - 1)]
    back_far = lax.ppermute(back_far, SPACE, pairs)
    parts = spread(part, ("yl", "yh"))
    (copies,) = local(gather_kernel, "gather", (((plane,) + part.shape, b16),), [whole], 4)(parts)
    half = lax.all_to_all(copies, ("x", "z"), 0, 0, tiled=True).reshape(2 * WIDTH, WIDTH)
    (grad_input,) = local(input_kernel, "grad_input", (rows,), [whole] * 6, 8, flops=10**10)(
        base, back_near, back_far, values, cot, gains
    )
    half, grad_input = lax.optimization_barrier((half, grad_input))
    other = lax.ppermute(half, "c", pair)

    grad_wqkv, grad_wout, grad_gain = local(
        output_kernel,
        "outputs",
        (((WIDTH, 3 * WIDTH), f32), ((WIDTH, WIDTH), f32), ((WIDTH,), f32)),
        [scalar] + [whole] * 4,
        8,
        moved=4 * 10**6,
    )(core, half, other, w_qkv, gain)
    return (grad_input[None], grad_wqkv, grad_wout, grad_gain)


def solution(mesh):
    fine = Mesh(mesh.devices.reshape(4, 2, 2, 4, 8), ("yl", "c", "yh", "x", "z"))
    region = ("yl", "c")
    split = P(region, SPACE, None)
    return jax.shard_map(
        shards,
        mesh=fine,
        in_specs=(split, split, split, P(region, SPACE), P(), P(), P()),
        out_specs=(split, P(), P(), P()),
        check_vma=False,
    )
```

time: 117 us -> 110 us (0.940)
  starting transfers between devices: 40.2 us -> 61.1 us
  blocking collectives: 20.1 us -> 0 us
  waiting for transfers between devices: 29.8 us -> 22.5 us
    all_to_all x1 -> x0, blocking collectives: 20.1 us -> none  [spread(): return lax.all_to_all(copies, axes, 0, 0, tiled=True)]
    all_to_all x1, waiting for transfers between devices: 12.5 us -> 0.01 us  [spread(): return lax.all_to_all(copies, axes, 0, 0, tiled=True)]
    all_to_all x0 -> x1, waiting for transfers between devices: none -> 12.2 us  [shards(): lax.all_to_all(copies, ('x', 'z'), 0, 0, tiled=True)]
    ppermute x1 -> x3, starting transfers between devices: 3.14 us -> 13.3 us  [the longest x1 7.15 us: shards(): crossed = lax.ppermute(back_far, SPACE, ends + [(b, a) for a, b in ends])]
    all_to_all x0 -> x1, starting transfers between devices: none -> 5.9 us  [shards(): lax.all_to_all(copies, ('x', 'z'), 0, 0, tiled=True)]
    all_to_all x1, starting transfers between devices: 4.03 us -> 8 us  [spread(): return lax.all_to_all(copies, axes, 0, 0, tiled=True)]
    ppermute x4 -> x3, waiting for transfers between devices: 3.33 us -> 0.01 us  [swapped(): return lax.ppermute(block, SPACE, pairs + [(b, a) for a, b in pairs])]
    all_to_all x1, waiting for transfers between devices: 11.7 us -> 8.7 us  [shards(): part = total(lax.all_to_all(parts, ('x', 'z'), 0, 0, tiled=True))]
  transfers between devices with their start and end apart: 8 -> 10, of which waited for: 5 -> 3; matrix products, arithmetic and copies ran while one was open for 3% -> 3% of each run, Pallas kernels for 3% -> 6%
where the time goes in v4:
time: 110 us; the launch traced here: 109 us
  starting transfers between devices  61.1 us (56%)
  waiting for transfers between devices  22.5 us (20%)
  Pallas kernels  14.9 us (14%)
  local copies, waits for them, and re-layouts  6.94 us (6%)
  other arithmetic  2.36 us (2%)
    ppermute x3, starting transfers between devices, swapped(): return lax.ppermute(block, SPACE, pairs + [(b, a) for a, b in pairs])  14.5 us
    all_to_all x1, waiting for transfers between devices, shards(): lax.all_to_all(copies, ('x', 'z'), 0, 0, tiled=True)  12.2 us
    all_to_all x1, starting transfers between devices, shards(): part = total(lax.all_to_all(parts, ('x', 'z'), 0, 0, tiled=True))  11.4 us
    all_to_all x1, waiting for transfers between devices, shards(): part = total(lax.all_to_all(parts, ('x', 'z'), 0, 0, tiled=True))  8.7 us
    ppermute x1, starting transfers between devices, shards(): other = lax.ppermute(half, 'c', pair)  8.04 us
    all_to_all x1, starting transfers between devices, spread(): return lax.all_to_all(copies, axes, 0, 0, tiled=True)  8 us
    ppermute x1, starting transfers between devices, shards(): crossed = lax.ppermute(back_far, SPACE, ends + [(b, a) for a, b in ends])  7.15 us
    pallas_call x1, Pallas kernels, shards(): local(attention_kernel, 'attention', (half_rows, ((2 * WIDTH, KEYS), b16)...  6.96 us
  transfers between devices with their start and end apart: 10, of which 3 were waited for; matrix products, arithmetic and copies ran while one was open for 3% of the time, Pallas kernels for 6%

profile of v4, /device:TPU:1, one launch (start us, length us, event | category | flops | bytes accessed | tf_op | source)
XLA Modules:
  0.0 108.8 jit_solution(17545646225635760397)
XLA Ops:
  0.6 0.7 collective-permute-start.1
  1.3 8.2 %collective-permute-start = (bf16[288,384]{1,0:T(8,128)(2,1)}, bf16[288,384]{1,0:T(8,128)(2,1)S(1)}, u32[]{:S(2)}, u32[]{:S(2)}) collective-permute-start(bf16[288,384]{1,0:T(8,128)(2,1)} %bitcast.21), channel_id=1, source_target_pairs={{0,1},{2,3},{4,5},{6,7},{8,9},{10,11},{12,13},{14,15},{16,17},{18,... | collective-permute-start | bytes 663560 | tf_op jit(solution)/shard_map/ppermute | solution.py:34
  9.5 0.7 broadcast_compare_fusion
  10.2 0.7 copy.16
  10.9 0.7 broadcast_in_dim.25.gain
  11.6 0.1 add_multiply_fusion
  11.7 0.1 iota_add_fusion
  11.7 0.1 add.54
  11.8 0.2 and_reduce_fusion
  12.0 0.1 copy.11
  12.2 0.1 fusion.fk
  12.2 0.0 copy-start
  12.2 1.2 %copy-done = bf16[384,1152]{1,0:T(8,128)(2,1)S(1)} copy-done((bf16[384,1152]{1,0:T(8,128)(2,1)S(1)}, bf16[384,1152]{1,0:T(8,128)(2,1)}, u32[]{:S(2)}) %copy-start) | copy-done | bytes 884760
  13.4 1.0 copy-done.2
  14.4 0.9 copy-done.3
  15.3 0.9 copy-done.5
  16.2 0.7 copy-done.8
  16.9 2.5 %prepare.1 = (bf16[288,384]{1,0:T(8,128)(2,1)S(1)}, bf16[288,768]{1,0:T(8,128)(2,1)S(1)}, bf16[288,384]{1,0:T(8,128)(2,1)S(1)}, bf16[384,288]{1,0:T(8,128)(2,1)S...) custom-call(s32[9]{0:T(128)S(1)} %bitcast.26, bf16[288,384]{1,0:T(8,128)(2,1)S(1)} %bitcast.22, ...), custom_call_target="tpu_custom_call" | custom-call | flops 400000000 | bytes 1000000 | tf_op jit(solution)/shard_map/prepare/pallas_call | solution.py:259
  19.4 0.2 fusion.1.fq
  19.6 0.0 collective-permute-done.1.far
  19.6 0.0 collective-permute-done.near
  19.6 7.0 %attention.1 = (bf16[768,384]{1,0:T(8,128)(2,1)S(1)}, bf16[768,896]{1,0:T(8,128)(2,1)S(1)}, bf16[288,384]{1,0:T(8,128)(2,1)S(1)}, bf16[384,896]{1,0:T(8,128)(2,1)S(1)}, bf16[384,288]{1,0:T(8,128)(2,1)S(1)}) custom-call(s32[1]{0:T(128)} %bitcast.core, bf16[288,384]{1,0:T(8,128)(2,1)S(1)} %collective-permute-done.near, ...), custom_call_target="tpu_custom_call" | custom-call | flops 3000000000 | bytes 4000000 | tf_op jit(solution)/shard_map/attention/pallas_call | solution.py:287
  26.6 3.1 %collective-permute-start.2 = (bf16[768,384]{1,0:T(8,128)(2,1)S(1)}, bf16[768,384]{1,0:T(8,128)(2,1)S(1)}, u32[]{:S(2)}, u32[]{:S(2)}) collective-permute-start(bf16[768,384]{1,0:T(8,128)(2,1)S(1)} %get-tuple-element.41), channel_id=1, source_target_pairs={{0,64},{64,0},{1,65},{65,1},{2,66},{66,2},{3,67},{67,3},{4,68},{68... | collective-permute-start | bytes 1769480 | tf_op jit(solution)/shard_map/ppermute | solution.py:306
  29.8 1.8 %back.1 = (bf16[768,384]{1,0:T(8,128)(2,1)S(1)}, f32[288,384]{1,0:T(8,128)S(1)}, bf16[288,384]{1,0:T(8,128)(2,1)S(1)}, bf16[288,384]{1,0:T(8,128)(2,1)S(1)}) custom-call(s32[1]{0:T(128)} %bitcast.core, bf16[768,896]{1,0:T(8,128)(2,1)S(1)} %get-tuple-element.36.dt, bf16[288,384]{1,0:T(8,128)(2,1)S(1)} %get-tuple-element.37.dq, ...), custom_call_target="tpu_custom_call" | custom-call | flops 1000000000 | bytes 1000000 | tf_op jit(solution)/shard_map/back/pallas_call | solution.py:307
  31.6 0.0 collective-permute-done.2
  31.6 1.0 add_convert_fusion
  32.5 11.4 %all-to-all-start = ((bf16[32,24,384]{2,1,0:T(8,128)(2,1)}), bf16[32,24,384]{2,1,0:T(8,128)(2,1)S(1)}, u32[]{:S(2)}, u32[]{:S(2)}) async-start(bf16[32,24,384]{2,1,0:T(8,128)(2,1)} %bitcast.9), calls=%async_computation | async-start | bytes 1179648 | tf_op jit(solution)/shard_map/all_to_all | solution.py:324
  43.9 7.1 %collective-permute-start.3 = (bf16[288,384]{1,0:T(8,128)(2,1)S(1)}, bf16[288,384]{1,0:T(8,128)(2,1)S(1)}, u32[]{:S(2)}, u32[]{:S(2)}) collective-permute-start(bf16[288,384]{1,0:T(8,128)(2,1)S(1)} %get-tuple-element.46), channel_id=1, source_target_pairs={{31,63},{0,32},{63,31},{32,0},{95,127},{64,96},{127,95},{96,64},{1... | collective-permute-start | bytes 663560 | tf_op jit(solution)/shard_map/ppermute | solution.py:321
  51.1 8.7 %all-to-all-done = bf16[32,24,384]{2,1,0:T(8,128)(2,1)S(1)} async-done(((bf16[32,24,384]{2,1,0:T(8,128)(2,1)}), bf16[32,24,384]{2,1,0:T(8,128)(2,1)S(1)}, u32[]{:S(2)}, u32[]{:S(2)}) %all-to-all-start) | async-done | bytes 589856 | tf_op jit(solution)/shard_map/all_to_all | solution.py:324
  59.8 0.1 reduce_sum.12
  59.9 0.0 collective-permute-done.3
  59.9 0.7 broadcast_in_dim.29
  60.5 8.0 %all-to-all-start.1 = ((bf16[8,24,384]{2,1,0:T(8,128)(2,1)}), bf16[8,24,384]{2,1,0:T(8,128)(2,1)S(1)}, u32[]{:S(2)}, u32[]{:S(2)}) async-start(bf16[8,24,384]{2,1,0:T(8,128)(2,1)} %broadcast_in_dim.29), calls=%async_computation.1 | async-start | bytes 294912 | tf_op jit(solution)/shard_map/all_to_all | solution.py:40
  68.6 0.0 copy-start.6
  68.6 5.7 %collective-permute-start.4 = (bf16[288,384]{1,0:T(8,128)(2,1)S(1)}, bf16[288,384]{1,0:T(8,128)(2,1)S(1)}, u32[]{:S(2)}, u32[]{:S(2)}) collective-permute-start(bf16[288,384]{1,0:T(8,128)(2,1)S(1)} %get-tuple-element.49), channel_id=1, source_target_pairs={{0,1},{2,3},{4,5},{6,7},{8,9},{10,11},{12,13},{14,15},{16,17},{18,... | collective-permute-start | bytes 663560 | tf_op jit(solution)/shard_map/ppermute | solution.py:34
  74.3 3.0 %collective-permute-start.5 = (bf16[288,384]{1,0:T(8,128)(2,1)S(1)}, bf16[288,384]{1,0:T(8,128)(2,1)S(1)}, u32[]{:S(2)}, u32[]{:S(2)}) collective-permute-start(bf16[288,384]{1,0:T(8,128)(2,1)S(1)} %broadcast_select_fusion), channel_id=1, source_target_pairs={{1,2},{3,4},{5,6},{7,8},{9,10},{11,12},{13,14},{15,16},{17,18},{19... | collective-permute-start | bytes 663560 | tf_op jit(solution)/shard_map/ppermute | solution.py:330
  77.3 0.0 all-to-all-done.1.parts
  77.3 0.9 gather.1
  78.2 5.9 %all-to-all-start.2 = ((bf16[32,24,384]{2,1,0:T(8,128)(2,1)}), bf16[32,24,384]{2,1,0:T(8,128)(2,1)S(1)}, u32[]{:S(2)}, u32[]{:S(2)}) async-start(bf16[32,24,384]{2,1,0:T(8,128)(2,1)} %gather.1), calls=%async_computation.2 | async-start | bytes 1179648 | tf_op jit(solution)/shard_map/all_to_all | solution.py:333
  84.1 0.0 copy-start.7
  84.1 0.0 collective-permute-done.4.near
  84.1 0.0 collective-permute-done.5.far
  84.1 0.0 copy-done.4
  84.1 1.0 grad_input.1
  85.1 12.2 %all-to-all-done.2 = bf16[32,24,384]{2,1,0:T(8,128)(2,1)S(1)} async-done(((bf16[32,24,384]{2,1,0:T(8,128)(2,1)}), bf16[32,24,384]{2,1,0:T(8,128)(2,1)S(1)}, u32[]{:S(2)}, u32[]{:S(2)}) %all-to-all-start.2) | async-done | bytes 589856 | tf_op jit(solution)/shard_map/all_to_all | solution.py:333
  97.3 8.0 %collective-permute-start.6 = (bf16[768,384]{1,0:T(8,128)(2,1)S(1)}, bf16[768,384]{1,0:T(8,128)(2,1)S(1)}, u32[]{:S(2)}, u32[]{:S(2)}) collective-permute-start(bf16[768,384]{1,0:T(8,128)(2,1)S(1)} %bitcast.18), channel_id=1, source_target_pairs={{0,64},{64,0},{1,65},{65,1},{2,66},{66,2},{3,67},{67,3},{4,68},{68... | collective-permute-start | bytes 1769480 | tf_op jit(solution)/shard_map/ppermute | solution.py:338
  105.4 1.6 %collective-permute-done.6.other = bf16[768,384]{1,0:T(8,128)(2,1)S(1)} collective-permute-done((bf16[768,384]{1,0:T(8,128)(2,1)S(1)}, bf16[768,384]{1,0:T(8,128)(2,1)S(1)}, u32[]{:S(2)}, u32[]{:S(2)}) %collective-permute-start.6) | collective-permute-done | bytes 589856 | tf_op jit(solution)/shard_map/ppermute | solution.py:338
  107.0 1.8 %outputs.1 = (f32[384,1152]{1,0:T(8,128)}, f32[384,384]{1,0:T(8,128)}, f32[384]{0:T(512)}) custom-call(s32[1]{0:T(128)} %bitcast.core, bf16[768,384]{1,0:T(8,128)(2,1)S(1)} %bitcast.19, bf16[768,384]{1,0:T(8,128)(2,1)S(1)} %collective-permute-done.6.other, bf16[384,1152]{1,0:T(8,128)(2,1)S(1)} %copy-done.1, f32[384]{0:T(512)S(1)} %copy-done.7), custom_call_target="tpu_custom_call" | custom-call | flops 100000000 | bytes 4000000 | tf_op jit(solution)/shard_map/outputs/pallas_call | solution.py:340
  (14 shorter events, 0.1 us)
Async XLA Ops:
  0.6 19.0 %collective-permute-start.1 = (bf16[288,384]{1,0:T(8,128)(2,1)}, bf16[288,384]{1,0:T(8,128)(2,1)S(1)}, u32[]{:S(2)}, u32[]{:S(2)}) collective-permute-start(bf16[288,384]{1,0:T(8,128)(2,1)} %bitcast.20), channel_id=1, source_target_pairs={{1,2},{3,4},{5,6},{7,8},{9,10},{11,12},{13,14},{15,16},{17,18},{19... | collective-permute-start | bytes 663560 | tf_op jit(solution)/shard_map/ppermute | solution.py:34
  1.3 18.3 %collective-permute-start = (bf16[288,384]{1,0:T(8,128)(2,1)}, bf16[288,384]{1,0:T(8,128)(2,1)S(1)}, u32[]{:S(2)}, u32[]{:S(2)}) collective-permute-start(bf16[288,384]{1,0:T(8,128)(2,1)} %bitcast.21), channel_id=1, source_target_pairs={{0,1},{2,3},{4,5},{6,7},{8,9},{10,11},{12,13},{14,15},{16,17},{18,... | collective-permute-start | bytes 663560 | tf_op jit(solution)/shard_map/ppermute | solution.py:34
  12.2 1.2 %copy-start = (bf16[384,1152]{1,0:T(8,128)(2,1)S(1)}, bf16[384,1152]{1,0:T(8,128)(2,1)}, u32[]{:S(2)}) copy-start(bf16[384,1152]{1,0:T(8,128)(2,1)} %wqkv.5) | copy-start | bytes 2654212
  13.4 1.0 copy-start.2
  14.4 0.9 copy-start.3
  15.3 0.9 copy-start.5
  16.2 0.7 copy-start.8
  16.9 2.8 %copy-start.1 = (bf16[384,1152]{1,0:T(8,128)(2,1)S(1)}, bf16[384,1152]{1,0:T(8,128)(2,1)}, u32[]{:S(2)}) copy-start(bf16[384,1152]{1,0:T(8,128)(2,1)} %wqkv.5) | copy-start | bytes 2654212
  26.6 5.0 %collective-permute-start.2 = (bf16[768,384]{1,0:T(8,128)(2,1)S(1)}, bf16[768,384]{1,0:T(8,128)(2,1)S(1)}, u32[]{:S(2)}, u32[]{:S(2)}) collective-permute-start(bf16[768,384]{1,0:T(8,128)(2,1)S(1)} %get-tuple-element.41), channel_id=1, source_target_pairs={{0,64},{64,0},{1,65},{65,1},{2,66},{66,2},{3,67},{67,3},{4,68},{68... | collective-permute-start | bytes 1769480 | tf_op jit(solution)/shard_map/ppermute | solution.py:306
  32.5 27.2 %all-to-all-start = ((bf16[32,24,384]{2,1,0:T(8,128)(2,1)}), bf16[32,24,384]{2,1,0:T(8,128)(2,1)S(1)}, u32[]{:S(2)}, u32[]{:S(2)}) async-start(bf16[32,24,384]{2,1,0:T(8,128)(2,1)} %bitcast.9), calls=%async_computation | async-start | bytes 1179648 | tf_op jit(solution)/shard_map/all_to_all | solution.py:324
  43.9 15.9 %collective-permute-start.3 = (bf16[288,384]{1,0:T(8,128)(2,1)S(1)}, bf16[288,384]{1,0:T(8,128)(2,1)S(1)}, u32[]{:S(2)}, u32[]{:S(2)}) collective-permute-start(bf16[288,384]{1,0:T(8,128)(2,1)S(1)} %get-tuple-element.46), channel_id=1, source_target_pairs={{31,63},{0,32},{63,31},{32,0},{95,127},{64,96},{127,95},{96,64},{1... | collective-permute-start | bytes 663560 | tf_op jit(solution)/shard_map/ppermute | solution.py:321
  60.5 16.7 %all-to-all-start.1 = ((bf16[8,24,384]{2,1,0:T(8,128)(2,1)}), bf16[8,24,384]{2,1,0:T(8,128)(2,1)S(1)}, u32[]{:S(2)}, u32[]{:S(2)}) async-start(bf16[8,24,384]{2,1,0:T(8,128)(2,1)} %broadcast_in_dim.29), calls=%async_computation.1 | async-start | bytes 294912 | tf_op jit(solution)/shard_map/all_to_all | solution.py:40
  68.5 15.5 %copy-start.4 = (bf16[1,288,384]{2,1,0:T(8,128)(2,1)S(1)}, bf16[1,288,384]{2,1,0:T(8,128)(2,1)}, u32[]{:S(2)}) copy-start(bf16[1,288,384]{2,1,0:T(8,128)(2,1)} %param.7) | copy-start | bytes 663556
  68.6 15.6 %copy-start.6 = (bf16[1,288,384]{2,1,0:T(8,128)(2,1)S(1)}, bf16[1,288,384]{2,1,0:T(8,128)(2,1)}, u32[]{:S(2)}) copy-start(bf16[1,288,384]{2,1,0:T(8,128)(2,1)} %param.8) | copy-start | bytes 663556
  68.6 15.5 %collective-permute-start.4 = (bf16[288,384]{1,0:T(8,128)(2,1)S(1)}, bf16[288,384]{1,0:T(8,128)(2,1)S(1)}, u32[]{:S(2)}, u32[]{:S(2)}) collective-permute-start(bf16[288,384]{1,0:T(8,128)(2,1)S(1)} %get-tuple-element.49), channel_id=1, source_target_pairs={{0,1},{2,3},{4,5},{6,7},{8,9},{10,11},{12,13},{14,15},{16,17},{18,... | collective-permute-start | bytes 663560 | tf_op jit(solution)/shard_map/ppermute | solution.py:34
  74.3 9.8 %collective-permute-start.5 = (bf16[288,384]{1,0:T(8,128)(2,1)S(1)}, bf16[288,384]{1,0:T(8,128)(2,1)S(1)}, u32[]{:S(2)}, u32[]{:S(2)}) collective-permute-start(bf16[288,384]{1,0:T(8,128)(2,1)S(1)} %broadcast_select_fusion), channel_id=1, source_target_pairs={{1,2},{3,4},{5,6},{7,8},{9,10},{11,12},{13,14},{15,16},{17,18},{19... | collective-permute-start | bytes 663560 | tf_op jit(solution)/shard_map/ppermute | solution.py:330
  78.2 19.1 %all-to-all-start.2 = ((bf16[32,24,384]{2,1,0:T(8,128)(2,1)}), bf16[32,24,384]{2,1,0:T(8,128)(2,1)S(1)}, u32[]{:S(2)}, u32[]{:S(2)}) async-start(bf16[32,24,384]{2,1,0:T(8,128)(2,1)} %gather.1), calls=%async_computation.2 | async-start | bytes 1179648 | tf_op jit(solution)/shard_map/all_to_all | solution.py:333
  84.1 22.9 %copy-start.7 = (f32[384]{0:T(512)S(1)}, f32[384]{0:T(512)}, u32[]{:S(2)}) copy-start(f32[384]{0:T(512)} %gain.1) | copy-start | bytes 4612
  97.3 9.7 %collective-permute-start.6 = (bf16[768,384]{1,0:T(8,128)(2,1)S(1)}, bf16[768,384]{1,0:T(8,128)(2,1)S(1)}, u32[]{:S(2)}, u32[]{:S(2)}) collective-permute-start(bf16[768,384]{1,0:T(8,128)(2,1)S(1)} %bitcast.18), channel_id=1, source_target_pairs={{0,64},{64,0},{1,65},{65,1},{2,66},{66,2},{3,67},{67,3},{4,68},{68... | collective-permute-start | bytes 1769480 | tf_op jit(solution)/shard_map/ppermute | solution.py:338

commit v5 on v4

--- a/solution.py
+++ b/solution.py
@@ -2,6 +2,7 @@
 
 import jax
 import jax.numpy as jnp
+import numpy as np
 from jax import lax
 from jax.experimental import pallas as pl
 from jax.experimental.pallas import tpu as pltpu
@@ -34,10 +35,17 @@
     return lax.ppermute(block, SPACE, pairs + [(b, a) for a, b in pairs])
 
 
-def spread(part, axes):
-    count = lax.axis_size(axes)
-    copies = jnp.broadcast_to(part[None], (count,) + part.shape)
-    return lax.all_to_all(copies, axes, 0, 0, tiled=True)
+AXES = ("yl", "c", "yh", "x", "z")
+SIZES = (4, 2, 2, 4, 8)
+GRID = np.arange(math.prod(SIZES)).reshape(SIZES)
+PLANES = [GRID[i, 0, j].ravel().tolist() for i in range(4) for j in range(2)]
+PLANES += [GRID[:, 1, :, :, k].ravel().tolist() for k in range(8)]
+RINGS = [GRID[:, 0, :, i, k].ravel().tolist() for i in range(4) for k in range(8)]
+RINGS += [GRID[i, 1, j, k].ravel().tolist() for i in range(4) for j in range(2) for k in range(4)]
+
+
+def exchanged(parts, groups):
+    return lax.all_to_all(parts, AXES, 0, 0, axis_index_groups=groups, tiled=True)
 
 
 def total(parts):
@@ -82,7 +90,7 @@
 
 
 def attention_kernel(
-    core, near, far, own, kv, q8, q8t, g, scaled, fq, fk, gain, wqkv,
+    core, far, near, own, kv, q8, q8t, g, scaled, fq, fk, gain, wqkv,
     send, dt, dq, normed_t, attn_t, normed, table, scores, expo, dshare, dscores,
 ):
     normed[0:ROWS] = own[...]
@@ -300,7 +308,7 @@
         ),
         flops=3 * 10**9,
         moved=4 * 10**6,
-    )(core, near, far, own, kv, q8, q8t, g, scaled, fq, fk, gains, w_qkv)
+    )(core, far, near, own, kv, q8, q8t, g, scaled, fq, fk, gains, w_qkv)
 
     pair = [(0, 1), (1, 0)]
     arrived = lax.ppermute(send, "c", pair)
@@ -317,20 +325,20 @@
     back_near = swapped(back_near, 0)
     count = lax.axis_size(SPACE)
     middle = count // 2
-    ends = [(middle - 1, count - 1), (0, middle)]
-    crossed = lax.ppermute(back_far, SPACE, ends + [(b, a) for a, b in ends])
-    plane = lax.axis_size(("x", "z"))
+    pairs = [(i, i + 1) for i in range(1, count - 1, 2) if i != middle - 1]
+    pairs = pairs + [(b, a) for a, b in pairs] + [(middle - 1, 0), (middle, count - 1)]
+    moved = lax.ppermute(back_far, SPACE, pairs)
+    plane, ring = len(PLANES[0]), len(RINGS[0])
     parts = half.reshape(plane, 2 * WIDTH // plane, WIDTH)
-    part = total(lax.all_to_all(parts, ("x", "z"), 0, 0, tiled=True))
-    part, crossed = lax.optimization_barrier((part, crossed))
-    at_end = jnp.logical_or(position == 0, position == count - 1)
-    back_far = jnp.where(at_end, crossed, back_far)
-    pairs = [(i, i + 1) for i in range(1, count - 1, 2) if i != middle - 1]
-    pairs = pairs + [(b, a) for a, b in pairs] + [(count - 1, middle), (0, middle - 1)]
-    back_far = lax.ppermute(back_far, SPACE, pairs)
-    parts = spread(part, ("yl", "yh"))
+    part = total(exchanged(parts, PLANES))
+    part, moved = lax.optimization_barrier((part, moved))
+    crossed = lax.ppermute(moved, SPACE, [(0, middle), (count - 1, middle - 1)])
+    inside = jnp.logical_and(position > 0, position < count - 1)
+    in_middle = jnp.logical_or(position == middle - 1, position == middle)
+    back_far = jnp.where(in_middle, crossed, jnp.where(inside, moved, jnp.zeros_like(moved)))
+    parts = exchanged(jnp.broadcast_to(part[None], (ring,) + part.shape), RINGS)
     (copies,) = local(gather_kernel, "gather", (((plane,) + part.shape, b16),), [whole], 4)(parts)
-    half = lax.all_to_all(copies, ("x", "z"), 0, 0, tiled=True).reshape(2 * WIDTH, WIDTH)
+    half = exchanged(copies, PLANES).reshape(2 * WIDTH, WIDTH)
     (grad_input,) = local(input_kernel, "grad_input", (rows,), [whole] * 6, 8, flops=10**10)(
         base, back_near, back_far, values, cot, gains
     )
@@ -349,7 +357,7 @@
 
 
 def solution(mesh):
-    fine = Mesh(mesh.devices.reshape(4, 2, 2, 4, 8), ("yl", "c", "yh", "x", "z"))
+    fine = Mesh(mesh.devices.reshape(SIZES), AXES)
     region = ("yl", "c")
     split = P(region, SPACE, None)
     return jax.shard_map(

time: 110 us -> 106 us (0.964)
  starting transfers between devices: 61.1 us -> 50.1 us
  waiting for transfers between devices: 22.5 us -> 29.7 us
    all_to_all x3, waiting for transfers between devices: 20.9 us -> 26.7 us  [exchanged(): lax.all_to_all(parts, AXES, 0, 0, axis_index_groups=groups, tiled=True)]
    ppermute x2, starting transfers between devices: 10.1 us -> 6.41 us  [the longest x1 5.12 us: shards(): crossed = lax.ppermute(moved, SPACE, [(0, middle), (count - 1, middle - 1)])]
    ppermute x3, starting transfers between devices: 14.5 us -> 10.9 us  [swapped(): return lax.ppermute(block, SPACE, pairs + [(b, a) for a, b in pairs])]
    ppermute x1, starting transfers between devices: 8.04 us -> 5.16 us  [shards(): other = lax.ppermute(half, 'c', pair)]
    ppermute x2, waiting for transfers between devices: 0.01 us -> 1.39 us  [the longest x1 1.39 us: shards(): moved = lax.ppermute(back_far, SPACE, pairs)]
  transfers between devices with their start and end apart: 10 -> 10, of which waited for: 3 -> 5; matrix products, arithmetic and copies ran while one was open for 3% -> 3% of each run, Pallas kernels for 6% -> 6%
where the time goes in v5:
time: 106 us; the launch traced here: 105 us
  starting transfers between devices  50.1 us (47%)
  waiting for transfers between devices  29.7 us (28%)
  Pallas kernels  14.9 us (14%)
  local copies, waits for them, and re-layouts  6.95 us (7%)
  other arithmetic  2.37 us (2%)
    all_to_all x3, waiting for transfers between devices, exchanged(): lax.all_to_all(parts, AXES, 0, 0, axis_index_groups=groups, tiled=True)  26.7 us
    all_to_all x3, starting transfers between devices, exchanged(): lax.all_to_all(parts, AXES, 0, 0, axis_index_groups=groups, tiled=True)  24.5 us
    ppermute x3, starting transfers between devices, swapped(): return lax.ppermute(block, SPACE, pairs + [(b, a) for a, b in pairs])  10.9 us
    pallas_call x1, Pallas kernels, shards(): local(attention_kernel, 'attention', (half_rows, ((2 * WIDTH, KEYS), b16)...  6.97 us
    unnamed x19, local copies, waits for them, and re-layouts  5.37 us
    ppermute x1, starting transfers between devices, shards(): other = lax.ppermute(half, 'c', pair)  5.16 us
    ppermute x1, starting transfers between devices, shards(): crossed = lax.ppermute(moved, SPACE, [(0, middle), (count - 1, middle - 1)])  5.12 us
    ppermute x1, starting transfers between devices, shards(): arrived = lax.ppermute(send, 'c', pair)  3.14 us
  transfers between devices with their start and end apart: 10, of which 5 were waited for; matrix products, arithmetic and copies ran while one was open for 3% of the time, Pallas kernels for 6%

profile of v5, /device:TPU:1, one launch (start us, length us, event | category | flops | bytes accessed | tf_op | source)
XLA Modules:
  0.0 105.0 jit_solution(7197020359967584743)
XLA Ops:
  0.6 0.7 collective-permute-start
  1.3 8.2 %collective-permute-start.1 = (bf16[288,384]{1,0:T(8,128)(2,1)}, bf16[288,384]{1,0:T(8,128)(2,1)S(1)}, u32[]{:S(2)}, u32[]{:S(2)}) collective-permute-start(bf16[288,384]{1,0:T(8,128)(2,1)} %bitcast.21), channel_id=1, source_target_pairs={{0,1},{2,3},{4,5},{6,7},{8,9},{10,11},{12,13},{14,15},{16,17},{18,... | collective-permute-start | bytes 663560 | tf_op jit(solution)/shard_map/ppermute | solution.py:35
  9.5 0.7 copy.16
  10.2 0.7 broadcast_compare_fusion
  10.9 0.1 add_multiply_fusion
  11.0 0.1 iota_add_fusion
  11.1 0.1 add.54
  11.1 0.2 and_reduce_fusion
  11.3 0.1 copy.11
  11.5 0.1 fusion.fk
  11.5 0.7 broadcast_in_dim.28.gain
  12.2 1.2 %copy-done = bf16[384,1152]{1,0:T(8,128)(2,1)S(1)} copy-done((bf16[384,1152]{1,0:T(8,128)(2,1)S(1)}, bf16[384,1152]{1,0:T(8,128)(2,1)}, u32[]{:S(2)}) %copy-start) | copy-done | bytes 884760
  13.4 1.0 copy-done.2
  14.4 0.9 copy-done.3
  15.3 0.9 copy-done.5
  16.2 0.7 copy-done.8
  16.9 2.5 %prepare.1 = (bf16[288,384]{1,0:T(8,128)(2,1)S(1)}, bf16[288,768]{1,0:T(8,128)(2,1)S(1)}, bf16[288,384]{1,0:T(8,128)(2,1)S(1)}, bf16[384,288]{1,0:T(8,128)(2,1)S...) custom-call(s32[9]{0:T(128)S(1)} %bitcast.26, bf16[288,384]{1,0:T(8,128)(2,1)S(1)} %bitcast.22, ...), custom_call_target="tpu_custom_call" | custom-call | flops 400000000 | bytes 1000000 | tf_op jit(solution)/shard_map/prepare/pallas_call | solution.py:267
  19.4 0.2 fusion.1.fq
  19.6 0.0 collective-permute-done.far
  19.6 0.0 collective-permute-done.1.near
  19.6 0.0 copy-done.1
  19.7 7.0 %attention.1 = (bf16[768,384]{1,0:T(8,128)(2,1)S(1)}, bf16[768,896]{1,0:T(8,128)(2,1)S(1)}, bf16[288,384]{1,0:T(8,128)(2,1)S(1)}, bf16[384,896]{1,0:T(8,128)(2,1)S(1)}, bf16[384,288]{1,0:T(8,128)(2,1)S(1)}) custom-call(s32[1]{0:T(128)} %bitcast.core, bf16[288,384]{1,0:T(8,128)(2,1)S(1)} %collective-permute-done.far, ...), custom_call_target="tpu_custom_call" | custom-call | flops 3000000000 | bytes 4000000 | tf_op jit(solution)/shard_map/attention/pallas_call | solution.py:295
  26.6 3.1 %collective-permute-start.2 = (bf16[768,384]{1,0:T(8,128)(2,1)S(1)}, bf16[768,384]{1,0:T(8,128)(2,1)S(1)}, u32[]{:S(2)}, u32[]{:S(2)}) collective-permute-start(bf16[768,384]{1,0:T(8,128)(2,1)S(1)} %get-tuple-element.41), channel_id=1, source_target_pairs={{0,64},{64,0},{1,65},{65,1},{2,66},{66,2},{3,67},{67,3},{4,68},{68... | collective-permute-start | bytes 1769480 | tf_op jit(solution)/shard_map/ppermute | solution.py:314
  29.8 1.8 %back.1 = (bf16[768,384]{1,0:T(8,128)(2,1)S(1)}, f32[288,384]{1,0:T(8,128)S(1)}, bf16[288,384]{1,0:T(8,128)(2,1)S(1)}, bf16[288,384]{1,0:T(8,128)(2,1)S(1)}) custom-call(s32[1]{0:T(128)} %bitcast.core, bf16[768,896]{1,0:T(8,128)(2,1)S(1)} %get-tuple-element.36.dt, bf16[288,384]{1,0:T(8,128)(2,1)S(1)} %get-tuple-element.37.dq, ...), custom_call_target="tpu_custom_call" | custom-call | flops 1000000000 | bytes 1000000 | tf_op jit(solution)/shard_map/back/pallas_call | solution.py:315
  31.6 0.0 collective-permute-done.2
  31.6 1.0 add_convert_fusion
  32.6 14.0 %all-to-all-start = ((bf16[32,24,384]{2,1,0:T(8,128)(2,1)}), bf16[32,24,384]{2,1,0:T(8,128)(2,1)S(1)}, u32[]{:S(2)}, u32[]{:S(2)}) async-start(bf16[32,24,384]{2,1,0:T(8,128)(2,1)} %bitcast.9), calls=%async_computation | async-start | bytes 1179648 | tf_op jit(solution)/shard_map/all_to_all | solution.py:48
  46.5 1.3 %collective-permute-start.3 = (bf16[288,384]{1,0:T(8,128)(2,1)S(1)}, bf16[288,384]{1,0:T(8,128)(2,1)S(1)}, u32[]{:S(2)}, u32[]{:S(2)}) collective-permute-start(bf16[288,384]{1,0:T(8,128)(2,1)S(1)} %get-tuple-element.46), channel_id=1, source_target_pairs={{1,2},{3,4},{5,6},{7,8},{9,10},{11,12},{13,14},{15,16},{17,18},{19... | collective-permute-start | bytes 663560 | tf_op jit(solution)/shard_map/ppermute | solution.py:330
  47.8 12.9 %all-to-all-done = bf16[32,24,384]{2,1,0:T(8,128)(2,1)S(1)} async-done(((bf16[32,24,384]{2,1,0:T(8,128)(2,1)}), bf16[32,24,384]{2,1,0:T(8,128)(2,1)S(1)}, u32[]{:S(2)}, u32[]{:S(2)}) %all-to-all-start) | async-done | bytes 589856 | tf_op jit(solution)/shard_map/all_to_all | solution.py:48
  60.8 0.1 reduce_sum.12
  60.8 1.4 %collective-permute-done.3 = bf16[288,384]{1,0:T(8,128)(2,1)S(1)} collective-permute-done((bf16[288,384]{1,0:T(8,128)(2,1)S(1)}, bf16[288,384]{1,0:T(8,128)(2,1)S(1)}, u32[]{:S(2)}, u32[]{:S(2)}) %collective-permute-start.3) | collective-permute-done | bytes 221216 | tf_op jit(solution)/shard_map/ppermute | solution.py:330
  62.2 0.7 broadcast_in_dim.32
  62.9 3.5 %all-to-all-start.1 = ((bf16[8,24,384]{2,1,0:T(8,128)(2,1)}), bf16[8,24,384]{2,1,0:T(8,128)(2,1)S(1)}, u32[]{:S(2)}, u32[]{:S(2)}) async-start(bf16[8,24,384]{2,1,0:T(8,128)(2,1)} %broadcast_in_dim.32), calls=%async_computation.1 | async-start | bytes 294912 | tf_op jit(solution)/shard_map/all_to_all | solution.py:48
  66.4 5.1 %collective-permute-start.5 = (bf16[288,384]{1,0:T(8,128)(2,1)S(1)}, bf16[288,384]{1,0:T(8,128)(2,1)S(1)}, u32[]{:S(2)}, u32[]{:S(2)}) collective-permute-start(bf16[288,384]{1,0:T(8,128)(2,1)S(1)} %collective-permute-done.3), channel_id=1, source_target_pairs={{0,32},{63,31},{64,96},{127,95},{128,160},{191,159},{192,224},{255... | collective-permute-start | bytes 663560 | tf_op jit(solution)/shard_map/ppermute | solution.py:335
  71.6 0.0 copy-start.4
  71.6 0.0 copy-start.6
  71.6 2.1 %collective-permute-start.4 = (bf16[288,384]{1,0:T(8,128)(2,1)S(1)}, bf16[288,384]{1,0:T(8,128)(2,1)S(1)}, u32[]{:S(2)}, u32[]{:S(2)}) collective-permute-start(bf16[288,384]{1,0:T(8,128)(2,1)S(1)} %get-tuple-element.49), channel_id=1, source_target_pairs={{0,1},{2,3},{4,5},{6,7},{8,9},{10,11},{12,13},{14,15},{16,17},{18,... | collective-permute-start | bytes 663560 | tf_op jit(solution)/shard_map/ppermute | solution.py:35
  73.6 1.0 all-to-all-done.1.parts
  74.6 0.9 gather.1
  75.5 7.0 %all-to-all-start.2 = ((bf16[32,24,384]{2,1,0:T(8,128)(2,1)}), bf16[32,24,384]{2,1,0:T(8,128)(2,1)S(1)}, u32[]{:S(2)}, u32[]{:S(2)}) async-start(bf16[32,24,384]{2,1,0:T(8,128)(2,1)} %gather.1), calls=%async_computation.2 | async-start | bytes 1179648 | tf_op jit(solution)/shard_map/all_to_all | solution.py:48
  82.5 0.0 collective-permute-done.5
  82.6 0.0 copy-start.7
  82.6 0.0 collective-permute-done.4.near
  82.6 1.0 grad_input.1
  83.6 12.8 %all-to-all-done.2 = bf16[32,24,384]{2,1,0:T(8,128)(2,1)S(1)} async-done(((bf16[32,24,384]{2,1,0:T(8,128)(2,1)}), bf16[32,24,384]{2,1,0:T(8,128)(2,1)S(1)}, u32[]{:S(2)}, u32[]{:S(2)}) %all-to-all-start.2) | async-done | bytes 589856 | tf_op jit(solution)/shard_map/all_to_all | solution.py:48
  96.4 5.2 %collective-permute-start.6 = (bf16[768,384]{1,0:T(8,128)(2,1)S(1)}, bf16[768,384]{1,0:T(8,128)(2,1)S(1)}, u32[]{:S(2)}, u32[]{:S(2)}) collective-permute-start(bf16[768,384]{1,0:T(8,128)(2,1)S(1)} %bitcast.18), channel_id=1, source_target_pairs={{0,64},{64,0},{1,65},{65,1},{2,66},{66,2},{3,67},{67,3},{4,68},{68... | collective-permute-start | bytes 1769480 | tf_op jit(solution)/shard_map/ppermute | solution.py:346
  101.6 1.6 %collective-permute-done.6.other = bf16[768,384]{1,0:T(8,128)(2,1)S(1)} collective-permute-done((bf16[768,384]{1,0:T(8,128)(2,1)S(1)}, bf16[768,384]{1,0:T(8,128)(2,1)S(1)}, u32[]{:S(2)}, u32[]{:S(2)}) %collective-permute-start.6) | collective-permute-done | bytes 589856 | tf_op jit(solution)/shard_map/ppermute | solution.py:346
  103.2 1.8 %outputs.1 = (f32[384,1152]{1,0:T(8,128)}, f32[384,384]{1,0:T(8,128)}, f32[384]{0:T(512)}) custom-call(s32[1]{0:T(128)} %bitcast.core, bf16[768,384]{1,0:T(8,128)(2,1)S(1)} %bitcast.19, bf16[768,384]{1,0:T(8,128)(2,1)S(1)} %collective-permute-done.6.other, bf16[384,1152]{1,0:T(8,128)(2,1)S(1)} %copy-done.1, f32[384]{0:T(512)S(1)} %copy-done.7), custom_call_target="tpu_custom_call" | custom-call | flops 100000000 | bytes 4000000 | tf_op jit(solution)/shard_map/outputs/pallas_call | solution.py:348
  (14 shorter events, 0.1 us)
Async XLA Ops:
  0.6 19.0 %collective-permute-start = (bf16[288,384]{1,0:T(8,128)(2,1)}, bf16[288,384]{1,0:T(8,128)(2,1)S(1)}, u32[]{:S(2)}, u32[]{:S(2)}) collective-permute-start(bf16[288,384]{1,0:T(8,128)(2,1)} %bitcast.20), channel_id=1, source_target_pairs={{1,2},{3,4},{5,6},{7,8},{9,10},{11,12},{13,14},{15,16},{17,18},{19... | collective-permute-start | bytes 663560 | tf_op jit(solution)/shard_map/ppermute | solution.py:35
  1.3 18.3 %collective-permute-start.1 = (bf16[288,384]{1,0:T(8,128)(2,1)}, bf16[288,384]{1,0:T(8,128)(2,1)S(1)}, u32[]{:S(2)}, u32[]{:S(2)}) collective-permute-start(bf16[288,384]{1,0:T(8,128)(2,1)} %bitcast.21), channel_id=1, source_target_pairs={{0,1},{2,3},{4,5},{6,7},{8,9},{10,11},{12,13},{14,15},{16,17},{18,... | collective-permute-start | bytes 663560 | tf_op jit(solution)/shard_map/ppermute | solution.py:35
  12.2 1.2 %copy-start = (bf16[384,1152]{1,0:T(8,128)(2,1)S(1)}, bf16[384,1152]{1,0:T(8,128)(2,1)}, u32[]{:S(2)}) copy-start(bf16[384,1152]{1,0:T(8,128)(2,1)} %wqkv.5) | copy-start | bytes 2654212
  13.4 1.0 copy-start.2
  14.4 0.9 copy-start.3
  15.3 0.9 copy-start.5
  16.2 0.7 copy-start.8
  16.9 2.8 %copy-start.1 = (bf16[384,1152]{1,0:T(8,128)(2,1)S(1)}, bf16[384,1152]{1,0:T(8,128)(2,1)}, u32[]{:S(2)}) copy-start(bf16[384,1152]{1,0:T(8,128)(2,1)} %wqkv.5) | copy-start | bytes 2654212
  26.6 5.0 %collective-permute-start.2 = (bf16[768,384]{1,0:T(8,128)(2,1)S(1)}, bf16[768,384]{1,0:T(8,128)(2,1)S(1)}, u32[]{:S(2)}, u32[]{:S(2)}) collective-permute-start(bf16[768,384]{1,0:T(8,128)(2,1)S(1)} %get-tuple-element.41), channel_id=1, source_target_pairs={{0,64},{64,0},{1,65},{65,1},{2,66},{66,2},{3,67},{67,3},{4,68},{68... | collective-permute-start | bytes 1769480 | tf_op jit(solution)/shard_map/ppermute | solution.py:314
  32.6 28.2 %all-to-all-start = ((bf16[32,24,384]{2,1,0:T(8,128)(2,1)}), bf16[32,24,384]{2,1,0:T(8,128)(2,1)S(1)}, u32[]{:S(2)}, u32[]{:S(2)}) async-start(bf16[32,24,384]{2,1,0:T(8,128)(2,1)} %bitcast.9), calls=%async_computation | async-start | bytes 1179648 | tf_op jit(solution)/shard_map/all_to_all | solution.py:48
  46.5 15.7 %collective-permute-start.3 = (bf16[288,384]{1,0:T(8,128)(2,1)S(1)}, bf16[288,384]{1,0:T(8,128)(2,1)S(1)}, u32[]{:S(2)}, u32[]{:S(2)}) collective-permute-start(bf16[288,384]{1,0:T(8,128)(2,1)S(1)} %get-tuple-element.46), channel_id=1, source_target_pairs={{1,2},{3,4},{5,6},{7,8},{9,10},{11,12},{13,14},{15,16},{17,18},{19... | collective-permute-start | bytes 663560 | tf_op jit(solution)/shard_map/ppermute | solution.py:330
  62.9 11.7 %all-to-all-start.1 = ((bf16[8,24,384]{2,1,0:T(8,128)(2,1)}), bf16[8,24,384]{2,1,0:T(8,128)(2,1)S(1)}, u32[]{:S(2)}, u32[]{:S(2)}) async-start(bf16[8,24,384]{2,1,0:T(8,128)(2,1)} %broadcast_in_dim.32), calls=%async_computation.1 | async-start | bytes 294912 | tf_op jit(solution)/shard_map/all_to_all | solution.py:48
  66.4 16.1 %collective-permute-start.5 = (bf16[288,384]{1,0:T(8,128)(2,1)S(1)}, bf16[288,384]{1,0:T(8,128)(2,1)S(1)}, u32[]{:S(2)}, u32[]{:S(2)}) collective-permute-start(bf16[288,384]{1,0:T(8,128)(2,1)S(1)} %collective-permute-done.3), channel_id=1, source_target_pairs={{0,32},{63,31},{64,96},{127,95},{128,160},{191,159},{192,224},{255... | collective-permute-start | bytes 663560 | tf_op jit(solution)/shard_map/ppermute | solution.py:335
  71.6 11.1 %copy-start.4 = (bf16[1,288,384]{2,1,0:T(8,128)(2,1)S(1)}, bf16[1,288,384]{2,1,0:T(8,128)(2,1)}, u32[]{:S(2)}) copy-start(bf16[1,288,384]{2,1,0:T(8,128)(2,1)} %param.7) | copy-start | bytes 663556
  71.6 11.1 %copy-start.6 = (bf16[1,288,384]{2,1,0:T(8,128)(2,1)S(1)}, bf16[1,288,384]{2,1,0:T(8,128)(2,1)}, u32[]{:S(2)}) copy-start(bf16[1,288,384]{2,1,0:T(8,128)(2,1)} %param.8) | copy-start | bytes 663556
  71.6 11.0 %collective-permute-start.4 = (bf16[288,384]{1,0:T(8,128)(2,1)S(1)}, bf16[288,384]{1,0:T(8,128)(2,1)S(1)}, u32[]{:S(2)}, u32[]{:S(2)}) collective-permute-start(bf16[288,384]{1,0:T(8,128)(2,1)S(1)} %get-tuple-element.49), channel_id=1, source_target_pairs={{0,1},{2,3},{4,5},{6,7},{8,9},{10,11},{12,13},{14,15},{16,17},{18,... | collective-permute-start | bytes 663560 | tf_op jit(solution)/shard_map/ppermute | solution.py:35
  75.5 20.9 %all-to-all-start.2 = ((bf16[32,24,384]{2,1,0:T(8,128)(2,1)}), bf16[32,24,384]{2,1,0:T(8,128)(2,1)S(1)}, u32[]{:S(2)}, u32[]{:S(2)}) async-start(bf16[32,24,384]{2,1,0:T(8,128)(2,1)} %gather.1), calls=%async_computation.2 | async-start | bytes 1179648 | tf_op jit(solution)/shard_map/all_to_all | solution.py:48
  82.6 20.6 %copy-start.7 = (f32[384]{0:T(512)S(1)}, f32[384]{0:T(512)}, u32[]{:S(2)}) copy-start(f32[384]{0:T(512)} %gain.1) | copy-start | bytes 4612
  96.4 6.8 %collective-permute-start.6 = (bf16[768,384]{1,0:T(8,128)(2,1)S(1)}, bf16[768,384]{1,0:T(8,128)(2,1)S(1)}, u32[]{:S(2)}, u32[]{:S(2)}) collective-permute-start(bf16[768,384]{1,0:T(8,128)(2,1)S(1)} %bitcast.18), channel_id=1, source_target_pairs={{0,64},{64,0},{1,65},{65,1},{2,66},{66,2},{3,67},{67,3},{4,68},{68... | collective-permute-start | bytes 1769480 | tf_op jit(solution)/shard_map/ppermute | solution.py:346

commit v6 on v5

--- a/solution.py
+++ b/solution.py
@@ -90,7 +90,7 @@
 
 
 def attention_kernel(
-    core, far, near, own, kv, q8, q8t, g, scaled, fq, fk, gain, wqkv,
+    core, near, far, own, kv, q8, q8t, g, scaled, fq, fk, gain, wqkv,
     send, dt, dq, normed_t, attn_t, normed, table, scores, expo, dshare, dscores,
 ):
     normed[0:ROWS] = own[...]
@@ -308,7 +308,7 @@
         ),
         flops=3 * 10**9,
         moved=4 * 10**6,
-    )(core, far, near, own, kv, q8, q8t, g, scaled, fq, fk, gains, w_qkv)
+    )(core, near, far, own, kv, q8, q8t, g, scaled, fq, fk, gains, w_qkv)
 
     pair = [(0, 1), (1, 0)]
     arrived = lax.ppermute(send, "c", pair)
@@ -325,17 +325,14 @@
     back_near = swapped(back_near, 0)
     count = lax.axis_size(SPACE)
     middle = count // 2
-    pairs = [(i, i + 1) for i in range(1, count - 1, 2) if i != middle - 1]
-    pairs = pairs + [(b, a) for a, b in pairs] + [(middle - 1, 0), (middle, count - 1)]
-    moved = lax.ppermute(back_far, SPACE, pairs)
+    moved = lax.ppermute(back_far, SPACE, [(middle - 1, 0), (middle, count - 1)])
     plane, ring = len(PLANES[0]), len(RINGS[0])
     parts = half.reshape(plane, 2 * WIDTH // plane, WIDTH)
     part = total(exchanged(parts, PLANES))
-    part, moved = lax.optimization_barrier((part, moved))
-    crossed = lax.ppermute(moved, SPACE, [(0, middle), (count - 1, middle - 1)])
-    inside = jnp.logical_and(position > 0, position < count - 1)
-    in_middle = jnp.logical_or(position == middle - 1, position == middle)
-    back_far = jnp.where(in_middle, crossed, jnp.where(inside, moved, jnp.zeros_like(moved)))
+    at_end = jnp.logical_or(position == 0, position == count - 1)
+    pairs = [(i, i + 1) for i in range(1, count - 1, 2) if i != middle - 1]
+    pairs = pairs + [(b, a) for a, b in pairs] + [(0, middle), (count - 1, middle - 1)]
+    back_far = lax.ppermute(jnp.where(at_end, moved, back_far), SPACE, pairs)
     parts = exchanged(jnp.broadcast_to(part[None], (ring,) + part.shape), RINGS)
     (copies,) = local(gather_kernel, "gather", (((plane,) + part.shape, b16),), [whole], 4)(parts)
     half = exchanged(copies, PLANES).reshape(2 * WIDTH, WIDTH)

time: 106 us -> 104 us (0.981)
  starting transfers between devices: 50.1 us -> 48.8 us
    ppermute x2, starting transfers between devices: 6.41 us -> 4.19 us  [the longest x1 2.9 us: shards(): back_far = lax.ppermute(jnp.where(at_end, moved, back_far), SPACE, pairs)]
    all_to_all x3, starting transfers between devices: 24.5 us -> 23 us  [exchanged(): lax.all_to_all(parts, AXES, 0, 0, axis_index_groups=groups, tiled=True)]
    ppermute x3, starting transfers between devices: 10.9 us -> 12.3 us  [swapped(): return lax.ppermute(block, SPACE, pairs + [(b, a) for a, b in pairs])]
    ppermute x2, waiting for transfers between devices: 1.39 us -> 0.01 us  [the longest x1 0.01 us: shards(): lax.ppermute(back_far, SPACE, [(middle - 1, 0), (middle, count - 1)])]
    all_to_all x3, waiting for transfers between devices: 26.7 us -> 27.8 us  [exchanged(): lax.all_to_all(parts, AXES, 0, 0, axis_index_groups=groups, tiled=True)]
  transfers between devices with their start and end apart: 10 -> 10, of which waited for: 5 -> 4; matrix products, arithmetic and copies ran while one was open for 3% -> 4% of each run, Pallas kernels for 6% -> 6%
where the time goes in v6:
time: 104 us; the launch traced here: 103 us
  starting transfers between devices  48.8 us (47%)
  waiting for transfers between devices  29.4 us (28%)
  Pallas kernels  14.9 us (14%)
  local copies, waits for them, and re-layouts  6.94 us (7%)
  other arithmetic  2.36 us (2%)
    all_to_all x3, waiting for transfers between devices, exchanged(): lax.all_to_all(parts, AXES, 0, 0, axis_index_groups=groups, tiled=True)  27.8 us
    all_to_all x3, starting transfers between devices, exchanged(): lax.all_to_all(parts, AXES, 0, 0, axis_index_groups=groups, tiled=True)  23 us
    ppermute x3, starting transfers between devices, swapped(): return lax.ppermute(block, SPACE, pairs + [(b, a) for a, b in pairs])  12.3 us
    pallas_call x1, Pallas kernels, shards(): local(attention_kernel, 'attention', (half_rows, ((2 * WIDTH, KEYS), b16)...  6.96 us
    ppermute x1, starting transfers between devices, shards(): other = lax.ppermute(half, 'c', pair)  6.13 us
    unnamed x19, local copies, waits for them, and re-layouts  5.36 us
    ppermute x1, starting transfers between devices, shards(): arrived = lax.ppermute(send, 'c', pair)  3.14 us
    ppermute x1, starting transfers between devices, shards(): back_far = lax.ppermute(jnp.where(at_end, moved, back_far), SPACE, pairs)  2.9 us
  transfers between devices with their start and end apart: 10, of which 4 were waited for; matrix products, arithmetic and copies ran while one was open for 4% of the time, Pallas kernels for 6%

profile of v6, /device:TPU:1, one launch (start us, length us, event | category | flops | bytes accessed | tf_op | source)
XLA Modules:
  0.0 103.4 jit_solution(7209250563385469033)
XLA Ops:
  0.6 0.7 collective-permute-start.1
  1.3 8.2 %collective-permute-start = (bf16[288,384]{1,0:T(8,128)(2,1)}, bf16[288,384]{1,0:T(8,128)(2,1)S(1)}, u32[]{:S(2)}, u32[]{:S(2)}) collective-permute-start(bf16[288,384]{1,0:T(8,128)(2,1)} %bitcast.21), channel_id=1, source_target_pairs={{0,1},{2,3},{4,5},{6,7},{8,9},{10,11},{12,13},{14,15},{16,17},{18,... | collective-permute-start | bytes 663560 | tf_op jit(solution)/shard_map/ppermute | solution.py:35
  9.5 0.7 broadcast_compare_fusion
  10.2 0.7 copy.16
  10.9 0.7 broadcast_in_dim.25.gain
  11.6 0.1 add_multiply_fusion
  11.7 0.1 iota_add_fusion
  11.7 0.1 add.54
  11.8 0.2 and_reduce_fusion
  12.0 0.1 copy.11
  12.2 0.1 fusion.fk
  12.2 0.0 copy-start
  12.2 1.2 %copy-done = bf16[384,1152]{1,0:T(8,128)(2,1)S(1)} copy-done((bf16[384,1152]{1,0:T(8,128)(2,1)S(1)}, bf16[384,1152]{1,0:T(8,128)(2,1)}, u32[]{:S(2)}) %copy-start) | copy-done | bytes 884760
  13.4 1.0 copy-done.2
  14.4 0.9 copy-done.3
  15.3 0.9 copy-done.5
  16.2 0.7 copy-done.8
  16.9 2.5 %prepare.1 = (bf16[288,384]{1,0:T(8,128)(2,1)S(1)}, bf16[288,768]{1,0:T(8,128)(2,1)S(1)}, bf16[288,384]{1,0:T(8,128)(2,1)S(1)}, bf16[384,288]{1,0:T(8,128)(2,1)S...) custom-call(s32[9]{0:T(128)S(1)} %bitcast.26, bf16[288,384]{1,0:T(8,128)(2,1)S(1)} %bitcast.22, ...), custom_call_target="tpu_custom_call" | custom-call | flops 400000000 | bytes 1000000 | tf_op jit(solution)/shard_map/prepare/pallas_call | solution.py:267
  19.4 0.2 fusion.1.fq
  19.6 0.0 collective-permute-done.1.far
  19.6 0.0 collective-permute-done.near
  19.6 0.0 copy-done.1
  19.6 7.0 %attention.1 = (bf16[768,384]{1,0:T(8,128)(2,1)S(1)}, bf16[768,896]{1,0:T(8,128)(2,1)S(1)}, bf16[288,384]{1,0:T(8,128)(2,1)S(1)}, bf16[384,896]{1,0:T(8,128)(2,1)S(1)}, bf16[384,288]{1,0:T(8,128)(2,1)S(1)}) custom-call(s32[1]{0:T(128)} %bitcast.core, bf16[288,384]{1,0:T(8,128)(2,1)S(1)} %collective-permute-done.near, ...), custom_call_target="tpu_custom_call" | custom-call | flops 3000000000 | bytes 4000000 | tf_op jit(solution)/shard_map/attention/pallas_call | solution.py:295
  26.6 3.1 %collective-permute-start.2 = (bf16[768,384]{1,0:T(8,128)(2,1)S(1)}, bf16[768,384]{1,0:T(8,128)(2,1)S(1)}, u32[]{:S(2)}, u32[]{:S(2)}) collective-permute-start(bf16[768,384]{1,0:T(8,128)(2,1)S(1)} %get-tuple-element.39), channel_id=1, source_target_pairs={{0,64},{64,0},{1,65},{65,1},{2,66},{66,2},{3,67},{67,3},{4,68},{68... | collective-permute-start | bytes 1769480 | tf_op jit(solution)/shard_map/ppermute | solution.py:314
  29.8 1.8 %back.1 = (bf16[768,384]{1,0:T(8,128)(2,1)S(1)}, f32[288,384]{1,0:T(8,128)S(1)}, bf16[288,384]{1,0:T(8,128)(2,1)S(1)}, bf16[288,384]{1,0:T(8,128)(2,1)S(1)}) custom-call(s32[1]{0:T(128)} %bitcast.core, bf16[768,896]{1,0:T(8,128)(2,1)S(1)} %get-tuple-element.34.dt, bf16[288,384]{1,0:T(8,128)(2,1)S(1)} %get-tuple-element.35.dq, ...), custom_call_target="tpu_custom_call" | custom-call | flops 1000000000 | bytes 1000000 | tf_op jit(solution)/shard_map/back/pallas_call | solution.py:315
  31.6 0.0 collective-permute-done.2
  31.6 1.0 add_convert_fusion
  32.5 14.0 %all-to-all-start = ((bf16[32,24,384]{2,1,0:T(8,128)(2,1)}), bf16[32,24,384]{2,1,0:T(8,128)(2,1)S(1)}, u32[]{:S(2)}, u32[]{:S(2)}) async-start(bf16[32,24,384]{2,1,0:T(8,128)(2,1)} %bitcast.9), calls=%async_computation | async-start | bytes 1179648 | tf_op jit(solution)/shard_map/all_to_all | solution.py:48
  46.5 1.3 %collective-permute-start.4 = (bf16[288,384]{1,0:T(8,128)(2,1)S(1)}, bf16[288,384]{1,0:T(8,128)(2,1)S(1)}, u32[]{:S(2)}, u32[]{:S(2)}) collective-permute-start(bf16[288,384]{1,0:T(8,128)(2,1)S(1)} %get-tuple-element.46), channel_id=1, source_target_pairs={{31,0},{32,63},{95,64},{96,127},{159,128},{160,191},{223,192},{224... | collective-permute-start | bytes 663560 | tf_op jit(solution)/shard_map/ppermute | solution.py:328
  47.8 12.7 %all-to-all-done = bf16[32,24,384]{2,1,0:T(8,128)(2,1)S(1)} async-done(((bf16[32,24,384]{2,1,0:T(8,128)(2,1)}), bf16[32,24,384]{2,1,0:T(8,128)(2,1)S(1)}, u32[]{:S(2)}, u32[]{:S(2)}) %all-to-all-start) | async-done | bytes 589856 | tf_op jit(solution)/shard_map/all_to_all | solution.py:48
  60.5 0.1 reduce_sum.12
  60.6 0.7 broadcast_in_dim.29
  61.3 5.1 %all-to-all-start.1 = ((bf16[8,24,384]{2,1,0:T(8,128)(2,1)}), bf16[8,24,384]{2,1,0:T(8,128)(2,1)S(1)}, u32[]{:S(2)}, u32[]{:S(2)}) async-start(bf16[8,24,384]{2,1,0:T(8,128)(2,1)} %broadcast_in_dim.29), calls=%async_computation.1 | async-start | bytes 294912 | tf_op jit(solution)/shard_map/all_to_all | solution.py:48
  66.4 0.0 copy-start.6
  66.4 3.5 %collective-permute-start.3 = (bf16[288,384]{1,0:T(8,128)(2,1)S(1)}, bf16[288,384]{1,0:T(8,128)(2,1)S(1)}, u32[]{:S(2)}, u32[]{:S(2)}) collective-permute-start(bf16[288,384]{1,0:T(8,128)(2,1)S(1)} %get-tuple-element.45), channel_id=1, source_target_pairs={{0,1},{2,3},{4,5},{6,7},{8,9},{10,11},{12,13},{14,15},{16,17},{18,... | collective-permute-start | bytes 663560 | tf_op jit(solution)/shard_map/ppermute | solution.py:35
  69.9 0.0 collective-permute-done.4
  70.0 2.9 %collective-permute-start.5 = (bf16[288,384]{1,0:T(8,128)(2,1)S(1)}, bf16[288,384]{1,0:T(8,128)(2,1)S(1)}, u32[]{:S(2)}, u32[]{:S(2)}) collective-permute-start(bf16[288,384]{1,0:T(8,128)(2,1)S(1)} %broadcast_select_fusion), channel_id=1, source_target_pairs={{1,2},{3,4},{5,6},{7,8},{9,10},{11,12},{13,14},{15,16},{17,18},{19... | collective-permute-start | bytes 663560 | tf_op jit(solution)/shard_map/ppermute | solution.py:335
  72.9 2.4 %all-to-all-done.1.parts = bf16[8,24,384]{2,1,0:T(8,128)(2,1)S(1)} async-done(((bf16[8,24,384]{2,1,0:T(8,128)(2,1)}), bf16[8,24,384]{2,1,0:T(8,128)(2,1)S(1)}, u32[]{:S(2)}, u32[]{:S(2)}) %all-to-all-start.1) | async-done | bytes 147488 | tf_op jit(solution)/shard_map/all_to_all | solution.py:48
  75.3 0.9 gather.1
  76.2 3.9 %all-to-all-start.2 = ((bf16[32,24,384]{2,1,0:T(8,128)(2,1)}), bf16[32,24,384]{2,1,0:T(8,128)(2,1)S(1)}, u32[]{:S(2)}, u32[]{:S(2)}) async-start(bf16[32,24,384]{2,1,0:T(8,128)(2,1)} %gather.1), calls=%async_computation.2 | async-start | bytes 1179648 | tf_op jit(solution)/shard_map/all_to_all | solution.py:48
  80.1 0.0 copy-start.7
  80.1 0.0 collective-permute-done.3.near
  80.1 0.0 collective-permute-done.5.far
  80.1 1.0 grad_input.1
  81.1 12.7 %all-to-all-done.2 = bf16[32,24,384]{2,1,0:T(8,128)(2,1)S(1)} async-done(((bf16[32,24,384]{2,1,0:T(8,128)(2,1)}), bf16[32,24,384]{2,1,0:T(8,128)(2,1)S(1)}, u32[]{:S(2)}, u32[]{:S(2)}) %all-to-all-start.2) | async-done | bytes 589856 | tf_op jit(solution)/shard_map/all_to_all | solution.py:48
  93.8 6.1 %collective-permute-start.6 = (bf16[768,384]{1,0:T(8,128)(2,1)S(1)}, bf16[768,384]{1,0:T(8,128)(2,1)S(1)}, u32[]{:S(2)}, u32[]{:S(2)}) collective-permute-start(bf16[768,384]{1,0:T(8,128)(2,1)S(1)} %bitcast.18), channel_id=1, source_target_pairs={{0,64},{64,0},{1,65},{65,1},{2,66},{66,2},{3,67},{67,3},{4,68},{68... | collective-permute-start | bytes 1769480 | tf_op jit(solution)/shard_map/ppermute | solution.py:343
  99.9 1.6 %collective-permute-done.6.other = bf16[768,384]{1,0:T(8,128)(2,1)S(1)} collective-permute-done((bf16[768,384]{1,0:T(8,128)(2,1)S(1)}, bf16[768,384]{1,0:T(8,128)(2,1)S(1)}, u32[]{:S(2)}, u32[]{:S(2)}) %collective-permute-start.6) | collective-permute-done | bytes 589856 | tf_op jit(solution)/shard_map/ppermute | solution.py:343
  101.6 1.8 %outputs.1 = (f32[384,1152]{1,0:T(8,128)}, f32[384,384]{1,0:T(8,128)}, f32[384]{0:T(512)}) custom-call(s32[1]{0:T(128)} %bitcast.core, bf16[768,384]{1,0:T(8,128)(2,1)S(1)} %bitcast.19, bf16[768,384]{1,0:T(8,128)(2,1)S(1)} %collective-permute-done.6.other, bf16[384,1152]{1,0:T(8,128)(2,1)S(1)} %copy-done.1, f32[384]{0:T(512)S(1)} %copy-done.7), custom_call_target="tpu_custom_call" | custom-call | flops 100000000 | bytes 4000000 | tf_op jit(solution)/shard_map/outputs/pallas_call | solution.py:345
  (14 shorter events, 0.1 us)
Async XLA Ops:
  0.6 19.0 %collective-permute-start.1 = (bf16[288,384]{1,0:T(8,128)(2,1)}, bf16[288,384]{1,0:T(8,128)(2,1)S(1)}, u32[]{:S(2)}, u32[]{:S(2)}) collective-permute-start(bf16[288,384]{1,0:T(8,128)(2,1)} %bitcast.20), channel_id=1, source_target_pairs={{1,2},{3,4},{5,6},{7,8},{9,10},{11,12},{13,14},{15,16},{17,18},{19... | collective-permute-start | bytes 663560 | tf_op jit(solution)/shard_map/ppermute | solution.py:35
  1.3 18.3 %collective-permute-start = (bf16[288,384]{1,0:T(8,128)(2,1)}, bf16[288,384]{1,0:T(8,128)(2,1)S(1)}, u32[]{:S(2)}, u32[]{:S(2)}) collective-permute-start(bf16[288,384]{1,0:T(8,128)(2,1)} %bitcast.21), channel_id=1, source_target_pairs={{0,1},{2,3},{4,5},{6,7},{8,9},{10,11},{12,13},{14,15},{16,17},{18,... | collective-permute-start | bytes 663560 | tf_op jit(solution)/shard_map/ppermute | solution.py:35
  12.2 1.2 %copy-start = (bf16[384,1152]{1,0:T(8,128)(2,1)S(1)}, bf16[384,1152]{1,0:T(8,128)(2,1)}, u32[]{:S(2)}) copy-start(bf16[384,1152]{1,0:T(8,128)(2,1)} %wqkv.5) | copy-start | bytes 2654212
  13.4 1.0 copy-start.2
  14.4 0.9 copy-start.3
  15.3 0.9 copy-start.5
  16.2 0.7 copy-start.8
  16.9 2.8 %copy-start.1 = (bf16[384,1152]{1,0:T(8,128)(2,1)S(1)}, bf16[384,1152]{1,0:T(8,128)(2,1)}, u32[]{:S(2)}) copy-start(bf16[384,1152]{1,0:T(8,128)(2,1)} %wqkv.5) | copy-start | bytes 2654212
  26.6 5.0 %collective-permute-start.2 = (bf16[768,384]{1,0:T(8,128)(2,1)S(1)}, bf16[768,384]{1,0:T(8,128)(2,1)S(1)}, u32[]{:S(2)}, u32[]{:S(2)}) collective-permute-start(bf16[768,384]{1,0:T(8,128)(2,1)S(1)} %get-tuple-element.39), channel_id=1, source_target_pairs={{0,64},{64,0},{1,65},{65,1},{2,66},{66,2},{3,67},{67,3},{4,68},{68... | collective-permute-start | bytes 1769480 | tf_op jit(solution)/shard_map/ppermute | solution.py:314
  32.5 28.0 %all-to-all-start = ((bf16[32,24,384]{2,1,0:T(8,128)(2,1)}), bf16[32,24,384]{2,1,0:T(8,128)(2,1)S(1)}, u32[]{:S(2)}, u32[]{:S(2)}) async-start(bf16[32,24,384]{2,1,0:T(8,128)(2,1)} %bitcast.9), calls=%async_computation | async-start | bytes 1179648 | tf_op jit(solution)/shard_map/all_to_all | solution.py:48
  46.5 23.4 %collective-permute-start.4 = (bf16[288,384]{1,0:T(8,128)(2,1)S(1)}, bf16[288,384]{1,0:T(8,128)(2,1)S(1)}, u32[]{:S(2)}, u32[]{:S(2)}) collective-permute-start(bf16[288,384]{1,0:T(8,128)(2,1)S(1)} %get-tuple-element.46), channel_id=1, source_target_pairs={{31,0},{32,63},{95,64},{96,127},{159,128},{160,191},{223,192},{224... | collective-permute-start | bytes 663560 | tf_op jit(solution)/shard_map/ppermute | solution.py:328
  61.3 14.0 %all-to-all-start.1 = ((bf16[8,24,384]{2,1,0:T(8,128)(2,1)}), bf16[8,24,384]{2,1,0:T(8,128)(2,1)S(1)}, u32[]{:S(2)}, u32[]{:S(2)}) async-start(bf16[8,24,384]{2,1,0:T(8,128)(2,1)} %broadcast_in_dim.29), calls=%async_computation.1 | async-start | bytes 294912 | tf_op jit(solution)/shard_map/all_to_all | solution.py:48
  66.4 13.7 %copy-start.4 = (bf16[1,288,384]{2,1,0:T(8,128)(2,1)S(1)}, bf16[1,288,384]{2,1,0:T(8,128)(2,1)}, u32[]{:S(2)}) copy-start(bf16[1,288,384]{2,1,0:T(8,128)(2,1)} %param.7) | copy-start | bytes 663556
  66.4 13.7 %copy-start.6 = (bf16[1,288,384]{2,1,0:T(8,128)(2,1)S(1)}, bf16[1,288,384]{2,1,0:T(8,128)(2,1)}, u32[]{:S(2)}) copy-start(bf16[1,288,384]{2,1,0:T(8,128)(2,1)} %param.8) | copy-start | bytes 663556
  66.4 13.7 %collective-permute-start.3 = (bf16[288,384]{1,0:T(8,128)(2,1)S(1)}, bf16[288,384]{1,0:T(8,128)(2,1)S(1)}, u32[]{:S(2)}, u32[]{:S(2)}) collective-permute-start(bf16[288,384]{1,0:T(8,128)(2,1)S(1)} %get-tuple-element.45), channel_id=1, source_target_pairs={{0,1},{2,3},{4,5},{6,7},{8,9},{10,11},{12,13},{14,15},{16,17},{18,... | collective-permute-start | bytes 663560 | tf_op jit(solution)/shard_map/ppermute | solution.py:35
  70.0 10.2 %collective-permute-start.5 = (bf16[288,384]{1,0:T(8,128)(2,1)S(1)}, bf16[288,384]{1,0:T(8,128)(2,1)S(1)}, u32[]{:S(2)}, u32[]{:S(2)}) collective-permute-start(bf16[288,384]{1,0:T(8,128)(2,1)S(1)} %broadcast_select_fusion), channel_id=1, source_target_pairs={{1,2},{3,4},{5,6},{7,8},{9,10},{11,12},{13,14},{15,16},{17,18},{19... | collective-permute-start | bytes 663560 | tf_op jit(solution)/shard_map/ppermute | solution.py:335
  76.2 17.6 %all-to-all-start.2 = ((bf16[32,24,384]{2,1,0:T(8,128)(2,1)}), bf16[32,24,384]{2,1,0:T(8,128)(2,1)S(1)}, u32[]{:S(2)}, u32[]{:S(2)}) async-start(bf16[32,24,384]{2,1,0:T(8,128)(2,1)} %gather.1), calls=%async_computation.2 | async-start | bytes 1179648 | tf_op jit(solution)/shard_map/all_to_all | solution.py:48
  80.1 21.5 %copy-start.7 = (f32[384]{0:T(512)S(1)}, f32[384]{0:T(512)}, u32[]{:S(2)}) copy-start(f32[384]{0:T(512)} %gain.1) | copy-start | bytes 4612
  93.8 7.7 %collective-permute-start.6 = (bf16[768,384]{1,0:T(8,128)(2,1)S(1)}, bf16[768,384]{1,0:T(8,128)(2,1)S(1)}, u32[]{:S(2)}, u32[]{:S(2)}) collective-permute-start(bf16[768,384]{1,0:T(8,128)(2,1)S(1)} %bitcast.18), channel_id=1, source_target_pairs={{0,64},{64,0},{1,65},{65,1},{2,66},{66,2},{3,67},{67,3},{4,68},{68... | collective-permute-start | bytes 1769480 | tf_op jit(solution)/shard_map/ppermute | solution.py:343

commit v7 on v6

--- a/solution.py
+++ b/solution.py
@@ -329,6 +329,7 @@
     plane, ring = len(PLANES[0]), len(RINGS[0])
     parts = half.reshape(plane, 2 * WIDTH // plane, WIDTH)
     part = total(exchanged(parts, PLANES))
+    moved, back_near = lax.optimization_barrier((moved, back_near))
     at_end = jnp.logical_or(position == 0, position == count - 1)
     pairs = [(i, i + 1) for i in range(1, count - 1, 2) if i != middle - 1]
     pairs = pairs + [(b, a) for a, b in pairs] + [(0, middle), (count - 1, middle - 1)]

time: 104 us -> 107 us (1.029)
  the two profiles are of different devices: /device:TPU:1 before, /device:TPU:41 now
where the time goes in v7:
time: 107 us; the launch traced here: 106 us
  starting transfers between devices  62.6 us (59%)
  waiting for transfers between devices  18 us (17%)
  Pallas kernels  14.9 us (14%)
  local copies, waits for them, and re-layouts  6.94 us (6%)
  other arithmetic  2.36 us (2%)
    all_to_all x3, starting transfers between devices, exchanged(): lax.all_to_all(parts, AXES, 0, 0, axis_index_groups=groups, tiled=True)  19.1 us
    ppermute x3, starting transfers between devices, swapped(): return lax.ppermute(block, SPACE, pairs + [(b, a) for a, b in pairs])  18.9 us
    all_to_all x3, waiting for transfers between devices, exchanged(): lax.all_to_all(parts, AXES, 0, 0, axis_index_groups=groups, tiled=True)  16.4 us
    ppermute x1, starting transfers between devices, shards(): other = lax.ppermute(half, 'c', pair)  13.9 us
    pallas_call x1, Pallas kernels, shards(): local(attention_kernel, 'attention', (half_rows, ((2 * WIDTH, KEYS), b16)...  6.97 us
    ppermute x1, starting transfers between devices, shards(): lax.ppermute(back_far, SPACE, [(middle - 1, 0), (middle, count - 1)])  6.42 us
    unnamed x19, local copies, waits for them, and re-layouts  5.36 us
    ppermute x1, starting transfers between devices, shards(): arrived = lax.ppermute(send, 'c', pair)  2.86 us
  transfers between devices with their start and end apart: 10, of which 4 were waited for; matrix products, arithmetic and copies ran while one was open for 3% of the time, Pallas kernels for 6%

profile of v7, /device:TPU:41, one launch (start us, length us, event | category | flops | bytes accessed | tf_op | source)
XLA Modules:
  0.0 105.8 jit_solution(7247098974955128940)
XLA Ops:
  0.6 13.3 %collective-permute-start.1 = (bf16[288,384]{1,0:T(8,128)(2,1)}, bf16[288,384]{1,0:T(8,128)(2,1)S(1)}, u32[]{:S(2)}, u32[]{:S(2)}) collective-permute-start(bf16[288,384]{1,0:T(8,128)(2,1)} %bitcast.20), channel_id=1, source_target_pairs={{1,2},{3,4},{5,6},{7,8},{9,10},{11,12},{13,14},{15,16},{17,18},{19... | collective-permute-start | bytes 663560 | tf_op jit(solution)/shard_map/ppermute | solution.py:35
  13.9 1.9 %collective-permute-start = (bf16[288,384]{1,0:T(8,128)(2,1)}, bf16[288,384]{1,0:T(8,128)(2,1)S(1)}, u32[]{:S(2)}, u32[]{:S(2)}) collective-permute-start(bf16[288,384]{1,0:T(8,128)(2,1)} %bitcast.21), channel_id=1, source_target_pairs={{0,1},{2,3},{4,5},{6,7},{8,9},{10,11},{12,13},{14,15},{16,17},{18,... | collective-permute-start | bytes 663560 | tf_op jit(solution)/shard_map/ppermute | solution.py:35
  15.9 0.7 broadcast_compare_fusion
  16.6 0.7 copy.16
  17.3 0.7 broadcast_in_dim.25.gain
  18.0 0.1 add_multiply_fusion
  18.1 0.1 iota_add_fusion
  18.1 0.1 add.54
  18.2 0.2 and_reduce_fusion
  18.4 0.1 copy.11
  18.5 0.1 fusion.fk
  18.6 0.0 copy-start
  18.6 1.2 %copy-done = bf16[384,1152]{1,0:T(8,128)(2,1)S(1)} copy-done((bf16[384,1152]{1,0:T(8,128)(2,1)S(1)}, bf16[384,1152]{1,0:T(8,128)(2,1)}, u32[]{:S(2)}) %copy-start) | copy-done | bytes 884760
  19.8 1.0 copy-done.2
  20.8 0.9 copy-done.3
  21.7 0.9 copy-done.5
  22.6 0.7 copy-done.8
  23.3 2.5 %prepare.1 = (bf16[288,384]{1,0:T(8,128)(2,1)S(1)}, bf16[288,768]{1,0:T(8,128)(2,1)S(1)}, bf16[288,384]{1,0:T(8,128)(2,1)S(1)}, bf16[384,288]{1,0:T(8,128)(2,1)S...) custom-call(s32[9]{0:T(128)S(1)} %bitcast.26, bf16[288,384]{1,0:T(8,128)(2,1)S(1)} %bitcast.22, ...), custom_call_target="tpu_custom_call" | custom-call | flops 400000000 | bytes 1000000 | tf_op jit(solution)/shard_map/prepare/pallas_call | solution.py:267
  25.8 0.2 fusion.1.fq
  26.0 0.0 collective-permute-done.1.far
  26.0 0.0 collective-permute-done.near
  26.0 7.0 %attention.1 = (bf16[768,384]{1,0:T(8,128)(2,1)S(1)}, bf16[768,896]{1,0:T(8,128)(2,1)S(1)}, bf16[288,384]{1,0:T(8,128)(2,1)S(1)}, bf16[384,896]{1,0:T(8,128)(2,1)S(1)}, bf16[384,288]{1,0:T(8,128)(2,1)S(1)}) custom-call(s32[1]{0:T(128)} %bitcast.core, bf16[288,384]{1,0:T(8,128)(2,1)S(1)} %collective-permute-done.near, ...), custom_call_target="tpu_custom_call" | custom-call | flops 3000000000 | bytes 4000000 | tf_op jit(solution)/shard_map/attention/pallas_call | solution.py:295
  33.0 2.9 %collective-permute-start.2 = (bf16[768,384]{1,0:T(8,128)(2,1)S(1)}, bf16[768,384]{1,0:T(8,128)(2,1)S(1)}, u32[]{:S(2)}, u32[]{:S(2)}) collective-permute-start(bf16[768,384]{1,0:T(8,128)(2,1)S(1)} %get-tuple-element.41), channel_id=1, source_target_pairs={{0,64},{64,0},{1,65},{65,1},{2,66},{66,2},{3,67},{67,3},{4,68},{68... | collective-permute-start | bytes 1769480 | tf_op jit(solution)/shard_map/ppermute | solution.py:314
  35.9 1.8 %back.1 = (bf16[768,384]{1,0:T(8,128)(2,1)S(1)}, f32[288,384]{1,0:T(8,128)S(1)}, bf16[288,384]{1,0:T(8,128)(2,1)S(1)}, bf16[288,384]{1,0:T(8,128)(2,1)S(1)}) custom-call(s32[1]{0:T(128)} %bitcast.core, bf16[768,896]{1,0:T(8,128)(2,1)S(1)} %get-tuple-element.36.dt, bf16[288,384]{1,0:T(8,128)(2,1)S(1)} %get-tuple-element.37.dq, ...), custom_call_target="tpu_custom_call" | custom-call | flops 1000000000 | bytes 1000000 | tf_op jit(solution)/shard_map/back/pallas_call | solution.py:315
  37.7 0.0 collective-permute-done.2
  37.7 1.0 add_convert_fusion
  38.7 6.5 %all-to-all-start = ((bf16[32,24,384]{2,1,0:T(8,128)(2,1)}), bf16[32,24,384]{2,1,0:T(8,128)(2,1)S(1)}, u32[]{:S(2)}, u32[]{:S(2)}) async-start(bf16[32,24,384]{2,1,0:T(8,128)(2,1)} %bitcast.9), calls=%async_computation | async-start | bytes 1179648 | tf_op jit(solution)/shard_map/all_to_all | solution.py:48
  45.2 3.6 %collective-permute-start.4 = (bf16[288,384]{1,0:T(8,128)(2,1)S(1)}, bf16[288,384]{1,0:T(8,128)(2,1)S(1)}, u32[]{:S(2)}, u32[]{:S(2)}) collective-permute-start(bf16[288,384]{1,0:T(8,128)(2,1)S(1)} %get-tuple-element.48), channel_id=1, source_target_pairs={{0,1},{2,3},{4,5},{6,7},{8,9},{10,11},{12,13},{14,15},{16,17},{18,... | collective-permute-start | bytes 663560 | tf_op jit(solution)/shard_map/ppermute | solution.py:35
  48.8 6.4 %collective-permute-start.3 = (bf16[288,384]{1,0:T(8,128)(2,1)S(1)}, bf16[288,384]{1,0:T(8,128)(2,1)S(1)}, u32[]{:S(2)}, u32[]{:S(2)}) collective-permute-start(bf16[288,384]{1,0:T(8,128)(2,1)S(1)} %get-tuple-element.47), channel_id=1, source_target_pairs={{31,0},{32,63},{95,64},{96,127},{159,128},{160,191},{223,192},{224... | collective-permute-start | bytes 663560 | tf_op jit(solution)/shard_map/ppermute | solution.py:328
  55.3 0.4 all-to-all-done
  55.7 0.1 reduce_sum.12
  55.8 0.7 broadcast_in_dim.29
  56.5 5.1 %all-to-all-start.1 = ((bf16[8,24,384]{2,1,0:T(8,128)(2,1)}), bf16[8,24,384]{2,1,0:T(8,128)(2,1)S(1)}, u32[]{:S(2)}, u32[]{:S(2)}) async-start(bf16[8,24,384]{2,1,0:T(8,128)(2,1)} %broadcast_in_dim.29), calls=%async_computation.1 | async-start | bytes 294912 | tf_op jit(solution)/shard_map/all_to_all | solution.py:48
  61.6 0.0 copy-start.6
  61.6 0.0 collective-permute-done.4.near
  61.6 0.0 collective-permute-done.3
  61.7 1.4 %collective-permute-start.5 = (bf16[288,384]{1,0:T(8,128)(2,1)S(1)}, bf16[288,384]{1,0:T(8,128)(2,1)S(1)}, u32[]{:S(2)}, u32[]{:S(2)}) collective-permute-start(bf16[288,384]{1,0:T(8,128)(2,1)S(1)} %broadcast_select_fusion), channel_id=1, source_target_pairs={{1,2},{3,4},{5,6},{7,8},{9,10},{11,12},{13,14},{15,16},{17,18},{19... | collective-permute-start | bytes 663560 | tf_op jit(solution)/shard_map/ppermute | solution.py:336
  63.1 6.7 %all-to-all-done.1.parts = bf16[8,24,384]{2,1,0:T(8,128)(2,1)S(1)} async-done(((bf16[8,24,384]{2,1,0:T(8,128)(2,1)}), bf16[8,24,384]{2,1,0:T(8,128)(2,1)S(1)}, u32[]{:S(2)}, u32[]{:S(2)}) %all-to-all-start.1) | async-done | bytes 147488 | tf_op jit(solution)/shard_map/all_to_all | solution.py:48
  69.8 0.9 gather.1
  70.7 7.4 %all-to-all-start.2 = ((bf16[32,24,384]{2,1,0:T(8,128)(2,1)}), bf16[32,24,384]{2,1,0:T(8,128)(2,1)S(1)}, u32[]{:S(2)}, u32[]{:S(2)}) async-start(bf16[32,24,384]{2,1,0:T(8,128)(2,1)} %gather.1), calls=%async_computation.2 | async-start | bytes 1179648 | tf_op jit(solution)/shard_map/all_to_all | solution.py:48
  78.2 0.0 copy-start.7
  78.2 0.0 collective-permute-done.5.far
  78.2 0.0 copy-done.4
  78.2 1.0 grad_input.1
  79.2 9.2 %all-to-all-done.2 = bf16[32,24,384]{2,1,0:T(8,128)(2,1)S(1)} async-done(((bf16[32,24,384]{2,1,0:T(8,128)(2,1)}), bf16[32,24,384]{2,1,0:T(8,128)(2,1)S(1)}, u32[]{:S(2)}, u32[]{:S(2)}) %all-to-all-start.2) | async-done | bytes 589856 | tf_op jit(solution)/shard_map/all_to_all | solution.py:48
  88.4 13.9 %collective-permute-start.6 = (bf16[768,384]{1,0:T(8,128)(2,1)S(1)}, bf16[768,384]{1,0:T(8,128)(2,1)S(1)}, u32[]{:S(2)}, u32[]{:S(2)}) collective-permute-start(bf16[768,384]{1,0:T(8,128)(2,1)S(1)} %bitcast.18), channel_id=1, source_target_pairs={{0,64},{64,0},{1,65},{65,1},{2,66},{66,2},{3,67},{67,3},{4,68},{68... | collective-permute-start | bytes 1769480 | tf_op jit(solution)/shard_map/ppermute | solution.py:344
  102.4 1.6 %collective-permute-done.6.other = bf16[768,384]{1,0:T(8,128)(2,1)S(1)} collective-permute-done((bf16[768,384]{1,0:T(8,128)(2,1)S(1)}, bf16[768,384]{1,0:T(8,128)(2,1)S(1)}, u32[]{:S(2)}, u32[]{:S(2)}) %collective-permute-start.6) | collective-permute-done | bytes 589856 | tf_op jit(solution)/shard_map/ppermute | solution.py:344
  104.0 1.8 %outputs.1 = (f32[384,1152]{1,0:T(8,128)}, f32[384,384]{1,0:T(8,128)}, f32[384]{0:T(512)}) custom-call(s32[1]{0:T(128)} %bitcast.core, bf16[768,384]{1,0:T(8,128)(2,1)S(1)} %bitcast.19, bf16[768,384]{1,0:T(8,128)(2,1)S(1)} %collective-permute-done.6.other, bf16[384,1152]{1,0:T(8,128)(2,1)S(1)} %copy-done.1, f32[384]{0:T(512)S(1)} %copy-done.7), custom_call_target="tpu_custom_call" | custom-call | flops 100000000 | bytes 4000000 | tf_op jit(solution)/shard_map/outputs/pallas_call | solution.py:346
  (14 shorter events, 0.1 us)
Async XLA Ops:
  0.6 25.4 %collective-permute-start.1 = (bf16[288,384]{1,0:T(8,128)(2,1)}, bf16[288,384]{1,0:T(8,128)(2,1)S(1)}, u32[]{:S(2)}, u32[]{:S(2)}) collective-permute-start(bf16[288,384]{1,0:T(8,128)(2,1)} %bitcast.20), channel_id=1, source_target_pairs={{1,2},{3,4},{5,6},{7,8},{9,10},{11,12},{13,14},{15,16},{17,18},{19... | collective-permute-start | bytes 663560 | tf_op jit(solution)/shard_map/ppermute | solution.py:35
  13.9 12.1 %collective-permute-start = (bf16[288,384]{1,0:T(8,128)(2,1)}, bf16[288,384]{1,0:T(8,128)(2,1)S(1)}, u32[]{:S(2)}, u32[]{:S(2)}) collective-permute-start(bf16[288,384]{1,0:T(8,128)(2,1)} %bitcast.21), channel_id=1, source_target_pairs={{0,1},{2,3},{4,5},{6,7},{8,9},{10,11},{12,13},{14,15},{16,17},{18,... | collective-permute-start | bytes 663560 | tf_op jit(solution)/shard_map/ppermute | solution.py:35
  18.6 1.2 %copy-start = (bf16[384,1152]{1,0:T(8,128)(2,1)S(1)}, bf16[384,1152]{1,0:T(8,128)(2,1)}, u32[]{:S(2)}) copy-start(bf16[384,1152]{1,0:T(8,128)(2,1)} %wqkv.5) | copy-start | bytes 2654212
  19.8 1.0 copy-start.2
  20.7 0.9 copy-start.3
  21.7 0.9 copy-start.5
  22.6 0.7 copy-start.8
  23.3 2.8 %copy-start.1 = (bf16[384,1152]{1,0:T(8,128)(2,1)S(1)}, bf16[384,1152]{1,0:T(8,128)(2,1)}, u32[]{:S(2)}) copy-start(bf16[384,1152]{1,0:T(8,128)(2,1)} %wqkv.5) | copy-start | bytes 2654212
  33.0 4.7 %collective-permute-start.2 = (bf16[768,384]{1,0:T(8,128)(2,1)S(1)}, bf16[768,384]{1,0:T(8,128)(2,1)S(1)}, u32[]{:S(2)}, u32[]{:S(2)}) collective-permute-start(bf16[768,384]{1,0:T(8,128)(2,1)S(1)} %get-tuple-element.41), channel_id=1, source_target_pairs={{0,64},{64,0},{1,65},{65,1},{2,66},{66,2},{3,67},{67,3},{4,68},{68... | collective-permute-start | bytes 1769480 | tf_op jit(solution)/shard_map/ppermute | solution.py:314
  38.7 17.0 %all-to-all-start = ((bf16[32,24,384]{2,1,0:T(8,128)(2,1)}), bf16[32,24,384]{2,1,0:T(8,128)(2,1)S(1)}, u32[]{:S(2)}, u32[]{:S(2)}) async-start(bf16[32,24,384]{2,1,0:T(8,128)(2,1)} %bitcast.9), calls=%async_computation | async-start | bytes 1179648 | tf_op jit(solution)/shard_map/all_to_all | solution.py:48
  45.2 16.4 %collective-permute-start.4 = (bf16[288,384]{1,0:T(8,128)(2,1)S(1)}, bf16[288,384]{1,0:T(8,128)(2,1)S(1)}, u32[]{:S(2)}, u32[]{:S(2)}) collective-permute-start(bf16[288,384]{1,0:T(8,128)(2,1)S(1)} %get-tuple-element.48), channel_id=1, source_target_pairs={{0,1},{2,3},{4,5},{6,7},{8,9},{10,11},{12,13},{14,15},{16,17},{18,... | collective-permute-start | bytes 663560 | tf_op jit(solution)/shard_map/ppermute | solution.py:35
  48.8 12.8 %collective-permute-start.3 = (bf16[288,384]{1,0:T(8,128)(2,1)S(1)}, bf16[288,384]{1,0:T(8,128)(2,1)S(1)}, u32[]{:S(2)}, u32[]{:S(2)}) collective-permute-start(bf16[288,384]{1,0:T(8,128)(2,1)S(1)} %get-tuple-element.47), channel_id=1, source_target_pairs={{31,0},{32,63},{95,64},{96,127},{159,128},{160,191},{223,192},{224... | collective-permute-start | bytes 663560 | tf_op jit(solution)/shard_map/ppermute | solution.py:328
  56.5 13.4 %all-to-all-start.1 = ((bf16[8,24,384]{2,1,0:T(8,128)(2,1)}), bf16[8,24,384]{2,1,0:T(8,128)(2,1)S(1)}, u32[]{:S(2)}, u32[]{:S(2)}) async-start(bf16[8,24,384]{2,1,0:T(8,128)(2,1)} %broadcast_in_dim.29), calls=%async_computation.1 | async-start | bytes 294912 | tf_op jit(solution)/shard_map/all_to_all | solution.py:48
  61.6 16.6 %copy-start.4 = (bf16[1,288,384]{2,1,0:T(8,128)(2,1)S(1)}, bf16[1,288,384]{2,1,0:T(8,128)(2,1)}, u32[]{:S(2)}) copy-start(bf16[1,288,384]{2,1,0:T(8,128)(2,1)} %param.7) | copy-start | bytes 663556
  61.6 16.6 %copy-start.6 = (bf16[1,288,384]{2,1,0:T(8,128)(2,1)S(1)}, bf16[1,288,384]{2,1,0:T(8,128)(2,1)}, u32[]{:S(2)}) copy-start(bf16[1,288,384]{2,1,0:T(8,128)(2,1)} %param.8) | copy-start | bytes 663556
  61.7 16.5 %collective-permute-start.5 = (bf16[288,384]{1,0:T(8,128)(2,1)S(1)}, bf16[288,384]{1,0:T(8,128)(2,1)S(1)}, u32[]{:S(2)}, u32[]{:S(2)}) collective-permute-start(bf16[288,384]{1,0:T(8,128)(2,1)S(1)} %broadcast_select_fusion), channel_id=1, source_target_pairs={{1,2},{3,4},{5,6},{7,8},{9,10},{11,12},{13,14},{15,16},{17,18},{19... | collective-permute-start | bytes 663560 | tf_op jit(solution)/shard_map/ppermute | solution.py:336
  70.7 17.7 %all-to-all-start.2 = ((bf16[32,24,384]{2,1,0:T(8,128)(2,1)}), bf16[32,24,384]{2,1,0:T(8,128)(2,1)S(1)}, u32[]{:S(2)}, u32[]{:S(2)}) async-start(bf16[32,24,384]{2,1,0:T(8,128)(2,1)} %gather.1), calls=%async_computation.2 | async-start | bytes 1179648 | tf_op jit(solution)/shard_map/all_to_all | solution.py:48
  78.2 25.8 %copy-start.7 = (f32[384]{0:T(512)S(1)}, f32[384]{0:T(512)}, u32[]{:S(2)}) copy-start(f32[384]{0:T(512)} %gain.1) | copy-start | bytes 4612
  88.4 15.6 %collective-permute-start.6 = (bf16[768,384]{1,0:T(8,128)(2,1)S(1)}, bf16[768,384]{1,0:T(8,128)(2,1)S(1)}, u32[]{:S(2)}, u32[]{:S(2)}) collective-permute-start(bf16[768,384]{1,0:T(8,128)(2,1)S(1)} %bitcast.18), channel_id=1, source_target_pairs={{0,64},{64,0},{1,65},{65,1},{2,66},{66,2},{3,67},{67,3},{4,68},{68... | collective-permute-start | bytes 1769480 | tf_op jit(solution)/shard_map/ppermute | solution.py:344

commit v8 on v6

--- a/solution.py
+++ b/solution.py
@@ -131,7 +131,6 @@
             share.append(1.0 / jnp.sum(block, axis=1, keepdims=True))
             expo[pair, rows] = block.astype(jnp.bfloat16)
         shares.append(jnp.concatenate(share, axis=0))
-    for pair in pairs:
         results.append(dot(expo[pair], table[:, values[pair]]) * shares[pair])
         grad = jnp.where(keep, twice(g[:, lanes[pair]]) * shares[pair], zero)
         grads.append(grad.astype(jnp.bfloat16))

time: 104 us -> 104 us (level)
  no operation moved by 1% of the time
where the time goes in v8:
time: 104 us; the launch traced here: 103 us
  starting transfers between devices  48.8 us (47%)
  waiting for transfers between devices  29.4 us (28%)
  Pallas kernels  14.9 us (14%)
  local copies, waits for them, and re-layouts  6.94 us (7%)
  other arithmetic  2.36 us (2%)
    all_to_all x3, waiting for transfers between devices, exchanged(): lax.all_to_all(parts, AXES, 0, 0, axis_index_groups=groups, tiled=True)  27.8 us
    all_to_all x3, starting transfers between devices, exchanged(): lax.all_to_all(parts, AXES, 0, 0, axis_index_groups=groups, tiled=True)  23 us
    ppermute x3, starting transfers between devices, swapped(): return lax.ppermute(block, SPACE, pairs + [(b, a) for a, b in pairs])  12.3 us
    pallas_call x1, Pallas kernels, shards(): local(attention_kernel, 'attention', (half_rows, ((2 * WIDTH, KEYS), b16)...  6.96 us
    ppermute x1, starting transfers between devices, shards(): other = lax.ppermute(half, 'c', pair)  6.13 us
    unnamed x19, local copies, waits for them, and re-layouts  5.36 us
    ppermute x1, starting transfers between devices, shards(): arrived = lax.ppermute(send, 'c', pair)  3.14 us
    ppermute x1, starting transfers between devices, shards(): back_far = lax.ppermute(jnp.where(at_end, moved, back_far), SPACE, pairs)  2.9 us
  transfers between devices with their start and end apart: 10, of which 4 were waited for; matrix products, arithmetic and copies ran while one was open for 4% of the time, Pallas kernels for 6%

profile of v8, /device:TPU:1, one launch (start us, length us, event | category | flops | bytes accessed | tf_op | source)
XLA Modules:
  0.0 103.4 jit_solution(7209250563385469033)
XLA Ops:
  0.6 0.7 collective-permute-start.1
  1.3 8.2 %collective-permute-start = (bf16[288,384]{1,0:T(8,128)(2,1)}, bf16[288,384]{1,0:T(8,128)(2,1)S(1)}, u32[]{:S(2)}, u32[]{:S(2)}) collective-permute-start(bf16[288,384]{1,0:T(8,128)(2,1)} %bitcast.21), channel_id=1, source_target_pairs={{0,1},{2,3},{4,5},{6,7},{8,9},{10,11},{12,13},{14,15},{16,17},{18,... | collective-permute-start | bytes 663560 | tf_op jit(solution)/shard_map/ppermute | solution.py:35
  9.5 0.7 broadcast_compare_fusion
  10.2 0.7 copy.16
  10.9 0.7 broadcast_in_dim.25.gain
  11.6 0.1 add_multiply_fusion
  11.7 0.1 iota_add_fusion
  11.7 0.1 add.54
  11.8 0.2 and_reduce_fusion
  12.0 0.1 copy.11
  12.2 0.1 fusion.fk
  12.2 0.0 copy-start
  12.2 1.2 %copy-done = bf16[384,1152]{1,0:T(8,128)(2,1)S(1)} copy-done((bf16[384,1152]{1,0:T(8,128)(2,1)S(1)}, bf16[384,1152]{1,0:T(8,128)(2,1)}, u32[]{:S(2)}) %copy-start) | copy-done | bytes 884760
  13.4 1.0 copy-done.2
  14.4 0.9 copy-done.3
  15.3 0.9 copy-done.5
  16.2 0.7 copy-done.8
  16.9 2.5 %prepare.1 = (bf16[288,384]{1,0:T(8,128)(2,1)S(1)}, bf16[288,768]{1,0:T(8,128)(2,1)S(1)}, bf16[288,384]{1,0:T(8,128)(2,1)S(1)}, bf16[384,288]{1,0:T(8,128)(2,1)S...) custom-call(s32[9]{0:T(128)S(1)} %bitcast.26, bf16[288,384]{1,0:T(8,128)(2,1)S(1)} %bitcast.22, ...), custom_call_target="tpu_custom_call" | custom-call | flops 400000000 | bytes 1000000 | tf_op jit(solution)/shard_map/prepare/pallas_call | solution.py:266
  19.4 0.2 fusion.1.fq
  19.6 0.0 collective-permute-done.1.far
  19.6 0.0 collective-permute-done.near
  19.6 0.0 copy-done.1
  19.6 7.0 %attention.1 = (bf16[768,384]{1,0:T(8,128)(2,1)S(1)}, bf16[768,896]{1,0:T(8,128)(2,1)S(1)}, bf16[288,384]{1,0:T(8,128)(2,1)S(1)}, bf16[384,896]{1,0:T(8,128)(2,1)S(1)}, bf16[384,288]{1,0:T(8,128)(2,1)S(1)}) custom-call(s32[1]{0:T(128)} %bitcast.core, bf16[288,384]{1,0:T(8,128)(2,1)S(1)} %collective-permute-done.near, ...), custom_call_target="tpu_custom_call" | custom-call | flops 3000000000 | bytes 4000000 | tf_op jit(solution)/shard_map/attention/pallas_call | solution.py:294
  26.6 3.1 %collective-permute-start.2 = (bf16[768,384]{1,0:T(8,128)(2,1)S(1)}, bf16[768,384]{1,0:T(8,128)(2,1)S(1)}, u32[]{:S(2)}, u32[]{:S(2)}) collective-permute-start(bf16[768,384]{1,0:T(8,128)(2,1)S(1)} %get-tuple-element.39), channel_id=1, source_target_pairs={{0,64},{64,0},{1,65},{65,1},{2,66},{66,2},{3,67},{67,3},{4,68},{68... | collective-permute-start | bytes 1769480 | tf_op jit(solution)/shard_map/ppermute | solution.py:313
  29.8 1.8 %back.1 = (bf16[768,384]{1,0:T(8,128)(2,1)S(1)}, f32[288,384]{1,0:T(8,128)S(1)}, bf16[288,384]{1,0:T(8,128)(2,1)S(1)}, bf16[288,384]{1,0:T(8,128)(2,1)S(1)}) custom-call(s32[1]{0:T(128)} %bitcast.core, bf16[768,896]{1,0:T(8,128)(2,1)S(1)} %get-tuple-element.34.dt, bf16[288,384]{1,0:T(8,128)(2,1)S(1)} %get-tuple-element.35.dq, ...), custom_call_target="tpu_custom_call" | custom-call | flops 1000000000 | bytes 1000000 | tf_op jit(solution)/shard_map/back/pallas_call | solution.py:314
  31.6 0.0 collective-permute-done.2
  31.6 1.0 add_convert_fusion
  32.5 14.0 %all-to-all-start = ((bf16[32,24,384]{2,1,0:T(8,128)(2,1)}), bf16[32,24,384]{2,1,0:T(8,128)(2,1)S(1)}, u32[]{:S(2)}, u32[]{:S(2)}) async-start(bf16[32,24,384]{2,1,0:T(8,128)(2,1)} %bitcast.9), calls=%async_computation | async-start | bytes 1179648 | tf_op jit(solution)/shard_map/all_to_all | solution.py:48
  46.5 1.3 %collective-permute-start.4 = (bf16[288,384]{1,0:T(8,128)(2,1)S(1)}, bf16[288,384]{1,0:T(8,128)(2,1)S(1)}, u32[]{:S(2)}, u32[]{:S(2)}) collective-permute-start(bf16[288,384]{1,0:T(8,128)(2,1)S(1)} %get-tuple-element.46), channel_id=1, source_target_pairs={{31,0},{32,63},{95,64},{96,127},{159,128},{160,191},{223,192},{224... | collective-permute-start | bytes 663560 | tf_op jit(solution)/shard_map/ppermute | solution.py:327
  47.8 12.7 %all-to-all-done = bf16[32,24,384]{2,1,0:T(8,128)(2,1)S(1)} async-done(((bf16[32,24,384]{2,1,0:T(8,128)(2,1)}), bf16[32,24,384]{2,1,0:T(8,128)(2,1)S(1)}, u32[]{:S(2)}, u32[]{:S(2)}) %all-to-all-start) | async-done | bytes 589856 | tf_op jit(solution)/shard_map/all_to_all | solution.py:48
  60.5 0.1 reduce_sum.12
  60.6 0.7 broadcast_in_dim.29
  61.3 5.1 %all-to-all-start.1 = ((bf16[8,24,384]{2,1,0:T(8,128)(2,1)}), bf16[8,24,384]{2,1,0:T(8,128)(2,1)S(1)}, u32[]{:S(2)}, u32[]{:S(2)}) async-start(bf16[8,24,384]{2,1,0:T(8,128)(2,1)} %broadcast_in_dim.29), calls=%async_computation.1 | async-start | bytes 294912 | tf_op jit(solution)/shard_map/all_to_all | solution.py:48
  66.4 0.0 copy-start.6
  66.4 3.5 %collective-permute-start.3 = (bf16[288,384]{1,0:T(8,128)(2,1)S(1)}, bf16[288,384]{1,0:T(8,128)(2,1)S(1)}, u32[]{:S(2)}, u32[]{:S(2)}) collective-permute-start(bf16[288,384]{1,0:T(8,128)(2,1)S(1)} %get-tuple-element.45), channel_id=1, source_target_pairs={{0,1},{2,3},{4,5},{6,7},{8,9},{10,11},{12,13},{14,15},{16,17},{18,... | collective-permute-start | bytes 663560 | tf_op jit(solution)/shard_map/ppermute | solution.py:35
  69.9 0.0 collective-permute-done.4
  70.0 2.9 %collective-permute-start.5 = (bf16[288,384]{1,0:T(8,128)(2,1)S(1)}, bf16[288,384]{1,0:T(8,128)(2,1)S(1)}, u32[]{:S(2)}, u32[]{:S(2)}) collective-permute-start(bf16[288,384]{1,0:T(8,128)(2,1)S(1)} %broadcast_select_fusion), channel_id=1, source_target_pairs={{1,2},{3,4},{5,6},{7,8},{9,10},{11,12},{13,14},{15,16},{17,18},{19... | collective-permute-start | bytes 663560 | tf_op jit(solution)/shard_map/ppermute | solution.py:334
  72.9 2.4 %all-to-all-done.1.parts = bf16[8,24,384]{2,1,0:T(8,128)(2,1)S(1)} async-done(((bf16[8,24,384]{2,1,0:T(8,128)(2,1)}), bf16[8,24,384]{2,1,0:T(8,128)(2,1)S(1)}, u32[]{:S(2)}, u32[]{:S(2)}) %all-to-all-start.1) | async-done | bytes 147488 | tf_op jit(solution)/shard_map/all_to_all | solution.py:48
  75.3 0.9 gather.1
  76.2 3.9 %all-to-all-start.2 = ((bf16[32,24,384]{2,1,0:T(8,128)(2,1)}), bf16[32,24,384]{2,1,0:T(8,128)(2,1)S(1)}, u32[]{:S(2)}, u32[]{:S(2)}) async-start(bf16[32,24,384]{2,1,0:T(8,128)(2,1)} %gather.1), calls=%async_computation.2 | async-start | bytes 1179648 | tf_op jit(solution)/shard_map/all_to_all | solution.py:48
  80.1 0.0 copy-start.7
  80.1 0.0 collective-permute-done.3.near
  80.1 0.0 collective-permute-done.5.far
  80.1 1.0 grad_input.1
  81.1 12.7 %all-to-all-done.2 = bf16[32,24,384]{2,1,0:T(8,128)(2,1)S(1)} async-done(((bf16[32,24,384]{2,1,0:T(8,128)(2,1)}), bf16[32,24,384]{2,1,0:T(8,128)(2,1)S(1)}, u32[]{:S(2)}, u32[]{:S(2)}) %all-to-all-start.2) | async-done | bytes 589856 | tf_op jit(solution)/shard_map/all_to_all | solution.py:48
  93.8 6.1 %collective-permute-start.6 = (bf16[768,384]{1,0:T(8,128)(2,1)S(1)}, bf16[768,384]{1,0:T(8,128)(2,1)S(1)}, u32[]{:S(2)}, u32[]{:S(2)}) collective-permute-start(bf16[768,384]{1,0:T(8,128)(2,1)S(1)} %bitcast.18), channel_id=1, source_target_pairs={{0,64},{64,0},{1,65},{65,1},{2,66},{66,2},{3,67},{67,3},{4,68},{68... | collective-permute-start | bytes 1769480 | tf_op jit(solution)/shard_map/ppermute | solution.py:342
  99.9 1.6 %collective-permute-done.6.other = bf16[768,384]{1,0:T(8,128)(2,1)S(1)} collective-permute-done((bf16[768,384]{1,0:T(8,128)(2,1)S(1)}, bf16[768,384]{1,0:T(8,128)(2,1)S(1)}, u32[]{:S(2)}, u32[]{:S(2)}) %collective-permute-start.6) | collective-permute-done | bytes 589856 | tf_op jit(solution)/shard_map/ppermute | solution.py:342
  101.6 1.8 %outputs.1 = (f32[384,1152]{1,0:T(8,128)}, f32[384,384]{1,0:T(8,128)}, f32[384]{0:T(512)}) custom-call(s32[1]{0:T(128)} %bitcast.core, bf16[768,384]{1,0:T(8,128)(2,1)S(1)} %bitcast.19, bf16[768,384]{1,0:T(8,128)(2,1)S(1)} %collective-permute-done.6.other, bf16[384,1152]{1,0:T(8,128)(2,1)S(1)} %copy-done.1, f32[384]{0:T(512)S(1)} %copy-done.7), custom_call_target="tpu_custom_call" | custom-call | flops 100000000 | bytes 4000000 | tf_op jit(solution)/shard_map/outputs/pallas_call | solution.py:344
  (14 shorter events, 0.1 us)
Async XLA Ops:
  0.6 19.0 %collective-permute-start.1 = (bf16[288,384]{1,0:T(8,128)(2,1)}, bf16[288,384]{1,0:T(8,128)(2,1)S(1)}, u32[]{:S(2)}, u32[]{:S(2)}) collective-permute-start(bf16[288,384]{1,0:T(8,128)(2,1)} %bitcast.20), channel_id=1, source_target_pairs={{1,2},{3,4},{5,6},{7,8},{9,10},{11,12},{13,14},{15,16},{17,18},{19... | collective-permute-start | bytes 663560 | tf_op jit(solution)/shard_map/ppermute | solution.py:35
  1.3 18.3 %collective-permute-start = (bf16[288,384]{1,0:T(8,128)(2,1)}, bf16[288,384]{1,0:T(8,128)(2,1)S(1)}, u32[]{:S(2)}, u32[]{:S(2)}) collective-permute-start(bf16[288,384]{1,0:T(8,128)(2,1)} %bitcast.21), channel_id=1, source_target_pairs={{0,1},{2,3},{4,5},{6,7},{8,9},{10,11},{12,13},{14,15},{16,17},{18,... | collective-permute-start | bytes 663560 | tf_op jit(solution)/shard_map/ppermute | solution.py:35
  12.2 1.2 %copy-start = (bf16[384,1152]{1,0:T(8,128)(2,1)S(1)}, bf16[384,1152]{1,0:T(8,128)(2,1)}, u32[]{:S(2)}) copy-start(bf16[384,1152]{1,0:T(8,128)(2,1)} %wqkv.5) | copy-start | bytes 2654212
  13.4 1.0 copy-start.2
  14.4 0.9 copy-start.3
  15.3 0.9 copy-start.5
  16.2 0.7 copy-start.8
  16.9 2.8 %copy-start.1 = (bf16[384,1152]{1,0:T(8,128)(2,1)S(1)}, bf16[384,1152]{1,0:T(8,128)(2,1)}, u32[]{:S(2)}) copy-start(bf16[384,1152]{1,0:T(8,128)(2,1)} %wqkv.5) | copy-start | bytes 2654212
  26.6 5.0 %collective-permute-start.2 = (bf16[768,384]{1,0:T(8,128)(2,1)S(1)}, bf16[768,384]{1,0:T(8,128)(2,1)S(1)}, u32[]{:S(2)}, u32[]{:S(2)}) collective-permute-start(bf16[768,384]{1,0:T(8,128)(2,1)S(1)} %get-tuple-element.39), channel_id=1, source_target_pairs={{0,64},{64,0},{1,65},{65,1},{2,66},{66,2},{3,67},{67,3},{4,68},{68... | collective-permute-start | bytes 1769480 | tf_op jit(solution)/shard_map/ppermute | solution.py:313
  32.5 28.0 %all-to-all-start = ((bf16[32,24,384]{2,1,0:T(8,128)(2,1)}), bf16[32,24,384]{2,1,0:T(8,128)(2,1)S(1)}, u32[]{:S(2)}, u32[]{:S(2)}) async-start(bf16[32,24,384]{2,1,0:T(8,128)(2,1)} %bitcast.9), calls=%async_computation | async-start | bytes 1179648 | tf_op jit(solution)/shard_map/all_to_all | solution.py:48
  46.5 23.4 %collective-permute-start.4 = (bf16[288,384]{1,0:T(8,128)(2,1)S(1)}, bf16[288,384]{1,0:T(8,128)(2,1)S(1)}, u32[]{:S(2)}, u32[]{:S(2)}) collective-permute-start(bf16[288,384]{1,0:T(8,128)(2,1)S(1)} %get-tuple-element.46), channel_id=1, source_target_pairs={{31,0},{32,63},{95,64},{96,127},{159,128},{160,191},{223,192},{224... | collective-permute-start | bytes 663560 | tf_op jit(solution)/shard_map/ppermute | solution.py:327
  61.3 14.0 %all-to-all-start.1 = ((bf16[8,24,384]{2,1,0:T(8,128)(2,1)}), bf16[8,24,384]{2,1,0:T(8,128)(2,1)S(1)}, u32[]{:S(2)}, u32[]{:S(2)}) async-start(bf16[8,24,384]{2,1,0:T(8,128)(2,1)} %broadcast_in_dim.29), calls=%async_computation.1 | async-start | bytes 294912 | tf_op jit(solution)/shard_map/all_to_all | solution.py:48
  66.4 13.7 %copy-start.4 = (bf16[1,288,384]{2,1,0:T(8,128)(2,1)S(1)}, bf16[1,288,384]{2,1,0:T(8,128)(2,1)}, u32[]{:S(2)}) copy-start(bf16[1,288,384]{2,1,0:T(8,128)(2,1)} %param.7) | copy-start | bytes 663556
  66.4 13.7 %copy-start.6 = (bf16[1,288,384]{2,1,0:T(8,128)(2,1)S(1)}, bf16[1,288,384]{2,1,0:T(8,128)(2,1)}, u32[]{:S(2)}) copy-start(bf16[1,288,384]{2,1,0:T(8,128)(2,1)} %param.8) | copy-start | bytes 663556
  66.4 13.7 %collective-permute-start.3 = (bf16[288,384]{1,0:T(8,128)(2,1)S(1)}, bf16[288,384]{1,0:T(8,128)(2,1)S(1)}, u32[]{:S(2)}, u32[]{:S(2)}) collective-permute-start(bf16[288,384]{1,0:T(8,128)(2,1)S(1)} %get-tuple-element.45), channel_id=1, source_target_pairs={{0,1},{2,3},{4,5},{6,7},{8,9},{10,11},{12,13},{14,15},{16,17},{18,... | collective-permute-start | bytes 663560 | tf_op jit(solution)/shard_map/ppermute | solution.py:35
  70.0 10.2 %collective-permute-start.5 = (bf16[288,384]{1,0:T(8,128)(2,1)S(1)}, bf16[288,384]{1,0:T(8,128)(2,1)S(1)}, u32[]{:S(2)}, u32[]{:S(2)}) collective-permute-start(bf16[288,384]{1,0:T(8,128)(2,1)S(1)} %broadcast_select_fusion), channel_id=1, source_target_pairs={{1,2},{3,4},{5,6},{7,8},{9,10},{11,12},{13,14},{15,16},{17,18},{19... | collective-permute-start | bytes 663560 | tf_op jit(solution)/shard_map/ppermute | solution.py:334
  76.2 17.6 %all-to-all-start.2 = ((bf16[32,24,384]{2,1,0:T(8,128)(2,1)}), bf16[32,24,384]{2,1,0:T(8,128)(2,1)S(1)}, u32[]{:S(2)}, u32[]{:S(2)}) async-start(bf16[32,24,384]{2,1,0:T(8,128)(2,1)} %gather.1), calls=%async_computation.2 | async-start | bytes 1179648 | tf_op jit(solution)/shard_map/all_to_all | solution.py:48
  80.1 21.5 %copy-start.7 = (f32[384]{0:T(512)S(1)}, f32[384]{0:T(512)}, u32[]{:S(2)}) copy-start(f32[384]{0:T(512)} %gain.1) | copy-start | bytes 4612
  93.8 7.7 %collective-permute-start.6 = (bf16[768,384]{1,0:T(8,128)(2,1)S(1)}, bf16[768,384]{1,0:T(8,128)(2,1)S(1)}, u32[]{:S(2)}, u32[]{:S(2)}) collective-permute-start(bf16[768,384]{1,0:T(8,128)(2,1)S(1)} %bitcast.18), channel_id=1, source_target_pairs={{0,64},{64,0},{1,65},{65,1},{2,66},{66,2},{3,67},{67,3},{4,68},{68... | collective-permute-start | bytes 1769480 | tf_op jit(solution)/shard_map/ppermute | solution.py:342
